TPU v7x, 32 devices: a whole 2x2x4 slice. The times are simulated.
32 devices in a mesh: clus: 8 (over z, x), tgt: 4 (over y, core).
Axes of the slice: x: 2, y: 2, z: 4, core: 2. Of those that a mesh axis runs over, the one named last changes fastest.
Arguments:
- src_pos: float32 [3, 65536], P(None, ('clus', 'tgt')), may hold values from 0 to 1
- src_weight: float32 [65536], P(('clus', 'tgt')), may hold values from 0.1 to 1
- src_pot: float32 [65536], P(('clus', 'tgt')), may hold values from -0.1 to 0.05
- src_count: int32 [256], P(('clus', 'tgt')), may hold values from 128 to 256, as said below
- tgt_pos: float32 [3, 65536], P(None, ('clus', 'tgt')), may hold values from 0 to 1
- tgt_weight: float32 [65536], P(('clus', 'tgt')), may hold values from 0.1 to 1
- tgt_pot: float32 [65536], P(('clus', 'tgt')), may hold values from -0.1 to 0.05
- tgt_count: int32 [256], P(('clus', 'tgt')), may hold values from 128 to 256, as said below
- requests: int32 [256, 2], P(('clus', 'tgt')), may hold values from 0 to 7, as said below
- pair_src: int32 [1024], P(('clus', 'tgt')), may hold values from 0 to 31, as said below
- pair_slot: int32 [1024], P(('clus', 'tgt')), may hold values from 0 to 15, as said below
- pair_count: int32 [32], P(('clus', 'tgt')), may hold values from 16 to 32, as said below
Outputs:
- grad_src_pos: float32 [3, 65536], P(None, ('clus', 'tgt'))
- grad_src_weight: float32 [65536], P(('clus', 'tgt'))
- grad_tgt_pos: float32 [3, 65536], P(None, ('clus', 'tgt'))
- grad_tgt_weight: float32 [65536], P(('clus', 'tgt'))
Inputs may be any that keep to these rules, and one draw needn't show every extreme that they name: `src_count`: counts of live points, the rest of each block is padding; some block is full and some is half full. `tgt_count`: counts of live points, the rest of each block is padding; some block is full and some is half full. `requests`: each row holds 2 different local block numbers of one owner: row r of group d names blocks of the owner with clus index r and the tgt index of d. `pair_src`: source block within the group's 32 source blocks of its clus index, all tgt indices in order. `pair_slot`: slot r * 2 + m of the group's request rows; the live entries of a group name every one of its 16 slots. `pair_count`: entries past the count are padding with valid numbers and must not count.
All inputs are finite; a program needn't handle non-finite values.
Results may differ from a plain program's by a relative error of at most 0.0003.
Values sent between devices are 32-bit elements; how exact they have to be, the bound alone decides.
No kernel may reach another device: no remote copies, remote signals or barrier semaphores. Data moves between devices by JAX's collectives and lax.ppermute only.
A program may use at most 64 MiB of HBM per device.

v0:
```python
import math

import jax
import jax.numpy as jnp
from jax import lax
from jax.sharding import PartitionSpec as P

BLK = 256


entropic = 0.05
highest = lax.Precision.HIGHEST


def local_pack(positions, weights, potentials, counts):
    block_count = counts.shape[0]
    block_len = positions.shape[1] // block_count
    offsets = jnp.arange(block_len, dtype=jnp.int32)[None, :]
    live_mask = (offsets < counts[:, None]).astype(jnp.float32).reshape(-1)
    packed = jnp.concatenate([positions, (weights * live_mask)[None, :], potentials[None, :]], 0)
    return (packed, live_mask)


def tile_kernel(src_tiles, tgt_tiles, live_mask):
    crossed = jnp.einsum("cpi,cpj->pij", src_tiles[:3], tgt_tiles[:3], precision=highest)
    left_part = src_tiles[4] - 0.5 * jnp.sum(src_tiles[:3] * src_tiles[:3], 0)
    right_part = tgt_tiles[4] - 0.5 * jnp.sum(tgt_tiles[:3] * tgt_tiles[:3], 0)
    expo = (left_part[:, :, None] + right_part[:, None, :] + crossed) / entropic
    return jnp.exp(expo) * live_mask[:, None, None]


def source_terms(kernel, src_tiles, tgt_tiles):
    weighted = kernel * tgt_tiles[3][:, None, :]
    row_totals = jnp.sum(weighted, 2)
    shifted = jnp.einsum("pij,cpj->cpi", weighted, tgt_tiles[:3], precision=highest)
    motion = src_tiles[3][None] * (src_tiles[:3] * row_totals[None] - shifted)
    return jnp.concatenate([motion, (-entropic * row_totals)[None]], 0)


def target_terms(kernel, src_tiles, tgt_tiles):
    weighted = kernel * src_tiles[3][:, :, None]
    col_totals = jnp.sum(weighted, 1)
    shifted = jnp.einsum("pij,cpi->cpj", weighted, src_tiles[:3], precision=highest)
    motion = tgt_tiles[3][None] * (tgt_tiles[:3] * col_totals[None] - shifted)
    return jnp.concatenate([motion, (-entropic * col_totals)[None]], 0)


def shards(
    src_pos,
    src_weight,
    src_pot,
    src_count,
    tgt_pos,
    tgt_weight,
    tgt_pot,
    tgt_count,
    requests,
    pair_src,
    pair_slot,
    pair_count,
):
    src_packed, src_live = local_pack(src_pos, src_weight, src_pot, src_count)
    tgt_packed, tgt_live = local_pack(tgt_pos, tgt_weight, tgt_pot, tgt_count)
    group_blocks = lax.all_gather(src_packed, "tgt", axis=1, tiled=True).reshape(5, -1, BLK)
    own_blocks = tgt_packed.reshape(5, -1, BLK)
    owned_count = own_blocks.shape[1]
    peer_count = lax.axis_size("clus")
    req_len = requests.shape[1]
    slot_total = peer_count * req_len
    asked_ids = lax.all_to_all(requests, "clus", split_axis=0, concat_axis=0, tiled=True)
    chosen_blocks = jnp.take(own_blocks, asked_ids.reshape(-1), axis=1).reshape(
        5, peer_count, req_len * BLK
    )
    fetched = lax.all_to_all(
        chosen_blocks, "clus", split_axis=1, concat_axis=1, tiled=True
    ).reshape(5, slot_total, BLK)
    slot_map = jnp.arange(slot_total, dtype=jnp.int32)
    pair_total = pair_src.shape[0]
    batch_len = math.gcd(pair_total, 32)
    batches = pair_total // batch_len
    live_pairs = pair_count[0]

    def gather_batch(batch_idx):
        first_pair = batch_idx * batch_len
        sources = lax.dynamic_slice_in_dim(pair_src, first_pair, batch_len)
        targets = jnp.take(slot_map, lax.dynamic_slice_in_dim(pair_slot, first_pair, batch_len))
        live_mask = (first_pair + jnp.arange(batch_len, dtype=jnp.int32) < live_pairs).astype(
            jnp.float32
        )
        src_tiles = jnp.take(group_blocks, sources, axis=1)
        tgt_tiles = jnp.take(fetched, targets, axis=1)
        return (
            sources,
            targets,
            src_tiles,
            tgt_tiles,
            tile_kernel(src_tiles, tgt_tiles, live_mask),
        )

    src_zero = jnp.zeros((4, group_blocks.shape[1], BLK), jnp.float32)
    tgt_zero = jnp.zeros((4, fetched.shape[1], BLK), jnp.float32)

    def both_sides(batch_idx, carry):
        sources, targets, src_tiles, tgt_tiles, kernel = gather_batch(batch_idx)
        src_acc = carry[0].at[:, sources, :].add(source_terms(kernel, src_tiles, tgt_tiles))
        tgt_acc = carry[1].at[:, targets, :].add(target_terms(kernel, src_tiles, tgt_tiles))
        return (src_acc, tgt_acc)

    src_acc, tgt_acc = lax.fori_loop(0, batches, both_sides, (src_zero, tgt_zero))
    returned = lax.all_to_all(
        tgt_acc.reshape(4, peer_count, req_len * BLK),
        "clus",
        split_axis=1,
        concat_axis=1,
        tiled=True,
    )
    returned = returned.reshape(4, slot_total, BLK)
    onehot = (
        asked_ids.reshape(-1)[None, :] == jnp.arange(owned_count, dtype=jnp.int32)[:, None]
    ).astype(jnp.float32)
    tgt_sums = jnp.einsum("tq,cqk->ctk", onehot, returned, precision=highest).reshape(4, -1)
    src_sums = lax.psum_scatter(src_acc.reshape(4, -1), "tgt", scatter_dimension=1, tiled=True)
    grad_src_pos = src_sums[:3] * src_live[None, :]
    grad_src_weight = (src_pot + src_sums[3]) * src_live
    grad_tgt_pos = tgt_sums[:3] * tgt_live[None, :]
    grad_tgt_weight = (tgt_pot + tgt_sums[3]) * tgt_live
    return (grad_src_pos, grad_src_weight, grad_tgt_pos, grad_tgt_weight)


def solution(mesh):
    placed = (
        P(None, ("clus", "tgt")),
        P(("clus", "tgt")),
        P(("clus", "tgt")),
        P(("clus", "tgt")),
        P(None, ("clus", "tgt")),
        P(("clus", "tgt")),
        P(("clus", "tgt")),
        P(("clus", "tgt")),
        P(("clus", "tgt"), None),
        P(("clus", "tgt")),
        P(("clus", "tgt")),
        P(("clus", "tgt")),
    )
    return jax.shard_map(
        shards,
        mesh=mesh,
        in_specs=placed,
        out_specs=(
            P(None, ("clus", "tgt")),
            P(("clus", "tgt")),
            P(None, ("clus", "tgt")),
            P(("clus", "tgt")),
        ),
        check_vma=False,
    )
```

profile of v0, /device:TPU:0, one launch (start us, length us, event | category | flops | bytes accessed | tf_op | source)
XLA Modules:
  0.0 141.8 jit_solution(15619849590621399606)
XLA Ops:
  7.2 1.3 copy.48
  8.5 7.3 %all-to-all-start = ((s32[8,1,2]{2,1,0:T(1,128)}), s32[8,1,2]{2,1,0:T(1,128)S(1)}, u32[]{:S(2)}, u32[]{:S(2)}) async-start(s32[8,1,2]{2,1,0:T(1,128)} %copy.48), calls=%async_computation | async-start | bytes 8192 | tf_op jit(solution)/shard_map/all_to_all | solution.py:70
  15.8 0.7 compare_select_fusion.4
  16.4 0.7 compare_and_fusion.2
  17.1 0.7 iota_compare_fusion
  17.8 0.7 compare_select_fusion.3
  18.5 0.7 gather_fusion.1
  19.2 0.7 compare_and_fusion.1
  19.9 0.7 iota_compare_fusion.1
  20.6 0.7 broadcast_select_fusion.2
  21.3 0.8 pad_maximum_fusion
  22.1 5.8 %all_gather.3 = f32[5,8192]{1,0:T(8,128)S(1)} all-gather(f32[5,2048]{1,0:T(8,128)S(1)} %pad_maximum_fusion), channel_id=1, replica_groups=mesh['clus'=8,'tgt'=4] {'tgt'}, dimensions={1}, use_global_device_ids=true | all-gather | bytes 204800 | tf_op jit(solution)/shard_map/all_gather | solution.py:64
  27.9 0.6 gather_fusion
  28.5 0.1 fusion.15
  28.6 0.7 broadcast_select_fusion.1
  29.3 0.8 pad_maximum_fusion.1
  30.8 0.0 all-to-all-done
  30.8 0.5 broadcast.193
  31.3 0.7 reduce.5
  31.9 0.1 reshape.188
  32.0 0.6 gather_fusion.2
  32.7 0.1 copy.49
  32.8 0.1 copy.50
  32.9 0.1 broadcast_bitcast_fusion
  33.0 0.7 copy.52
  33.7 6.0 %all-to-all-start.1 = ((f32[5,8,512]{2,0,1:T(8,128)}), f32[5,8,512]{2,0,1:T(8,128)S(1)}, u32[]{:S(2)}, u32[]{:S(2)}) async-start(f32[5,8,512]{2,0,1:T(8,128)} %copy.52), calls=%async_computation.1 | async-start | bytes 262144 | tf_op jit(solution)/shard_map/all_to_all | solution.py:74
  39.7 0.1 reshape.193
  39.8 7.4 %all-to-all-done.1 = f32[5,8,512]{2,0,1:T(8,128)S(1)} async-done(((f32[5,8,512]{2,0,1:T(8,128)}), f32[5,8,512]{2,0,1:T(8,128)S(1)}, u32[]{:S(2)}, u32[]{:S(2)}) %all-to-all-start.1) | async-done | bytes 81952 | tf_op jit(solution)/shard_map/all_to_all | solution.py:74
  47.2 0.6 gather_fusion.3
  47.8 0.1 copy_select_fusion
  47.8 0.1 copy.87
  48.0 0.1 fusion.26
  48.0 0.1 multiply_reduce_fusion.2
  48.2 11.8 %multiply_reduce_fusion = (f32[32,256]{1,0:T(8,128)S(1)}, f32[32,256]{1,0:T(8,128)S(1)}, f32[32,256,256]{2,1,0:T(8,128)S(1)}) fusion(f32[32,256]{1,0:T(8,128)S(1)} %get-tuple-element.45, f32[32,256]{1,0:T(8,128)S(1)} %get-tuple-element.46, f32[32]{0:T(128)S(1)} %compare_convert_fusion, f32[5,32,256]{2,0,1:T(8,128)S(1)} %bitcast.73, ...), kind=kOutput, calls=%fused_computation.9 | convolution fusion | flops 92258304 | bytes 8815104 | tf_op jit(solution)/shard_map/while/body/eval_jaxpr/cpi,cpj->pij/dot_general | solution.py:25
  59.9 4.8 %fusion.12 = f32[3,32,256]{2,0,1:T(4,128)S(1)} fusion(f32[32,256,256]{2,1,0:T(8,128)S(1)} %get-tuple-element.42, f32[32,256]{1,0:T(8,128)S(1)} %get-tuple-element.45, f32[3,32,256]{2,1,0:T(8,128)S(1)} %get-tuple-element.40, f32[5,32,256]{2,0,1:T(8,128)S(1)} %bitcast.74, f32[32,256]{1,0:T(8,128)S(1)} %get-tuple-element.24, f32[32,256]{1,0:T(8,128)S(1)} %get-tuple-element.46), kind=kOutput, calls=%fused_computation.17 | convolution fusion | flops 77668352 | bytes 8781824 | tf_op jit(solution)/shard_map/while/body/eval_jaxpr/pij,cpi->cpj/dot_general | solution.py:43
  64.7 0.0 copy-start
  64.7 7.0 %fusion.2 = f32[32,3,256]{2,1,0:T(4,128)S(1)} fusion(f32[32,256,256]{2,1,0:T(8,128)S(1)} %get-tuple-element.42, f32[32,256]{1,0:T(8,128)S(1)} %get-tuple-element.46, f32[5,32,256]{2,0,1:T(8,128)S(1)} %bitcast.75), kind=kOutput, calls=%fused_computation.10 | convolution fusion | flops 77594624 | bytes 8650752 | tf_op jit(solution)/shard_map/while/body/eval_jaxpr/pij,cpj->cpi/dot_general | solution.py:35
  71.7 0.0 copy-start.1
  71.8 0.1 maximum_bitcast_fusion.1
  71.9 0.6 broadcast_in_dim.97
  72.5 3.8 %scatter_fusion.1 = f32[4,16,256]{2,0,1:T(4,128)} fusion(f32[4,16,256]{2,0,1:T(4,128)} %broadcast_in_dim.97, s32[32]{0:T(128)S(1)} %get-tuple-element.27, f32[32,4,256]{2,1,0:T(4,128)S(1)} %maximum_bitcast_fusion.1), kind=kCustom, calls=%fused_computation.5 | custom fusion | flops 32768 | bytes 393344 | tf_op jit(solution)/shard_map/while/body/eval_jaxpr/scatter-add | solution.py:106
  76.3 3.3 %all-to-all-start.2 = ((f32[4,8,512]{2,0,1:T(4,128)}), f32[4,8,512]{2,0,1:T(4,128)S(1)}, u32[]{:S(2)}, u32[]{:S(2)}) async-start(f32[4,8,512]{2,0,1:T(4,128)} %bitcast.23), calls=%async_computation.2 | async-start | bytes 131072 | tf_op jit(solution)/shard_map/all_to_all | solution.py:110
  79.7 0.0 reduce-scatter.4.cloned.1.call-start
  79.8 0.1 copy.59
  79.9 1.7 %scatter_fusion = f32[4,32,256]{2,0,1:T(4,128)S(1)} fusion(f32[4,32,256]{2,0,1:T(4,128)S(1)} %broadcast_in_dim.84, s32[32]{0:T(128)S(1)} %compare_select_fusion.4, f32[32,4,256]{2,1,0:T(4,128)S(1)} %copy.59), kind=kCustom, calls=%fused_computation.4 | custom fusion | flops 32768 | bytes 393344 | tf_op jit(solution)/shard_map/while/body/eval_jaxpr/scatter-add | solution.py:105
  81.6 2.6 %copy.64 = f32[4,8192]{0,1:T(8,128)} copy(f32[4,8192]{1,0:T(4,128)S(1)} %bitcast.76) | data formatting | bytes 262144
  84.2 0.0 reduce-scatter.4.cloned.1.call-update
  84.3 2.2 %all-to-all-done.2 = f32[4,8,512]{2,0,1:T(4,128)S(1)} async-done(((f32[4,8,512]{2,0,1:T(4,128)}), f32[4,8,512]{2,0,1:T(4,128)S(1)}, u32[]{:S(2)}, u32[]{:S(2)}) %all-to-all-start.2) | async-done | bytes 65568 | tf_op jit(solution)/shard_map/all_to_all | solution.py:110
  86.5 0.1 convolution_bitcast_fusion
  86.7 0.6 broadcast_multiply_fusion
  87.4 0.0 copy-done
  87.4 0.6 add_select_fusion
  88.0 42.3 %reduce-scatter.4.cloned.1.call-done = f32[2048,4]{1,0:T(8,128)} async-done(((f32[8192,4]{1,0:T(8,128)}), f32[2048,4]{1,0:T(8,128)}) %reduce-scatter.4.cloned.1.call-update) | async-done | bytes 32784
  130.2 1.6 %slice.76 = f32[1,2048]{0,1:T(8,128)S(1)} slice(f32[4,2048]{0,1:T(8,128)} %bitcast.69), slice={[3:4], [0:2048]} | slice | bytes 16384 | tf_op jit(solution)/shard_map/slice | solution.py:124
  131.8 0.3 copy.69
  132.1 0.0 copy-done.1
  132.1 0.6 add_select_fusion.1
  132.7 1.6 %copy.68 = f32[3,2048]{1,0:T(4,128)S(1)} copy(f32[3,2048]{0,1:T(8,128)} %bitcast.70) | data formatting | bytes 49152
  134.3 0.6 broadcast_multiply_fusion.1
  (31 shorter events, 0.4 us)
Async XLA Ops:
  8.5 22.2 %all-to-all-start = ((s32[8,1,2]{2,1,0:T(1,128)}), s32[8,1,2]{2,1,0:T(1,128)S(1)}, u32[]{:S(2)}, u32[]{:S(2)}) async-start(s32[8,1,2]{2,1,0:T(1,128)} %copy.48), calls=%async_computation | async-start | bytes 8192 | tf_op jit(solution)/shard_map/all_to_all | solution.py:70
  33.7 13.5 %all-to-all-start.1 = ((f32[5,8,512]{2,0,1:T(8,128)}), f32[5,8,512]{2,0,1:T(8,128)S(1)}, u32[]{:S(2)}, u32[]{:S(2)}) async-start(f32[5,8,512]{2,0,1:T(8,128)} %copy.52), calls=%async_computation.1 | async-start | bytes 262144 | tf_op jit(solution)/shard_map/all_to_all | solution.py:74
  64.7 22.7 %copy-start = (f32[2048]{0:T(1024)S(1)}, f32[2048]{0:T(1024)}, u32[]{:S(2)}) copy-start(f32[2048]{0:T(1024)} %param.18) | copy-start | bytes 24580
  71.7 60.4 %copy-start.1 = (f32[2048]{0:T(1024)S(1)}, f32[2048]{0:T(1024)}, u32[]{:S(2)}) copy-start(f32[2048]{0:T(1024)} %param.14) | copy-start | bytes 24580
  76.3 10.2 %all-to-all-start.2 = ((f32[4,8,512]{2,0,1:T(4,128)}), f32[4,8,512]{2,0,1:T(4,128)S(1)}, u32[]{:S(2)}, u32[]{:S(2)}) async-start(f32[4,8,512]{2,0,1:T(4,128)} %bitcast.23), calls=%async_computation.2 | async-start | bytes 131072 | tf_op jit(solution)/shard_map/all_to_all | solution.py:110
  79.7 50.6 %reduce-scatter.4.cloned.1.call-start = ((), (), s32[]{:S(2)}) async-start(), calls=%async_computation.4 | async-start | bytes 5242880
Sparse Core Ops, SparseCore 0:
  84.4 45.8 reduce-scatter.3
where the time goes:
time: 143 us; the launch traced here: 142 us
  waiting for transfers between devices  51.9 us (36%)
  matrix products  23.7 us (17%)
  starting transfers between devices  16.6 us (12%)
  other arithmetic  16.2 us (11%)
  between operations  15 us (10%)
  local copies, waits for them, and re-layouts  12.6 us (9%)
  blocking collectives  5.79 us (4%)
    unnamed x2, waiting for transfers between devices  42.3 us
    dot_general x1, matrix products, tile_kernel(): jnp.einsum('cpi,cpj->pij', src_tiles[:3], tgt_tiles[:3], precision=highest)  11.8 us
    all_to_all x1, waiting for transfers between devices, shards(): lax.all_to_all(chosen_blocks, 'clus', split_axis=1, concat_axis=1, tiled=...  7.37 us
    all_to_all x1, starting transfers between devices, shards(): lax.all_to_all(requests, 'clus', split_axis=0, concat_axis=0, tiled=True)  7.25 us
    dot_general x1, matrix products, source_terms(): jnp.einsum('pij,cpj->cpi', weighted, tgt_tiles[:3], precision=highest)  7.04 us
    all_to_all x1, starting transfers between devices, shards(): lax.all_to_all(chosen_blocks, 'clus', split_axis=1, concat_axis=1, tiled=...  6 us
    all_gather x1, blocking collectives, shards(): lax.all_gather(src_packed, 'tgt', axis=1, tiled=True).reshape(5, -1, BLK)  5.79 us
    dot_general x1, matrix products, target_terms(): jnp.einsum('pij,cpi->cpj', weighted, src_tiles[:3], precision=highest)  4.75 us
  transfers between devices with their start and end apart: 4, of which 3 were waited for; matrix products, arithmetic and copies ran while one was open for 10% of the time, Pallas kernels for 0%

commit v1 on v0

v1 whole, which is shorter than its diff:
```python
import functools
import math

import jax
import jax.numpy as jnp
from jax import lax
from jax.experimental import pallas as pl
from jax.experimental.pallas import tpu as pltpu
from jax.sharding import PartitionSpec as P

BLK = 256
LANES = 128
GROUP = 2

entropic = 0.05
LOG2E = math.log2(math.e)
SCALE = LOG2E / entropic
DEAD = -4096.0

VMEM = pl.BlockSpec(memory_space=pltpu.VMEM)
SMEM = pl.BlockSpec(memory_space=pltpu.SMEM)


def partner(i, k, n):
    return i ^ k if n & (n - 1) == 0 else (i + k) % n


def origin(i, k, n):
    return i ^ k if n & (n - 1) == 0 else (i + n - k) % n


def shifted(x, axis, k):
    n = lax.axis_size(axis)
    return lax.ppermute(x, axis, [(i, partner(i, k, n)) for i in range(n)])


def live_row(count_ref, block):
    lane = lax.broadcasted_iota(jnp.int32, (1, BLK), 1)
    return lane < count_ref[block]


def pack_side(pos_ref, weight_ref, pot_ref, count_ref, out_ref):
    for b in range(count_ref.shape[0]):
        cols = slice(b * BLK, (b + 1) * BLK)
        pos = pos_ref[:, cols]
        norm = jnp.sum(pos * pos, axis=0, keepdims=True)
        expo = (pot_ref[:, cols] - 0.5 * norm) * SCALE + jnp.log(weight_ref[:, cols]) * LOG2E
        out_ref[0:3, cols] = pos
        out_ref[3:4, cols] = jnp.where(live_row(count_ref, b), expo, DEAD)


def pack_kernel(req_ref, sc_ref, tc_ref, sp_ref, sw_ref, so_ref, tp_ref, tw_ref, to_ref, src_ref, tgt_ref):
    pack_side(sp_ref, sw_ref, so_ref, sc_ref, src_ref)
    pack_side(tp_ref, tw_ref, to_ref, tc_ref, tgt_ref)
    rows, per = req_ref.shape
    own = tp_ref.shape[1]
    width = tgt_ref.shape[1] - own
    lane = lax.broadcasted_iota(jnp.int32, (4, width), 1)
    ids = jnp.zeros((4, width), jnp.float32)
    for r in range(rows):
        for m in range(per):
            ids = jnp.where(lane == r * per + m, req_ref[r, m].astype(jnp.float32), ids)
    tgt_ref[:, own:] = ids


def split3(x):
    high = x.astype(jnp.bfloat16).astype(jnp.float32)
    rest = x - high
    mid = rest.astype(jnp.bfloat16).astype(jnp.float32)
    return high, mid, rest - mid


def main_kernel(n_tgt, n_clus, me_ref, req_ref, ps_ref, pq_ref, pc_ref, *refs):
    src_in, refs = refs[:n_tgt], refs[n_tgt:]
    tgt_in, refs = refs[:n_clus], refs[n_clus:]
    src_out, refs = refs[:n_tgt], refs[n_tgt:]
    tgt_out, refs = refs[:n_clus], refs[n_clus:]
    left, right, src_rows, tgt_rows, src_acc, tgt_acc = refs
    tgt_me, clus_me = me_ref[0], me_ref[1]
    per_dev = src_in[0].shape[1] // BLK
    n_src = n_tgt * per_dev
    per_req = req_ref.shape[1]
    last = lax.broadcasted_iota(jnp.int32, (4, BLK), 0) == 3
    pad = jnp.zeros((8, BLK), jnp.float32)

    for k in range(n_tgt):
        base = origin(tgt_me, k, n_tgt) * per_dev
        for b in range(per_dev):
            high, mid, low = split3(src_in[k][:, b * BLK : (b + 1) * BLK])
            high1, mid1 = jnp.where(last, 1.0, high), jnp.where(last, 1.0, mid)
            left[base + b] = jnp.concatenate([high, high1, high1, mid, mid1, low, pad], 0).astype(jnp.bfloat16)
            src_rows[base + b] = jnp.concatenate([high1, jnp.where(last, 0.0, mid)], 0)
    dead = lax.broadcasted_iota(jnp.int32, (32, BLK), 0) == 3
    left[n_src] = jnp.where(dead, DEAD, 0.0).astype(jnp.bfloat16)
    src_rows[n_src] = pad
    src_acc[...] = jnp.zeros_like(src_acc)
    tgt_acc[...] = jnp.zeros_like(tgt_acc)

    for k in range(n_clus):
        owner = origin(clus_me, k, n_clus)
        for m in range(per_req):
            block = req_ref[owner, m]
            raw = tgt_in[k][:, pl.ds(pl.multiple_of(block * BLK, BLK), BLK)]
            high, mid, _ = split3(raw)
            tgt_rows[owner * per_req + m] = jnp.concatenate(
                [jnp.where(last, 1.0, high), jnp.where(last, 0.0, mid)], 0
            )
            high, mid, low = split3(jnp.where(last, raw, raw * SCALE))
            high1 = jnp.where(last, 1.0, high)
            wide = jnp.concatenate([high1, mid, low, high1, jnp.where(last, high, mid), high1, pad], 0)
            right[owner * per_req + m] = wide.T.astype(jnp.bfloat16)

    count = pc_ref[0]

    def one_pair(pair):
        inside = jnp.minimum(pair, ps_ref.shape[0] - 1)
        s = jnp.where(pair < count, ps_ref[inside], n_src)
        q = pq_ref[inside]
        expo = jnp.dot(right[q], left[s], preferred_element_type=jnp.float32)
        kern = jnp.exp2(expo)
        high = kern.astype(jnp.bfloat16)
        low = (kern - high.astype(jnp.float32)).astype(jnp.bfloat16)
        y = tgt_rows[q].astype(jnp.bfloat16)
        x = src_rows[s].astype(jnp.bfloat16)
        src_part = jnp.dot(y, high, preferred_element_type=jnp.float32) + jnp.dot(
            y, low, preferred_element_type=jnp.float32
        )
        nt = (((1,), (1,)), ((), ()))
        tgt_part = lax.dot_general(x, high, nt, preferred_element_type=jnp.float32) + lax.dot_general(
            x, low, nt, preferred_element_type=jnp.float32
        )
        return s, q, src_part, tgt_part

    def body(step, carry):
        parts = [one_pair(step * GROUP + g) for g in range(GROUP)]
        for s, q, src_part, tgt_part in parts:
            src_acc[s] += src_part
            tgt_acc[q] += tgt_part
        return carry

    lax.fori_loop(0, (count + GROUP - 1) // GROUP, body, 0)

    for k in range(n_tgt):
        base = partner(tgt_me, k, n_tgt) * per_dev
        for b in range(per_dev):
            total = src_acc[base + b]
            src_out[k][:, b * BLK : (b + 1) * BLK] = total[0:4] + total[4:8]
    for k in range(n_clus):
        base = partner(clus_me, k, n_clus) * per_req
        for m in range(per_req):
            total = tgt_acc[base + m]
            tgt_out[k][:, m * BLK : (m + 1) * BLK] = total[0:4] + total[4:8]


def finish_side(pos_ref, weight_ref, pot_ref, count_ref, sums, grad_pos_ref, grad_weight_ref):
    for b in range(count_ref.shape[0]):
        cols = slice(b * BLK, (b + 1) * BLK)
        total = sums(b, cols)
        mass = total[3:4]
        live = live_row(count_ref, b)
        grad_pos_ref[:, cols] = jnp.where(live, pos_ref[:, cols] * mass - total[0:3], 0.0)
        grad_weight_ref[:, cols] = jnp.where(
            live, pot_ref[:, cols] - entropic * mass / weight_ref[:, cols], 0.0
        )


def finish_kernel(n_tgt, n_clus, per_req, me_ref, sc_ref, tc_ref, sp_ref, sw_ref, so_ref, tp_ref, tw_ref, to_ref, *refs):
    src_parts, refs = refs[:n_tgt], refs[n_tgt:]
    tgt_parts, refs = refs[:n_clus], refs[n_clus:]
    tgt_in, refs = refs[:n_clus], refs[n_clus:]
    gsp_ref, gsw_ref, gtp_ref, gtw_ref = refs
    finish_side(
        sp_ref, sw_ref, so_ref, sc_ref, lambda b, cols: sum(p[:, cols] for p in src_parts), gsp_ref, gsw_ref
    )
    clus_me = me_ref[1]
    own = tp_ref.shape[1]
    width = tgt_in[0].shape[1] - own
    lane = lax.broadcasted_iota(jnp.int32, (4, width), 1)
    ids = []
    for k in range(n_clus):
        row = tgt_in[k][:, own:]
        for m in range(per_req):
            ids.append(jnp.sum(jnp.where(lane == clus_me * per_req + m, row, 0.0), axis=1, keepdims=True))

    def tgt_sum(b, cols):
        total = jnp.zeros((4, BLK), jnp.float32)
        for k in range(n_clus):
            for m in range(per_req):
                part = tgt_parts[k][:, m * BLK : (m + 1) * BLK]
                total += jnp.where(ids[k * per_req + m] == b, part, 0.0)
        return total

    finish_side(tp_ref, tw_ref, to_ref, tc_ref, tgt_sum, gtp_ref, gtw_ref)


def shards(
    src_pos,
    src_weight,
    src_pot,
    src_count,
    tgt_pos,
    tgt_weight,
    tgt_pot,
    tgt_count,
    requests,
    pair_src,
    pair_slot,
    pair_count,
):
    f32 = jnp.float32
    n_tgt, n_clus = lax.axis_size("tgt"), lax.axis_size("clus")
    ns, nt = src_pos.shape[1], tgt_pos.shape[1]
    per_dev = ns // BLK
    per_req = requests.shape[1]
    n_src, slots = n_tgt * per_dev, n_clus * per_req
    width = -(-slots // LANES) * LANES
    params = pltpu.CompilerParams(vmem_limit_bytes=48 * 2**20)
    me = jnp.stack([lax.axis_index("tgt"), lax.axis_index("clus")]).astype(jnp.int32)
    rows = [a.reshape(1, -1) for a in (src_weight, src_pot, tgt_weight, tgt_pot)]
    points = (src_pos, rows[0], rows[1], tgt_pos, rows[2], rows[3])

    src_pack, tgt_pack = pl.pallas_call(
        pack_kernel,
        name="pack",
        out_shape=(jax.ShapeDtypeStruct((4, ns), f32), jax.ShapeDtypeStruct((4, nt + width), f32)),
        in_specs=[SMEM] * 3 + [VMEM] * 6,
        out_specs=(VMEM, VMEM),
        compiler_params=params,
    )(requests, src_count, tgt_count, *points)

    src_in = [src_pack] + [shifted(src_pack, "tgt", k) for k in range(1, n_tgt)]
    tgt_in = [tgt_pack] + [shifted(tgt_pack, "clus", k) for k in range(1, n_clus)]

    outs = pl.pallas_call(
        functools.partial(main_kernel, n_tgt, n_clus),
        name="pairs",
        out_shape=[jax.ShapeDtypeStruct((4, ns), f32)] * n_tgt
        + [jax.ShapeDtypeStruct((4, per_req * BLK), f32)] * n_clus,
        in_specs=[SMEM] * 5 + [VMEM] * (n_tgt + n_clus),
        out_specs=[VMEM] * (n_tgt + n_clus),
        scratch_shapes=[
            pltpu.VMEM((n_src + 1, 32, BLK), jnp.bfloat16),
            pltpu.VMEM((slots, BLK, 32), jnp.bfloat16),
            pltpu.VMEM((n_src + 1, 8, BLK), f32),
            pltpu.VMEM((slots, 8, BLK), f32),
            pltpu.VMEM((n_src + 1, 8, BLK), f32),
            pltpu.VMEM((slots, 8, BLK), f32),
        ],
        compiler_params=params,
    )(me, requests, pair_src, pair_slot, pair_count, *src_in, *tgt_in)
    src_out, tgt_out = outs[:n_tgt], outs[n_tgt:]

    src_parts = [src_out[0]] + [shifted(src_out[k], "tgt", k) for k in range(1, n_tgt)]
    tgt_parts = [tgt_out[0]] + [shifted(tgt_out[k], "clus", k) for k in range(1, n_clus)]

    gsp, gsw, gtp, gtw = pl.pallas_call(
        functools.partial(finish_kernel, n_tgt, n_clus, per_req),
        name="finish",
        out_shape=(
            jax.ShapeDtypeStruct((3, ns), f32),
            jax.ShapeDtypeStruct((1, ns), f32),
            jax.ShapeDtypeStruct((3, nt), f32),
            jax.ShapeDtypeStruct((1, nt), f32),
        ),
        in_specs=[SMEM] * 3 + [VMEM] * (6 + n_tgt + 2 * n_clus),
        out_specs=(VMEM,) * 4,
        compiler_params=params,
    )(me, src_count, tgt_count, *points, *src_parts, *tgt_parts, *tgt_in)
    return gsp, gsw.reshape(-1), gtp, gtw.reshape(-1)


def solution(mesh):
    placed = (
        P(None, ("clus", "tgt")),
        P(("clus", "tgt")),
        P(("clus", "tgt")),
        P(("clus", "tgt")),
        P(None, ("clus", "tgt")),
        P(("clus", "tgt")),
        P(("clus", "tgt")),
        P(("clus", "tgt")),
        P(("clus", "tgt"), None),
        P(("clus", "tgt")),
        P(("clus", "tgt")),
        P(("clus", "tgt")),
    )
    return jax.shard_map(
        shards,
        mesh=mesh,
        in_specs=placed,
        out_specs=(
            P(None, ("clus", "tgt")),
            P(("clus", "tgt")),
            P(None, ("clus", "tgt")),
            P(("clus", "tgt")),
        ),
        check_vma=False,
    )
```

time: 143 us -> 58.8 us (0.41)
  waiting for transfers between devices: 51.9 us -> 9.67 us
  matrix products: 23.7 us -> 0 us
  other arithmetic: 16.2 us -> 0.07 us
  between operations: 15 us -> 1.47 us
  Pallas kernels: 0 us -> 12.8 us
  starting transfers between devices: 16.6 us -> 29.3 us
  local copies, waits for them, and re-layouts: 12.6 us -> 5.07 us
  blocking collectives: 5.79 us -> 0 us
    unnamed x2 -> x0, waiting for transfers between devices: 42.3 us -> none
    ppermute x0 -> x20, starting transfers between devices: none -> 29.3 us  [shifted(): return lax.ppermute(x, axis, [(i, partner(i, k, n)) for i in range(n)])]
    dot_general x4 -> x0, matrix products: 23.7 us -> none  [the longest x1 11.8 us: tile_kernel(): jnp.einsum('cpi,cpj->pij', src_tiles[:3], tgt_tiles[:3], precision=highest)]
    all_to_all x3 -> x0, starting transfers between devices: 16.6 us -> none  [the longest x1 7.25 us: shards(): lax.all_to_all(requests, 'clus', split_axis=0, concat_axis=0, tiled=True)]
    pallas_call x0 -> x3, Pallas kernels: none -> 12.8 us  [the longest x1 10.6 us: shards(): pl.pallas_call(functools.partial(main_kernel, n_tgt, n_clus), name='pairs...]
    ppermute x0 -> x20, waiting for transfers between devices: none -> 9.67 us  [shifted(): return lax.ppermute(x, axis, [(i, partner(i, k, n)) for i in range(n)])]
    all_to_all x3 -> x0, waiting for transfers between devices: 9.61 us -> none  [the longest x1 7.37 us: shards(): lax.all_to_all(chosen_blocks, 'clus', split_axis=1, concat_axis=1, tiled=...]
    all_gather x1 -> x0, blocking collectives: 5.79 us -> none  [shards(): lax.all_gather(src_packed, 'tgt', axis=1, tiled=True).reshape(5, -1, BLK)]
  transfers between devices with their start and end apart: 4 -> 20, of which waited for: 3 -> 9; matrix products, arithmetic and copies ran while one was open for 10% -> 0% of each run, Pallas kernels for 0% -> 0%
where the time goes in v1:
time: 58.8 us; the launch traced here: 58.4 us
  starting transfers between devices  29.3 us (50%)
  Pallas kernels  12.8 us (22%)
  waiting for transfers between devices  9.67 us (16%)
  local copies, waits for them, and re-layouts  5.07 us (9%)
  between operations  1.47 us (2%)
    ppermute x20, starting transfers between devices, shifted(): return lax.ppermute(x, axis, [(i, partner(i, k, n)) for i in range(n)])  29.3 us
    pallas_call x1, Pallas kernels, shards(): pl.pallas_call(functools.partial(main_kernel, n_tgt, n_clus), name='pairs...  10.6 us
    ppermute x20, waiting for transfers between devices, shifted(): return lax.ppermute(x, axis, [(i, partner(i, k, n)) for i in range(n)])  9.67 us
    unnamed x31, local copies, waits for them, and re-layouts  5.07 us
    pallas_call x1, Pallas kernels, shards(): pl.pallas_call(functools.partial(finish_kernel, n_tgt, n_clus, per_req),...  1.45 us
  transfers between devices with their start and end apart: 20, of which 9 were waited for; matrix products, arithmetic and copies ran while one was open for 0% of the time, Pallas kernels for 0%

profile of v1, /device:TPU:0, one launch (start us, length us, event | category | flops | bytes accessed | tf_op | source)
XLA Modules:
  0.0 58.4 jit_solution(66468774860245974)
XLA Ops:
  0.6 0.0 copy-start.4
  0.6 0.8 %copy.17.req_ref = s32[8,2]{1,0:T(8,128)S(1)} copy(s32[8,2]{0,1:T(2,128)} %param.20) | data formatting | bytes 128 | tf_op args[8]
  1.4 0.0 copy-done.4
  1.4 0.6 %copy-done.11 = s32[8]{0:T(128)S(1)} copy-done((s32[8]{0:T(128)S(1)}, s32[8]{0:T(128)}, u32[]{:S(2)}) %copy-start.11) | copy-done | bytes 56
  2.1 0.0 copy-done.12
  2.1 0.8 %copy-done = f32[3,2048]{1,0:T(4,128)S(1)} copy-done((f32[3,2048]{1,0:T(4,128)S(1)}, f32[3,2048]{1,0:T(4,128)}, u32[]{:S(2)}) %copy-start) | copy-done | bytes 24600
  2.8 0.8 %copy-done.2 = f32[3,2048]{1,0:T(4,128)S(1)} copy-done((f32[3,2048]{1,0:T(4,128)S(1)}, f32[3,2048]{1,0:T(4,128)}, u32[]{:S(2)}) %copy-start.2) | copy-done | bytes 24600
  3.6 0.7 %copy-done.5 = f32[2048]{0:T(1024)S(1)} copy-done((f32[2048]{0:T(1024)S(1)}, f32[2048]{0:T(1024)}, u32[]{:S(2)}) %copy-start.5) | copy-done | bytes 8216
  4.3 0.7 %copy-done.7 = f32[2048]{0:T(1024)S(1)} copy-done((f32[2048]{0:T(1024)S(1)}, f32[2048]{0:T(1024)}, u32[]{:S(2)}) %copy-start.7) | copy-done | bytes 8216
  5.0 0.7 %copy-done.9 = f32[2048]{0:T(1024)S(1)} copy-done((f32[2048]{0:T(1024)S(1)}, f32[2048]{0:T(1024)}, u32[]{:S(2)}) %copy-start.9) | copy-done | bytes 8216
  5.7 0.7 %pack.1 = (f32[4,2048]{1,0:T(4,128)S(1)}, f32[4,2176]{1,0:T(4,128)S(1)}) custom-call(s32[8,2]{1,0:T(8,128)S(1)} %copy.17.req_ref, s32[8]{0:T(128)S(1)} %copy-done.11, s32[8]{0:T(128)S(1)} %copy-done.12, f32[3,2048]{1,0:T(4,128)S(1)} %copy-done, f32[1,2048]{1,0:T(1,128)S(1)} %bitcast.8, f32[1,2048]{1,0:T(1,128)S(1)} %bitcast.10, f32[3,2048]{1,0:T(4,128)S(1)} %copy-done.2, ...), custom_call_target="tpu_custom_call" | custom-call | tf_op jit(solution)/shard_map/pack/pallas_call | solution.py:222
  6.4 6.0 %collective-permute-start.9 = (f32[4,2176]{1,0:T(4,128)S(1)}, f32[4,2176]{1,0:T(4,128)S(1)}, u32[]{:S(2)}, u32[]{:S(2)}) collective-permute-start(f32[4,2176]{1,0:T(4,128)S(1)} %get-tuple-element.23.refs_4_.refs_12_), channel_id=1, source_target_pairs={{0,28},{4,24},{8,20},{12,16},{16,12},{20,8},{24,4},{28,0},{1,29},{... | collective-permute-start | bytes 104456 | tf_op jit(solution)/shard_map/ppermute | solution.py:34
  12.4 0.2 collective-permute-start.8
  12.7 0.5 collective-permute-start.2
  13.1 1.1 %collective-permute-start.1 = (f32[4,2048]{1,0:T(4,128)S(1)}, f32[4,2048]{1,0:T(4,128)S(1)}, u32[]{:S(2)}, u32[]{:S(2)}) collective-permute-start(f32[4,2048]{1,0:T(4,128)S(1)} %get-tuple-element.22.refs_0_), channel_id=1, source_target_pairs={{0,2},{1,3},{2,0},{3,1},{4,6},{5,7},{6,4},{7,5},{8,10},{9,11},{10,... | collective-permute-start | bytes 98312 | tf_op jit(solution)/shard_map/ppermute | solution.py:34
  14.2 0.3 collective-permute-start
  14.5 1.8 %collective-permute-done.2.refs_3_ = f32[4,2048]{1,0:T(4,128)S(1)} collective-permute-done((f32[4,2048]{1,0:T(4,128)S(1)}, f32[4,2048]{1,0:T(4,128)S(1)}, u32[]{:S(2)}, u32[]{:S(2)}) %collective-permute-start.2) | collective-permute-done | bytes 32800 | tf_op jit(solution)/shard_map/ppermute | solution.py:34
  16.3 0.8 %collective-permute-start.7 = (f32[4,2176]{1,0:T(4,128)S(1)}, f32[4,2176]{1,0:T(4,128)S(1)}, u32[]{:S(2)}, u32[]{:S(2)}) collective-permute-start(f32[4,2176]{1,0:T(4,128)S(1)} %get-tuple-element.23.refs_4_.refs_12_), channel_id=1, source_target_pairs={{0,20},{4,16},{8,28},{12,24},{16,4},{20,0},{24,12},{28,8},{1,21},{... | collective-permute-start | bytes 104456 | tf_op jit(solution)/shard_map/ppermute | solution.py:34
  17.0 0.1 collective-permute-done.1.refs_2_
  17.2 1.8 %collective-permute-start.6 = (f32[4,2176]{1,0:T(4,128)S(1)}, f32[4,2176]{1,0:T(4,128)S(1)}, u32[]{:S(2)}, u32[]{:S(2)}) collective-permute-start(f32[4,2176]{1,0:T(4,128)S(1)} %get-tuple-element.23.refs_4_.refs_12_), channel_id=1, source_target_pairs={{0,16},{4,20},{8,24},{12,28},{16,0},{20,4},{24,8},{28,12},{1,17},{... | collective-permute-start | bytes 104456 | tf_op jit(solution)/shard_map/ppermute | solution.py:34
  18.9 0.0 collective-permute-done.refs_1_
  18.9 2.5 %collective-permute-start.5 = (f32[4,2176]{1,0:T(4,128)S(1)}, f32[4,2176]{1,0:T(4,128)S(1)}, u32[]{:S(2)}, u32[]{:S(2)}) collective-permute-start(f32[4,2176]{1,0:T(4,128)S(1)} %get-tuple-element.23.refs_4_.refs_12_), channel_id=1, source_target_pairs={{0,12},{4,8},{8,4},{12,0},{16,28},{20,24},{24,20},{28,16},{1,13},{... | collective-permute-start | bytes 104456 | tf_op jit(solution)/shard_map/ppermute | solution.py:34
  21.4 0.0 collective-permute-done.9.refs_11_.refs_19_
  21.4 0.7 %collective-permute-start.4 = (f32[4,2176]{1,0:T(4,128)S(1)}, f32[4,2176]{1,0:T(4,128)S(1)}, u32[]{:S(2)}, u32[]{:S(2)}) collective-permute-start(f32[4,2176]{1,0:T(4,128)S(1)} %get-tuple-element.23.refs_4_.refs_12_), channel_id=1, source_target_pairs={{0,8},{4,12},{8,0},{12,4},{16,24},{20,28},{24,16},{28,20},{1,9},{5... | collective-permute-start | bytes 104456 | tf_op jit(solution)/shard_map/ppermute | solution.py:34
  22.1 0.0 collective-permute-done.8.refs_10_.refs_18_
  22.1 0.6 %collective-permute-start.3 = (f32[4,2176]{1,0:T(4,128)S(1)}, f32[4,2176]{1,0:T(4,128)S(1)}, u32[]{:S(2)}, u32[]{:S(2)}) collective-permute-start(f32[4,2176]{1,0:T(4,128)S(1)} %get-tuple-element.23.refs_4_.refs_12_), channel_id=1, source_target_pairs={{0,4},{4,0},{8,12},{12,8},{16,20},{20,16},{24,28},{28,24},{1,5},{5... | collective-permute-start | bytes 104456 | tf_op jit(solution)/shard_map/ppermute | solution.py:34
  22.8 0.1 pad_add_fusion.me_ref
  23.5 0.0 collective-permute-done.7.refs_9_.refs_17_
  23.5 0.0 collective-permute-done.6.refs_8_.refs_16_
  23.5 0.2 collective-permute-done.5.refs_7_.refs_15_
  23.8 1.6 %collective-permute-done.4.refs_6_.refs_14_ = f32[4,2176]{1,0:T(4,128)S(1)} collective-permute-done((f32[4,2176]{1,0:T(4,128)S(1)}, f32[4,2176]{1,0:T(4,128)S(1)}, u32[]{:S(2)}, u32[]{:S(2)}) %collective-permute-start.4) | collective-permute-done | bytes 34848 | tf_op jit(solution)/shard_map/ppermute | solution.py:34
  25.4 0.7 %collective-permute-done.3.refs_5_.refs_13_ = f32[4,2176]{1,0:T(4,128)S(1)} collective-permute-done((f32[4,2176]{1,0:T(4,128)S(1)}, f32[4,2176]{1,0:T(4,128)S(1)}, u32[]{:S(2)}, u32[]{:S(2)}) %collective-permute-start.3) | collective-permute-done | bytes 34848 | tf_op jit(solution)/shard_map/ppermute | solution.py:34
  26.1 0.0 copy-done.13
  26.1 0.0 copy-done.14
  26.1 0.0 copy-start.10
  26.1 10.6 %pairs.1 = (f32[4,2048]{1,0:T(4,128)S(1)}, f32[4,2048]{1,0:T(4,128)S(1)}, f32[4,2048]{1,0:T(4,128)S(1)}, f32[4,2048]{1,0:T(4,128)S(1)}, f32[4,512]{1,0:T(4,128)S...) custom-call(s32[2]{0:T(128)S(1)} %pad_add_fusion.me_ref, ...), custom_call_target="tpu_custom_call" | custom-call | tf_op jit(solution)/shard_map/pairs/pallas_call | solution.py:234
  36.7 0.1 collective-permute-start.13
  36.8 0.1 collective-permute-start.10
  36.9 0.1 collective-permute-start.11
  37.0 0.0 copy-start.8
  37.0 0.0 copy-start.6
  37.0 1.8 %collective-permute-start.12 = (f32[4,2048]{1,0:T(4,128)S(1)}, f32[4,2048]{1,0:T(4,128)S(1)}, u32[]{:S(2)}, u32[]{:S(2)}) collective-permute-start(f32[4,2048]{1,0:T(4,128)S(1)} %get-tuple-element.27), channel_id=1, source_target_pairs={{0,3},{1,2},{2,1},{3,0},{4,7},{5,6},{6,5},{7,4},{8,11},{9,10},{10,... | collective-permute-start | bytes 98312 | tf_op jit(solution)/shard_map/ppermute | solution.py:34
  38.8 1.3 %collective-permute-start.14 = (f32[4,512]{1,0:T(4,128)S(1)}, f32[4,512]{1,0:T(4,128)S(1)}, u32[]{:S(2)}, u32[]{:S(2)}) collective-permute-start(f32[4,512]{1,0:T(4,128)S(1)} %get-tuple-element.30), channel_id=1, source_target_pairs={{0,8},{4,12},{8,0},{12,4},{16,24},{20,28},{24,16},{28,20},{1,9},{5... | collective-permute-start | bytes 24584 | tf_op jit(solution)/shard_map/ppermute | solution.py:34
  40.1 0.3 collective-permute-done.13.refs_5_
  40.5 1.7 %collective-permute-start.15 = (f32[4,512]{1,0:T(4,128)S(1)}, f32[4,512]{1,0:T(4,128)S(1)}, u32[]{:S(2)}, u32[]{:S(2)}) collective-permute-start(f32[4,512]{1,0:T(4,128)S(1)} %get-tuple-element.31), channel_id=1, source_target_pairs={{0,12},{4,8},{8,4},{12,0},{16,28},{20,24},{24,20},{28,16},{1,13},{... | collective-permute-start | bytes 24584 | tf_op jit(solution)/shard_map/ppermute | solution.py:34
  42.2 0.2 collective-permute-done.14.refs_6_
  42.4 2.7 %collective-permute-start.16 = (f32[4,512]{1,0:T(4,128)S(1)}, f32[4,512]{1,0:T(4,128)S(1)}, u32[]{:S(2)}, u32[]{:S(2)}) collective-permute-start(f32[4,512]{1,0:T(4,128)S(1)} %get-tuple-element.32), channel_id=1, source_target_pairs={{0,16},{4,20},{8,24},{12,28},{16,0},{20,4},{24,8},{28,12},{1,17},{... | collective-permute-start | bytes 24584 | tf_op jit(solution)/shard_map/ppermute | solution.py:34
  45.1 0.0 collective-permute-done.15.refs_7_
  45.1 2.1 %collective-permute-start.17 = (f32[4,512]{1,0:T(4,128)S(1)}, f32[4,512]{1,0:T(4,128)S(1)}, u32[]{:S(2)}, u32[]{:S(2)}) collective-permute-start(f32[4,512]{1,0:T(4,128)S(1)} %get-tuple-element.33), channel_id=1, source_target_pairs={{0,20},{4,16},{8,28},{12,24},{16,4},{20,0},{24,12},{28,8},{1,21},{... | collective-permute-start | bytes 24584 | tf_op jit(solution)/shard_map/ppermute | solution.py:34
  47.2 0.0 collective-permute-done.16.refs_8_
  47.2 2.7 %collective-permute-start.18 = (f32[4,512]{1,0:T(4,128)S(1)}, f32[4,512]{1,0:T(4,128)S(1)}, u32[]{:S(2)}, u32[]{:S(2)}) collective-permute-start(f32[4,512]{1,0:T(4,128)S(1)} %get-tuple-element.34), channel_id=1, source_target_pairs={{0,24},{4,28},{8,16},{12,20},{16,8},{20,12},{24,0},{28,4},{1,25},{... | collective-permute-start | bytes 24584 | tf_op jit(solution)/shard_map/ppermute | solution.py:34
  49.9 0.7 %collective-permute-done.17.refs_9_ = f32[4,512]{1,0:T(4,128)S(1)} collective-permute-done((f32[4,512]{1,0:T(4,128)S(1)}, f32[4,512]{1,0:T(4,128)S(1)}, u32[]{:S(2)}, u32[]{:S(2)}) %collective-permute-start.17) | collective-permute-done | bytes 8224 | tf_op jit(solution)/shard_map/ppermute | solution.py:34
  50.5 2.4 %collective-permute-start.19 = (f32[4,512]{1,0:T(4,128)S(1)}, f32[4,512]{1,0:T(4,128)S(1)}, u32[]{:S(2)}, u32[]{:S(2)}) collective-permute-start(f32[4,512]{1,0:T(4,128)S(1)} %get-tuple-element.35), channel_id=1, source_target_pairs={{0,28},{4,24},{8,20},{12,16},{16,12},{20,8},{24,4},{28,0},{1,29},{... | collective-permute-start | bytes 24584 | tf_op jit(solution)/shard_map/ppermute | solution.py:34
  52.9 0.0 collective-permute-done.18.refs_10_
  52.9 4.0 %collective-permute-done.19.refs_11_ = f32[4,512]{1,0:T(4,128)S(1)} collective-permute-done((f32[4,512]{1,0:T(4,128)S(1)}, f32[4,512]{1,0:T(4,128)S(1)}, u32[]{:S(2)}, u32[]{:S(2)}) %collective-permute-start.19) | collective-permute-done | bytes 8224 | tf_op jit(solution)/shard_map/ppermute | solution.py:34
  56.9 0.0 collective-permute-done.10.refs_1_
  56.9 0.0 collective-permute-done.11.refs_2_
  56.9 0.0 collective-permute-done.12.refs_3_
  56.9 0.0 copy-done.1
  56.9 0.0 copy-done.3
  56.9 0.0 copy-done.10
  56.9 0.0 copy-done.8
  57.0 0.0 copy-done.6
  57.0 1.4 %finish.1 = (f32[3,2048]{1,0:T(4,128)}, f32[1,2048]{1,0:T(1,128)}, f32[3,2048]{1,0:T(4,128)}, f32[1,2048]{1,0:T(1,128)}) custom-call(s32[2]{0:T(128)S(1)} %pad_add_fusion.me_ref, s32[8]{0:T(128)S(1)} %copy-done.11, s32[8]{0:T(128)S(1)} %copy-done.12, f32[3,2048]{1,0:T(4,128)S(1)} %copy-done.1, f32[1,2048]{1,0:T(1,128)S(1)} %bitcast.9, ...), custom_call_target="tpu_custom_call" | custom-call | tf_op jit(solution)/shard_map/finish/pallas_call | solution.py:256
  (11 shorter events, 0.0 us)
Async XLA Ops:
  0.6 0.8 %copy-start.4 = (f32[2048]{0:T(1024)S(1)}, f32[2048]{0:T(1024)}, u32[]{:S(2)}) copy-start(f32[2048]{0:T(1024)} %param.13) | copy-start | bytes 24580
  1.4 0.7 %copy-start.11 = (s32[8]{0:T(128)S(1)}, s32[8]{0:T(128)}, u32[]{:S(2)}) copy-start(s32[8]{0:T(128)} %sc_ref.3) | copy-start | bytes 100
  1.4 0.7 %copy-start.12 = (s32[8]{0:T(128)S(1)}, s32[8]{0:T(128)}, u32[]{:S(2)}) copy-start(s32[8]{0:T(128)} %tc_ref.3) | copy-start | bytes 100
  2.1 0.8 %copy-start = (f32[3,2048]{1,0:T(4,128)S(1)}, f32[3,2048]{1,0:T(4,128)}, u32[]{:S(2)}) copy-start(f32[3,2048]{1,0:T(4,128)} %sp_ref.3) | copy-start | bytes 73732
  2.8 0.8 %copy-start.2 = (f32[3,2048]{1,0:T(4,128)S(1)}, f32[3,2048]{1,0:T(4,128)}, u32[]{:S(2)}) copy-start(f32[3,2048]{1,0:T(4,128)} %tp_ref.3) | copy-start | bytes 73732
  3.6 0.7 %copy-start.5 = (f32[2048]{0:T(1024)S(1)}, f32[2048]{0:T(1024)}, u32[]{:S(2)}) copy-start(f32[2048]{0:T(1024)} %param.14) | copy-start | bytes 24580
  4.3 0.7 %copy-start.7 = (f32[2048]{0:T(1024)S(1)}, f32[2048]{0:T(1024)}, u32[]{:S(2)}) copy-start(f32[2048]{0:T(1024)} %param.17) | copy-start | bytes 24580
  5.0 0.7 %copy-start.9 = (f32[2048]{0:T(1024)S(1)}, f32[2048]{0:T(1024)}, u32[]{:S(2)}) copy-start(f32[2048]{0:T(1024)} %param.18) | copy-start | bytes 24580
  6.4 15.0 %collective-permute-start.9 = (f32[4,2176]{1,0:T(4,128)S(1)}, f32[4,2176]{1,0:T(4,128)S(1)}, u32[]{:S(2)}, u32[]{:S(2)}) collective-permute-start(f32[4,2176]{1,0:T(4,128)S(1)} %get-tuple-element.23.refs_4_.refs_12_), channel_id=1, source_target_pairs={{0,28},{4,24},{8,20},{12,16},{16,12},{20,8},{24,4},{28,0},{1,29},{... | collective-permute-start | bytes 104456 | tf_op jit(solution)/shard_map/ppermute | solution.py:34
  12.4 9.7 %collective-permute-start.8 = (f32[4,2176]{1,0:T(4,128)S(1)}, f32[4,2176]{1,0:T(4,128)S(1)}, u32[]{:S(2)}, u32[]{:S(2)}) collective-permute-start(f32[4,2176]{1,0:T(4,128)S(1)} %get-tuple-element.23.refs_4_.refs_12_), channel_id=1, source_target_pairs={{0,24},{4,28},{8,16},{12,20},{16,8},{20,12},{24,0},{28,4},{1,25},{... | collective-permute-start | bytes 104456 | tf_op jit(solution)/shard_map/ppermute | solution.py:34
  12.7 3.6 %collective-permute-start.2 = (f32[4,2048]{1,0:T(4,128)S(1)}, f32[4,2048]{1,0:T(4,128)S(1)}, u32[]{:S(2)}, u32[]{:S(2)}) collective-permute-start(f32[4,2048]{1,0:T(4,128)S(1)} %get-tuple-element.22.refs_0_), channel_id=1, source_target_pairs={{0,3},{1,2},{2,1},{3,0},{4,7},{5,6},{6,5},{7,4},{8,11},{9,10},{10,... | collective-permute-start | bytes 98312 | tf_op jit(solution)/shard_map/ppermute | solution.py:34
  13.1 4.1 %collective-permute-start.1 = (f32[4,2048]{1,0:T(4,128)S(1)}, f32[4,2048]{1,0:T(4,128)S(1)}, u32[]{:S(2)}, u32[]{:S(2)}) collective-permute-start(f32[4,2048]{1,0:T(4,128)S(1)} %get-tuple-element.22.refs_0_), channel_id=1, source_target_pairs={{0,2},{1,3},{2,0},{3,1},{4,6},{5,7},{6,4},{7,5},{8,10},{9,11},{10,... | collective-permute-start | bytes 98312 | tf_op jit(solution)/shard_map/ppermute | solution.py:34
  14.2 4.7 %collective-permute-start = (f32[4,2048]{1,0:T(4,128)S(1)}, f32[4,2048]{1,0:T(4,128)S(1)}, u32[]{:S(2)}, u32[]{:S(2)}) collective-permute-start(f32[4,2048]{1,0:T(4,128)S(1)} %get-tuple-element.22.refs_0_), channel_id=1, source_target_pairs={{0,1},{1,0},{2,3},{3,2},{4,5},{5,4},{6,7},{7,6},{8,9},{9,8},{10,11... | collective-permute-start | bytes 98312 | tf_op jit(solution)/shard_map/ppermute | solution.py:34
  16.3 7.2 %collective-permute-start.7 = (f32[4,2176]{1,0:T(4,128)S(1)}, f32[4,2176]{1,0:T(4,128)S(1)}, u32[]{:S(2)}, u32[]{:S(2)}) collective-permute-start(f32[4,2176]{1,0:T(4,128)S(1)} %get-tuple-element.23.refs_4_.refs_12_), channel_id=1, source_target_pairs={{0,20},{4,16},{8,28},{12,24},{16,4},{20,0},{24,12},{28,8},{1,21},{... | collective-permute-start | bytes 104456 | tf_op jit(solution)/shard_map/ppermute | solution.py:34
  17.2 6.4 %collective-permute-start.6 = (f32[4,2176]{1,0:T(4,128)S(1)}, f32[4,2176]{1,0:T(4,128)S(1)}, u32[]{:S(2)}, u32[]{:S(2)}) collective-permute-start(f32[4,2176]{1,0:T(4,128)S(1)} %get-tuple-element.23.refs_4_.refs_12_), channel_id=1, source_target_pairs={{0,16},{4,20},{8,24},{12,28},{16,0},{20,4},{24,8},{28,12},{1,17},{... | collective-permute-start | bytes 104456 | tf_op jit(solution)/shard_map/ppermute | solution.py:34
  18.9 4.8 %collective-permute-start.5 = (f32[4,2176]{1,0:T(4,128)S(1)}, f32[4,2176]{1,0:T(4,128)S(1)}, u32[]{:S(2)}, u32[]{:S(2)}) collective-permute-start(f32[4,2176]{1,0:T(4,128)S(1)} %get-tuple-element.23.refs_4_.refs_12_), channel_id=1, source_target_pairs={{0,12},{4,8},{8,4},{12,0},{16,28},{20,24},{24,20},{28,16},{1,13},{... | collective-permute-start | bytes 104456 | tf_op jit(solution)/shard_map/ppermute | solution.py:34
  21.4 3.9 %collective-permute-start.4 = (f32[4,2176]{1,0:T(4,128)S(1)}, f32[4,2176]{1,0:T(4,128)S(1)}, u32[]{:S(2)}, u32[]{:S(2)}) collective-permute-start(f32[4,2176]{1,0:T(4,128)S(1)} %get-tuple-element.23.refs_4_.refs_12_), channel_id=1, source_target_pairs={{0,8},{4,12},{8,0},{12,4},{16,24},{20,28},{24,16},{28,20},{1,9},{5... | collective-permute-start | bytes 104456 | tf_op jit(solution)/shard_map/ppermute | solution.py:34
  22.1 3.9 %collective-permute-start.3 = (f32[4,2176]{1,0:T(4,128)S(1)}, f32[4,2176]{1,0:T(4,128)S(1)}, u32[]{:S(2)}, u32[]{:S(2)}) collective-permute-start(f32[4,2176]{1,0:T(4,128)S(1)} %get-tuple-element.23.refs_4_.refs_12_), channel_id=1, source_target_pairs={{0,4},{4,0},{8,12},{12,8},{16,20},{20,16},{24,28},{28,24},{1,5},{5... | collective-permute-start | bytes 104456 | tf_op jit(solution)/shard_map/ppermute | solution.py:34
  22.8 3.2 %copy-start.13 = (s32[32]{0:T(128)S(1)}, s32[32]{0:T(128)}, u32[]{:S(2)}) copy-start(s32[32]{0:T(128)} %ps_ref.1) | copy-start | bytes 388
  22.8 3.2 %copy-start.14 = (s32[32]{0:T(128)S(1)}, s32[32]{0:T(128)}, u32[]{:S(2)}) copy-start(s32[32]{0:T(128)} %pq_ref.1) | copy-start | bytes 388
  26.1 30.8 %copy-start.1 = (f32[3,2048]{1,0:T(4,128)S(1)}, f32[3,2048]{1,0:T(4,128)}, u32[]{:S(2)}) copy-start(f32[3,2048]{1,0:T(4,128)} %sp_ref.3) | copy-start | bytes 73732
  26.1 30.8 %copy-start.3 = (f32[3,2048]{1,0:T(4,128)S(1)}, f32[3,2048]{1,0:T(4,128)}, u32[]{:S(2)}) copy-start(f32[3,2048]{1,0:T(4,128)} %tp_ref.3) | copy-start | bytes 73732
  26.1 30.8 %copy-start.10 = (f32[2048]{0:T(1024)S(1)}, f32[2048]{0:T(1024)}, u32[]{:S(2)}) copy-start(f32[2048]{0:T(1024)} %param.18) | copy-start | bytes 24580
  36.7 3.7 %collective-permute-start.13 = (f32[4,512]{1,0:T(4,128)S(1)}, f32[4,512]{1,0:T(4,128)S(1)}, u32[]{:S(2)}, u32[]{:S(2)}) collective-permute-start(f32[4,512]{1,0:T(4,128)S(1)} %get-tuple-element.29), channel_id=1, source_target_pairs={{0,4},{4,0},{8,12},{12,8},{16,20},{20,16},{24,28},{28,24},{1,5},{5... | collective-permute-start | bytes 24584 | tf_op jit(solution)/shard_map/ppermute | solution.py:34
  36.8 20.1 %collective-permute-start.10 = (f32[4,2048]{1,0:T(4,128)S(1)}, f32[4,2048]{1,0:T(4,128)S(1)}, u32[]{:S(2)}, u32[]{:S(2)}) collective-permute-start(f32[4,2048]{1,0:T(4,128)S(1)} %get-tuple-element.25), channel_id=1, source_target_pairs={{0,1},{1,0},{2,3},{3,2},{4,5},{5,4},{6,7},{7,6},{8,9},{9,8},{10,11... | collective-permute-start | bytes 98312 | tf_op jit(solution)/shard_map/ppermute | solution.py:34
  36.9 20.0 %collective-permute-start.11 = (f32[4,2048]{1,0:T(4,128)S(1)}, f32[4,2048]{1,0:T(4,128)S(1)}, u32[]{:S(2)}, u32[]{:S(2)}) collective-permute-start(f32[4,2048]{1,0:T(4,128)S(1)} %get-tuple-element.26), channel_id=1, source_target_pairs={{0,2},{1,3},{2,0},{3,1},{4,6},{5,7},{6,4},{7,5},{8,10},{9,11},{10,... | collective-permute-start | bytes 98312 | tf_op jit(solution)/shard_map/ppermute | solution.py:34
  37.0 20.0 %copy-start.8 = (f32[2048]{0:T(1024)S(1)}, f32[2048]{0:T(1024)}, u32[]{:S(2)}) copy-start(f32[2048]{0:T(1024)} %param.17) | copy-start | bytes 24580
  37.0 20.0 %copy-start.6 = (f32[2048]{0:T(1024)S(1)}, f32[2048]{0:T(1024)}, u32[]{:S(2)}) copy-start(f32[2048]{0:T(1024)} %param.14) | copy-start | bytes 24580
  37.0 19.9 %collective-permute-start.12 = (f32[4,2048]{1,0:T(4,128)S(1)}, f32[4,2048]{1,0:T(4,128)S(1)}, u32[]{:S(2)}, u32[]{:S(2)}) collective-permute-start(f32[4,2048]{1,0:T(4,128)S(1)} %get-tuple-element.27), channel_id=1, source_target_pairs={{0,3},{1,2},{2,1},{3,0},{4,7},{5,6},{6,5},{7,4},{8,11},{9,10},{10,... | collective-permute-start | bytes 98312 | tf_op jit(solution)/shard_map/ppermute | solution.py:34
  38.8 3.7 %collective-permute-start.14 = (f32[4,512]{1,0:T(4,128)S(1)}, f32[4,512]{1,0:T(4,128)S(1)}, u32[]{:S(2)}, u32[]{:S(2)}) collective-permute-start(f32[4,512]{1,0:T(4,128)S(1)} %get-tuple-element.30), channel_id=1, source_target_pairs={{0,8},{4,12},{8,0},{12,4},{16,24},{20,28},{24,16},{28,20},{1,9},{5... | collective-permute-start | bytes 24584 | tf_op jit(solution)/shard_map/ppermute | solution.py:34
  40.5 4.6 %collective-permute-start.15 = (f32[4,512]{1,0:T(4,128)S(1)}, f32[4,512]{1,0:T(4,128)S(1)}, u32[]{:S(2)}, u32[]{:S(2)}) collective-permute-start(f32[4,512]{1,0:T(4,128)S(1)} %get-tuple-element.31), channel_id=1, source_target_pairs={{0,12},{4,8},{8,4},{12,0},{16,28},{20,24},{24,20},{28,16},{1,13},{... | collective-permute-start | bytes 24584 | tf_op jit(solution)/shard_map/ppermute | solution.py:34
  42.4 4.8 %collective-permute-start.16 = (f32[4,512]{1,0:T(4,128)S(1)}, f32[4,512]{1,0:T(4,128)S(1)}, u32[]{:S(2)}, u32[]{:S(2)}) collective-permute-start(f32[4,512]{1,0:T(4,128)S(1)} %get-tuple-element.32), channel_id=1, source_target_pairs={{0,16},{4,20},{8,24},{12,28},{16,0},{20,4},{24,8},{28,12},{1,17},{... | collective-permute-start | bytes 24584 | tf_op jit(solution)/shard_map/ppermute | solution.py:34
  45.1 5.4 %collective-permute-start.17 = (f32[4,512]{1,0:T(4,128)S(1)}, f32[4,512]{1,0:T(4,128)S(1)}, u32[]{:S(2)}, u32[]{:S(2)}) collective-permute-start(f32[4,512]{1,0:T(4,128)S(1)} %get-tuple-element.33), channel_id=1, source_target_pairs={{0,20},{4,16},{8,28},{12,24},{16,4},{20,0},{24,12},{28,8},{1,21},{... | collective-permute-start | bytes 24584 | tf_op jit(solution)/shard_map/ppermute | solution.py:34
  47.2 5.7 %collective-permute-start.18 = (f32[4,512]{1,0:T(4,128)S(1)}, f32[4,512]{1,0:T(4,128)S(1)}, u32[]{:S(2)}, u32[]{:S(2)}) collective-permute-start(f32[4,512]{1,0:T(4,128)S(1)} %get-tuple-element.34), channel_id=1, source_target_pairs={{0,24},{4,28},{8,16},{12,20},{16,8},{20,12},{24,0},{28,4},{1,25},{... | collective-permute-start | bytes 24584 | tf_op jit(solution)/shard_map/ppermute | solution.py:34
  50.5 6.3 %collective-permute-start.19 = (f32[4,512]{1,0:T(4,128)S(1)}, f32[4,512]{1,0:T(4,128)S(1)}, u32[]{:S(2)}, u32[]{:S(2)}) collective-permute-start(f32[4,512]{1,0:T(4,128)S(1)} %get-tuple-element.35), channel_id=1, source_target_pairs={{0,28},{4,24},{8,20},{12,16},{16,12},{20,8},{24,4},{28,0},{1,29},{... | collective-permute-start | bytes 24584 | tf_op jit(solution)/shard_map/ppermute | solution.py:34

commit v2 on v1

v2 whole, which is shorter than its diff:
```python
import functools
import math

import jax
import jax.numpy as jnp
from jax import lax
from jax.experimental import pallas as pl
from jax.experimental.pallas import tpu as pltpu
from jax.sharding import PartitionSpec as P

BLK = 256
LANES = 128
GROUP = 4

entropic = 0.05
LOG2E = math.log2(math.e)
SCALE = LOG2E / entropic
DEAD = -4096.0
PACK_VMEM = 60 * 2**20
MAIN_VMEM = 24 * 2**20

VMEM = pl.BlockSpec(memory_space=pltpu.VMEM)
SMEM = pl.BlockSpec(memory_space=pltpu.SMEM)


def step(i, k, n):
    return i ^ k if n & (n - 1) == 0 else (i + k) % n


def back(i, k, n):
    return i ^ k if n & (n - 1) == 0 else (i + n - k) % n


def split_axis(n):
    inner = 2 if n % 2 == 0 else 1
    return n // inner, inner


def moved(x, axis, k):
    n = lax.axis_size(axis)
    return lax.ppermute(x, axis, [(i, step(i, k, n)) for i in range(n)])


def moved_outer(x, axis, k):
    outer, inner = split_axis(lax.axis_size(axis))
    pairs = [(o * inner + i, step(o, k, outer) * inner + i) for o in range(outer) for i in range(inner)]
    return lax.ppermute(x, axis, pairs)


def moved_inner(x, axis, k):
    outer, inner = split_axis(lax.axis_size(axis))
    pairs = [(o * inner + i, o * inner + step(i, k, inner)) for o in range(outer) for i in range(inner)]
    return lax.ppermute(x, axis, pairs)


def live_row(count_ref, block):
    lane = lax.broadcasted_iota(jnp.int32, (1, BLK), 1)
    return lane < count_ref[block]


def pack_side(pos_ref, weight_ref, pot_ref, count_ref, out_ref):
    for b in range(count_ref.shape[0]):
        cols = slice(b * BLK, (b + 1) * BLK)
        pos = pos_ref[:, cols]
        norm = jnp.sum(pos * pos, axis=0, keepdims=True)
        expo = (pot_ref[:, cols] - 0.5 * norm) * SCALE + jnp.log(weight_ref[:, cols]) * LOG2E
        out_ref[0:3, cols] = pos
        out_ref[3:4, cols] = jnp.where(live_row(count_ref, b), expo, DEAD)


def pack_kernel(req_ref, sc_ref, tc_ref, sp_ref, sw_ref, so_ref, tp_ref, tw_ref, to_ref, src_ref, tgt_ref):
    pack_side(sp_ref, sw_ref, so_ref, sc_ref, src_ref)
    pack_side(tp_ref, tw_ref, to_ref, tc_ref, tgt_ref)
    per, rows = req_ref.shape
    own = tp_ref.shape[1]
    width = tgt_ref.shape[1] - own
    lane = lax.broadcasted_iota(jnp.int32, (4, width), 1)
    ids = jnp.zeros((4, width), jnp.float32)
    for r in range(rows):
        for m in range(per):
            ids = jnp.where(lane == r * per + m, req_ref[m, r].astype(jnp.float32), ids)
    tgt_ref[:, own:] = ids


def split3(x):
    high = x.astype(jnp.bfloat16).astype(jnp.float32)
    rest = x - high
    mid = rest.astype(jnp.bfloat16).astype(jnp.float32)
    return high, mid, rest - mid


def main_kernel(n_tgt, n_clus, me_ref, req_ref, ps_ref, pq_ref, pc_ref, *refs):
    outer, inner = split_axis(n_clus)
    src_in, refs = refs[:n_tgt], refs[n_tgt:]
    tgt_in, refs = refs[:outer], refs[outer:]
    src_out, refs = refs[:n_tgt], refs[n_tgt:]
    tgt_out, left, right, src_rows, tgt_rows, src_acc, tgt_acc, *kern_bufs = refs
    tgt_me, outer_me, inner_me = me_ref[0], me_ref[1], me_ref[2]
    per_dev = src_in[0].shape[1] // BLK
    n_src = n_tgt * per_dev
    per_req = req_ref.shape[0]
    last = lax.broadcasted_iota(jnp.int32, (4, BLK), 0) == 3
    pad = jnp.zeros((8, BLK), jnp.float32)

    for k in range(n_tgt):
        base = back(tgt_me, k, n_tgt) * per_dev
        for b in range(per_dev):
            high, mid, low = split3(src_in[k][:, b * BLK : (b + 1) * BLK])
            high1, mid1 = jnp.where(last, 1.0, high), jnp.where(last, 1.0, mid)
            left[base + b] = jnp.concatenate([high, high1, high1, mid, mid1, low, pad], 0).astype(jnp.bfloat16)
            src_rows[base + b] = jnp.concatenate([high1, jnp.where(last, 0.0, mid)], 0)
    dead = lax.broadcasted_iota(jnp.int32, (32, BLK), 0) == 3
    left[n_src] = jnp.where(dead, DEAD, 0.0).astype(jnp.bfloat16)
    src_rows[n_src] = pad
    src_acc[...] = jnp.zeros_like(src_acc)
    tgt_acc[...] = jnp.zeros_like(tgt_acc)

    for k in range(outer):
        for i in range(inner):
            owner = back(outer_me, k, outer) * inner + back(inner_me, i, inner)
            for m in range(per_req):
                block = req_ref[m, owner]
                raw = tgt_in[k][4 * i : 4 * i + 4, pl.ds(pl.multiple_of(block * BLK, BLK), BLK)]
                high, mid, _ = split3(raw)
                tgt_rows[owner * per_req + m] = jnp.concatenate(
                    [jnp.where(last, 1.0, high), jnp.where(last, 0.0, mid)], 0
                )
                high, mid, low = split3(jnp.where(last, raw, raw * SCALE))
                high1 = jnp.where(last, 1.0, high)
                wide = jnp.concatenate([high1, mid, low, high1, jnp.where(last, high, mid), high1, pad], 0)
                right[owner * per_req + m] = wide.T.astype(jnp.bfloat16)

    count = pc_ref[0]

    def pair_ids(pair):
        inside = jnp.minimum(pair, ps_ref.shape[0] - 1)
        return jnp.where(pair < count, ps_ref[inside], n_src), pq_ref[inside]

    def weigh(pair, buf, g):
        s, q = pair_ids(pair)
        kern = jnp.exp2(jnp.dot(right[q], left[s], preferred_element_type=jnp.float32))
        high = kern.astype(jnp.bfloat16)
        buf[g, 0] = high
        buf[g, 1] = (kern - high.astype(jnp.float32)).astype(jnp.bfloat16)

    def reduce(pair, buf, g):
        s, q = pair_ids(pair)
        high, low = buf[g, 0], buf[g, 1]
        y = tgt_rows[q].astype(jnp.bfloat16)
        x = src_rows[s].astype(jnp.bfloat16)
        dot = functools.partial(jnp.dot, preferred_element_type=jnp.float32)
        dot_t = functools.partial(
            lax.dot_general, dimension_numbers=(((1,), (1,)), ((), ())), preferred_element_type=jnp.float32
        )
        return s, q, dot(y, high) + dot(y, low), dot_t(x, high) + dot_t(x, low)

    bufs = len(kern_bufs)
    for g in range(GROUP):
        weigh(g, kern_bufs[0], g)

    def body(turn, carry):
        first = turn * bufs * GROUP
        for u in range(bufs):
            parts = []
            for g in range(GROUP):
                weigh(first + (u + 1) * GROUP + g, kern_bufs[(u + 1) % bufs], g)
                parts.append(reduce(first + u * GROUP + g, kern_bufs[u], g))
            for s, q, src_part, tgt_part in parts:
                src_acc[s] += src_part
                tgt_acc[q] += tgt_part
        return carry

    lax.fori_loop(0, (count + GROUP * bufs - 1) // (GROUP * bufs), body, 0)

    for k in range(n_tgt):
        base = step(tgt_me, k, n_tgt) * per_dev
        for b in range(per_dev):
            total = src_acc[base + b]
            src_out[k][:, b * BLK : (b + 1) * BLK] = total[0:4] + total[4:8]
    for r in range(n_clus):
        for m in range(per_req):
            total = tgt_acc[r * per_req + m]
            tgt_out[r, :, m * BLK : (m + 1) * BLK] = total[0:4] + total[4:8]


def finish_side(pos_ref, weight_ref, pot_ref, count_ref, sums, grad_pos_ref, grad_weight_ref):
    for b in range(count_ref.shape[0]):
        cols = slice(b * BLK, (b + 1) * BLK)
        total = sums(b, cols)
        mass = total[3:4]
        live = live_row(count_ref, b)
        grad_pos_ref[:, cols] = jnp.where(live, pos_ref[:, cols] * mass - total[0:3], 0.0)
        grad_weight_ref[:, cols] = jnp.where(
            live, pot_ref[:, cols] - entropic * mass / weight_ref[:, cols], 0.0
        )


def src_kernel(n_tgt, per_req, me_ref, count_ref, pos_ref, weight_ref, pot_ref, *refs):
    parts, refs = refs[:n_tgt], refs[n_tgt:]
    *tgt_in, grad_pos_ref, grad_weight_ref, ids_ref = refs
    finish_side(
        pos_ref,
        weight_ref,
        pot_ref,
        count_ref,
        lambda b, cols: sum(p[:, cols] for p in parts),
        grad_pos_ref,
        grad_weight_ref,
    )
    outer = len(tgt_in)
    inner = tgt_in[0].shape[0] // 4
    outer_me, inner_me = me_ref[1], me_ref[2]
    me = outer_me * inner + inner_me
    width = tgt_in[0].shape[1] - count_ref.shape[0] * BLK
    lane = lax.broadcasted_iota(jnp.int32, (1, width), 1)
    for k in range(outer):
        for i in range(inner):
            peer = back(outer_me, k, outer) * inner + back(inner_me, i, inner)
            row = tgt_in[k][4 * i : 4 * i + 1, tgt_in[k].shape[1] - width :]
            for m in range(per_req):
                block = jnp.sum(jnp.where(lane == me * per_req + m, row, 0.0), axis=1, keepdims=True)
                ids_ref[peer * per_req + m] = jnp.broadcast_to(block, (1, BLK))


def tgt_kernel(count_ref, pos_ref, weight_ref, pot_ref, parts_ref, ids_ref, grad_pos_ref, grad_weight_ref):
    per_req = parts_ref.shape[2] // BLK

    def sums(b, cols):
        total = jnp.zeros((4, BLK), jnp.float32)
        for r in range(parts_ref.shape[0]):
            for m in range(per_req):
                part = parts_ref[r, :, m * BLK : (m + 1) * BLK]
                total += jnp.where(ids_ref[r * per_req + m] == b, part, 0.0)
        return total

    finish_side(pos_ref, weight_ref, pot_ref, count_ref, sums, grad_pos_ref, grad_weight_ref)


def shards(
    src_pos,
    src_weight,
    src_pot,
    src_count,
    tgt_pos,
    tgt_weight,
    tgt_pot,
    tgt_count,
    requests,
    pair_src,
    pair_slot,
    pair_count,
):
    f32 = jnp.float32
    n_tgt, n_clus = lax.axis_size("tgt"), lax.axis_size("clus")
    outer, inner = split_axis(n_clus)
    ns, nt = src_pos.shape[1], tgt_pos.shape[1]
    n_src = n_tgt * (ns // BLK)
    per_req = requests.shape[1]
    slots = n_clus * per_req
    width = -(-slots // LANES) * LANES
    asked = requests.T
    small = pltpu.CompilerParams(vmem_limit_bytes=MAIN_VMEM)
    clus_me = lax.axis_index("clus")
    me = jnp.stack([lax.axis_index("tgt"), clus_me // inner, clus_me % inner]).astype(jnp.int32)
    src_side = (src_pos, src_weight.reshape(1, -1), src_pot.reshape(1, -1))
    tgt_side = (tgt_pos, tgt_weight.reshape(1, -1), tgt_pot.reshape(1, -1))

    src_pack, tgt_pack = pl.pallas_call(
        pack_kernel,
        name="pack",
        out_shape=(jax.ShapeDtypeStruct((4, ns), f32), jax.ShapeDtypeStruct((4, nt + width), f32)),
        in_specs=[SMEM] * 3 + [VMEM] * 6,
        out_specs=(VMEM, VMEM),
        compiler_params=pltpu.CompilerParams(vmem_limit_bytes=PACK_VMEM),
    )(asked, src_count, tgt_count, *src_side, *tgt_side)

    src_in = [src_pack] + [moved(src_pack, "tgt", k) for k in range(1, n_tgt)]
    near = jnp.concatenate([tgt_pack] + [moved_inner(tgt_pack, "clus", k) for k in range(1, inner)], 0)
    tgt_in = [near] + [moved_outer(near, "clus", k) for k in range(1, outer)]

    *src_out, tgt_out = pl.pallas_call(
        functools.partial(main_kernel, n_tgt, n_clus),
        name="pairs",
        out_shape=[jax.ShapeDtypeStruct((4, ns), f32)] * n_tgt
        + [jax.ShapeDtypeStruct((n_clus, 4, per_req * BLK), f32)],
        in_specs=[SMEM] * 5 + [VMEM] * (n_tgt + outer),
        out_specs=[VMEM] * (n_tgt + 1),
        scratch_shapes=[
            pltpu.VMEM((n_src + 1, 32, BLK), jnp.bfloat16),
            pltpu.VMEM((slots, BLK, 32), jnp.bfloat16),
            pltpu.VMEM((n_src + 1, 8, BLK), f32),
            pltpu.VMEM((slots, 8, BLK), f32),
            pltpu.VMEM((n_src + 1, 8, BLK), f32),
            pltpu.VMEM((slots, 8, BLK), f32),
            pltpu.VMEM((GROUP, 2, BLK, BLK), jnp.bfloat16),
            pltpu.VMEM((GROUP, 2, BLK, BLK), jnp.bfloat16),
        ],
        compiler_params=small,
    )(me, asked, pair_src, pair_slot, pair_count, *src_in, *tgt_in)

    src_parts = [src_out[0]] + [moved(src_out[k], "tgt", k) for k in range(1, n_tgt)]
    tgt_parts = lax.all_to_all(tgt_out, "clus", split_axis=0, concat_axis=0, tiled=True)

    grad_src_pos, grad_src_weight, ids = pl.pallas_call(
        functools.partial(src_kernel, n_tgt, per_req),
        name="finish_src",
        out_shape=(
            jax.ShapeDtypeStruct((3, ns), f32),
            jax.ShapeDtypeStruct((1, ns), f32),
            jax.ShapeDtypeStruct((slots, 1, BLK), f32),
        ),
        in_specs=[SMEM] * 2 + [VMEM] * (3 + n_tgt + outer),
        out_specs=(VMEM,) * 3,
        compiler_params=small,
    )(me, src_count, *src_side, *src_parts, *tgt_in)
    grad_tgt_pos, grad_tgt_weight = pl.pallas_call(
        tgt_kernel,
        name="finish_tgt",
        out_shape=(jax.ShapeDtypeStruct((3, nt), f32), jax.ShapeDtypeStruct((1, nt), f32)),
        in_specs=[SMEM] + [VMEM] * 5,
        out_specs=(VMEM,) * 2,
        compiler_params=small,
    )(tgt_count, *tgt_side, tgt_parts, ids)
    return grad_src_pos, grad_src_weight.reshape(-1), grad_tgt_pos, grad_tgt_weight.reshape(-1)


def solution(mesh):
    placed = (
        P(None, ("clus", "tgt")),
        P(("clus", "tgt")),
        P(("clus", "tgt")),
        P(("clus", "tgt")),
        P(None, ("clus", "tgt")),
        P(("clus", "tgt")),
        P(("clus", "tgt")),
        P(("clus", "tgt")),
        P(("clus", "tgt"), None),
        P(("clus", "tgt")),
        P(("clus", "tgt")),
        P(("clus", "tgt")),
    )
    return jax.shard_map(
        shards,
        mesh=mesh,
        in_specs=placed,
        out_specs=(
            P(None, ("clus", "tgt")),
            P(("clus", "tgt")),
            P(None, ("clus", "tgt")),
            P(("clus", "tgt")),
        ),
        check_vma=False,
    )
```

time: 58.8 us -> 36.1 us (0.61)
  starting transfers between devices: 29.3 us -> 15.4 us
  local copies, waits for them, and re-layouts: 5.07 us -> 0.06 us
  Pallas kernels: 12.8 us -> 10.3 us
  waiting for transfers between devices: 9.67 us -> 8.28 us
    ppermute x20 -> x10, starting transfers between devices: 29.3 us -> 11.4 us  [the longest x3 4.77 us: moved_outer(): return lax.ppermute(x, axis, pairs)]
    unnamed x31 -> x26, local copies, waits for them, and re-layouts: 5.07 us -> 0.06 us
    pallas_call x1, Pallas kernels: 10.6 us -> 6.21 us  [shards(): pl.pallas_call(functools.partial(main_kernel, n_tgt, n_clus), name='pairs...]
    all_to_all x0 -> x1, starting transfers between devices: none -> 4.02 us  [shards(): lax.all_to_all(tgt_out, 'clus', split_axis=0, concat_axis=0, tiled=True)]
    ppermute x20 -> x10, waiting for transfers between devices: 9.67 us -> 7.55 us  [the longest x3 4.17 us: moved_outer(): return lax.ppermute(x, axis, pairs)]
    pallas_call x1 -> x2, Pallas kernels: 1.45 us -> 2.58 us  [the longest x1 1.37 us: shards(): pl.pallas_call(tgt_kernel, name='finish_tgt', out_shape=(jax.ShapeDtypeSt...]
    pallas_call x1, Pallas kernels: 0.7 us -> 1.54 us  [shards(): pl.pallas_call(pack_kernel, name='pack', out_shape=(jax.ShapeDtypeStruct(...]
    all_to_all x0 -> x1, waiting for transfers between devices: none -> 0.73 us  [shards(): lax.all_to_all(tgt_out, 'clus', split_axis=0, concat_axis=0, tiled=True)]
  transfers between devices with their start and end apart: 20 -> 11, of which waited for: 9 -> 7; matrix products, arithmetic and copies ran while one was open for 0% -> 0% of each run, Pallas kernels for 0% -> 3%
where the time goes in v2:
time: 36.1 us; the launch traced here: 35.6 us
  starting transfers between devices  15.4 us (43%)
  Pallas kernels  10.3 us (29%)
  waiting for transfers between devices  8.28 us (23%)
  between operations  1.41 us (4%)
    pallas_call x1, Pallas kernels, shards(): pl.pallas_call(functools.partial(main_kernel, n_tgt, n_clus), name='pairs...  6.21 us
    ppermute x3, starting transfers between devices, moved_outer(): return lax.ppermute(x, axis, pairs)  4.77 us
    ppermute x3, waiting for transfers between devices, moved_outer(): return lax.ppermute(x, axis, pairs)  4.17 us
    all_to_all x1, starting transfers between devices, shards(): lax.all_to_all(tgt_out, 'clus', split_axis=0, concat_axis=0, tiled=True)  4.02 us
    ppermute x6, starting transfers between devices, moved(): return lax.ppermute(x, axis, [(i, step(i, k, n)) for i in range(n)])  3.72 us
    ppermute x6, waiting for transfers between devices, moved(): return lax.ppermute(x, axis, [(i, step(i, k, n)) for i in range(n)])  3.04 us
    ppermute x1, starting transfers between devices, moved_inner(): return lax.ppermute(x, axis, pairs)  2.94 us
    pallas_call x1, Pallas kernels, shards(): pl.pallas_call(pack_kernel, name='pack', out_shape=(jax.ShapeDtypeStruct(...  1.54 us
  transfers between devices with their start and end apart: 11, of which 7 were waited for; matrix products, arithmetic and copies ran while one was open for 0% of the time, Pallas kernels for 3%

profile of v2, /device:TPU:0, one launch (start us, length us, event | category | flops | bytes accessed | tf_op | source)
XLA Modules:
  0.0 35.6 jit_solution(8351318993397675728)
XLA Ops:
  0.6 1.5 %pack.1 = (f32[4,2048]{1,0:T(4,128)}, f32[4,2176]{1,0:T(4,128)}) custom-call(s32[2,8]{1,0:T(2,128)} %bitcast.18, s32[8]{0:T(128)} %count_ref.2, s32[8]{0:T(128)} %count_ref.3, f32[3,2048]{1,0:T(4,128)} %pos_ref.2, f32[1,2048]{1,0:T(1,128)} %bitcast.10, f32[1,2048]{1,0:T(1,128)} %bitcast.12, f32[3,2048]{1,0:T(4,128)} %pos_ref.3, f32[1,2048]{1,0:T(1,128)} %bitcast.14, ...), custom_call_target="tpu_custom_call" | custom-call | tf_op jit(solution)/shard_map/pack/pallas_call | solution.py:268
  2.2 0.0 copy-start.12
  2.2 2.9 %collective-permute-start.3 = (f32[4,2176]{1,0:T(4,128)}, f32[4,2176]{1,0:T(4,128)S(1)}, u32[]{:S(2)}, u32[]{:S(2)}) collective-permute-start(f32[4,2176]{1,0:T(4,128)} %get-tuple-element.17), channel_id=1, source_target_pairs={{0,4},{4,0},{8,12},{12,8},{16,20},{20,16},{24,28},{28,24},{1,5},{5... | collective-permute-start | bytes 104456 | tf_op jit(solution)/shard_map/ppermute | solution.py:53
  5.1 0.7 %collective-permute-start.2 = (f32[4,2048]{1,0:T(4,128)}, f32[4,2048]{1,0:T(4,128)S(1)}, u32[]{:S(2)}, u32[]{:S(2)}) collective-permute-start(f32[4,2048]{1,0:T(4,128)} %get-tuple-element.16.refs_0_), channel_id=1, source_target_pairs={{0,3},{1,2},{2,1},{3,0},{4,7},{5,6},{6,5},{7,4},{8,11},{9,10},{10,... | collective-permute-start | bytes 98312 | tf_op jit(solution)/shard_map/ppermute | solution.py:41
  5.8 0.9 %collective-permute-start.1 = (f32[4,2048]{1,0:T(4,128)}, f32[4,2048]{1,0:T(4,128)S(1)}, u32[]{:S(2)}, u32[]{:S(2)}) collective-permute-start(f32[4,2048]{1,0:T(4,128)} %get-tuple-element.16.refs_0_), channel_id=1, source_target_pairs={{0,2},{1,3},{2,0},{3,1},{4,6},{5,7},{6,4},{7,5},{8,10},{9,11},{10,... | collective-permute-start | bytes 98312 | tf_op jit(solution)/shard_map/ppermute | solution.py:41
  6.7 0.3 collective-permute-start
  7.0 0.0 copy-start.4
  7.0 0.3 collective-permute-done.3
  7.3 0.0 copy-done.12
  7.3 4.1 %collective-permute-start.6 = (f32[8,2176]{1,0:T(8,128)S(1)}, f32[8,2176]{1,0:T(8,128)S(1)}, u32[]{:S(2)}, u32[]{:S(2)}) collective-permute-start(f32[8,2176]{1,0:T(8,128)S(1)} %pad_maximum_fusion.refs_4_), channel_id=1, source_target_pairs={{0,24},{4,28},{8,16},{12,20},{16,8},{20,12},{24,0},{28,4},{1,25},{... | collective-permute-start | bytes 208904 | tf_op jit(solution)/shard_map/ppermute | solution.py:47
  11.5 0.0 collective-permute-start.5
  11.5 0.0 collective-permute-done.2.refs_3_
  11.5 0.6 %collective-permute-start.4 = (f32[8,2176]{1,0:T(8,128)S(1)}, f32[8,2176]{1,0:T(8,128)S(1)}, u32[]{:S(2)}, u32[]{:S(2)}) collective-permute-start(f32[8,2176]{1,0:T(8,128)S(1)} %pad_maximum_fusion.refs_4_), channel_id=1, source_target_pairs={{0,8},{4,12},{8,0},{12,4},{16,24},{20,28},{24,16},{28,20},{1,9},{5... | collective-permute-start | bytes 208904 | tf_op jit(solution)/shard_map/ppermute | solution.py:47
  12.1 0.0 copy-start.11
  12.1 0.1 pad_add_fusion.me_ref
  12.2 0.0 copy-start.7
  12.2 0.0 copy-start.10
  12.9 0.0 collective-permute-done.1.refs_2_
  12.9 0.0 collective-permute-done.refs_1_
  12.9 1.6 %collective-permute-done.6.refs_7_ = f32[8,2176]{1,0:T(8,128)S(1)} collective-permute-done((f32[8,2176]{1,0:T(8,128)S(1)}, f32[8,2176]{1,0:T(8,128)S(1)}, u32[]{:S(2)}, u32[]{:S(2)}) %collective-permute-start.6) | collective-permute-done | bytes 69664 | tf_op jit(solution)/shard_map/ppermute | solution.py:47
  14.5 2.5 %collective-permute-done.5.refs_6_ = f32[8,2176]{1,0:T(8,128)S(1)} collective-permute-done((f32[8,2176]{1,0:T(8,128)S(1)}, f32[8,2176]{1,0:T(8,128)S(1)}, u32[]{:S(2)}, u32[]{:S(2)}) %collective-permute-start.5) | collective-permute-done | bytes 69664 | tf_op jit(solution)/shard_map/ppermute | solution.py:47
  17.0 0.1 collective-permute-done.4.refs_5_
  17.1 0.0 copy-done.4
  17.1 0.0 copy-done.11
  17.1 0.0 copy-done.7
  17.1 0.0 copy-done.10
  17.1 6.2 %pairs.1 = (f32[4,2048]{1,0:T(4,128)S(1)}, f32[4,2048]{1,0:T(4,128)S(1)}, f32[4,2048]{1,0:T(4,128)S(1)}, f32[4,2048]{1,0:T(4,128)S(1)}, f32[8,4,512]{2,1,0:T(4,128)}) custom-call(s32[3]{0:T(128)S(1)} %pad_add_fusion.me_ref, s32[2,8]{1,0:T(2,128)S(1)} %bitcast.19, s32[32]{0:T(128)S(1)} %copy-done.10, s32[32]{0:T(128)S(1)} %copy-done.11, s32[1]{0:T(128)S(6)} %copy.16.pc_ref, ...), custom_call_target="tpu_custom_call" | custom-call | tf_op jit(solution)/shard_map/pairs/pallas_call | solution.py:281
  23.3 0.0 copy-start
  23.3 0.0 copy-start.2
  23.3 0.0 copy-start.3
  23.3 4.0 %all-to-all-start = ((f32[8,4,512]{2,1,0:T(4,128)}), f32[8,4,512]{2,1,0:T(4,128)S(1)}, u32[]{:S(2)}, u32[]{:S(2)}) async-start(f32[8,4,512]{2,1,0:T(4,128)} %get-tuple-element.24), calls=%async_computation | async-start | bytes 131072 | tf_op jit(solution)/shard_map/all_to_all | solution.py:302
  27.3 0.0 collective-permute-start.7
  27.3 1.5 %collective-permute-start.8 = (f32[4,2048]{1,0:T(4,128)S(1)}, f32[4,2048]{1,0:T(4,128)S(1)}, u32[]{:S(2)}, u32[]{:S(2)}) collective-permute-start(f32[4,2048]{1,0:T(4,128)S(1)} %get-tuple-element.20), channel_id=1, source_target_pairs={{0,2},{1,3},{2,0},{3,1},{4,6},{5,7},{6,4},{7,5},{8,10},{9,11},{10,... | collective-permute-start | bytes 98312 | tf_op jit(solution)/shard_map/ppermute | solution.py:41
  28.9 0.0 copy-start.8
  28.9 0.3 collective-permute-start.9
  29.2 0.0 collective-permute-done.7.refs_1_
  29.2 2.1 %collective-permute-done.8.refs_2_ = f32[4,2048]{1,0:T(4,128)S(1)} collective-permute-done((f32[4,2048]{1,0:T(4,128)S(1)}, f32[4,2048]{1,0:T(4,128)S(1)}, u32[]{:S(2)}, u32[]{:S(2)}) %collective-permute-start.8) | collective-permute-done | bytes 32800 | tf_op jit(solution)/shard_map/ppermute | solution.py:41
  31.3 0.9 %collective-permute-done.9.refs_3_ = f32[4,2048]{1,0:T(4,128)S(1)} collective-permute-done((f32[4,2048]{1,0:T(4,128)S(1)}, f32[4,2048]{1,0:T(4,128)S(1)}, u32[]{:S(2)}, u32[]{:S(2)}) %collective-permute-start.9) | collective-permute-done | bytes 32800 | tf_op jit(solution)/shard_map/ppermute | solution.py:41
  32.2 0.0 copy-done
  32.2 0.0 copy-done.2
  32.2 0.0 copy-done.3
  32.2 0.0 copy-done.8
  32.2 0.0 copy-start.1
  32.3 0.0 copy-start.5
  32.3 0.0 copy-start.6
  32.3 1.2 %finish_src.1 = (f32[3,2048]{1,0:T(4,128)}, f32[1,2048]{1,0:T(1,128)}, f32[16,1,256]{2,1,0:T(1,128)S(1)}) custom-call(s32[3]{0:T(128)S(1)} %pad_add_fusion.me_ref, s32[8]{0:T(128)S(1)} %copy-done.8, f32[3,2048]{1,0:T(4,128)S(1)} %copy-done, f32[1,2048]{1,0:T(1,128)S(1)} %bitcast.11, f32[1,2048]{1,0:T(1,128)S(1)} %bitcast.13, ...), custom_call_target="tpu_custom_call" | custom-call | tf_op jit(solution)/shard_map/finish_src/pallas_call | solution.py:304
  33.5 0.0 copy-start.9
  33.5 0.7 %all-to-all-done.parts_ref = f32[8,4,512]{2,1,0:T(4,128)S(1)} async-done(((f32[8,4,512]{2,1,0:T(4,128)}), f32[8,4,512]{2,1,0:T(4,128)S(1)}, u32[]{:S(2)}, u32[]{:S(2)}) %all-to-all-start) | async-done | bytes 65568 | tf_op jit(solution)/shard_map/all_to_all | solution.py:302
  34.2 0.0 copy-done.1
  34.2 0.0 copy-done.5
  34.2 0.0 copy-done.6
  34.2 0.0 copy-done.9
  34.2 1.4 %finish_tgt.1 = (f32[3,2048]{1,0:T(4,128)}, f32[1,2048]{1,0:T(1,128)}) custom-call(s32[8]{0:T(128)S(1)} %copy-done.9, f32[3,2048]{1,0:T(4,128)S(1)} %copy-done.1, f32[1,2048]{1,0:T(1,128)S(1)} %bitcast.15, f32[1,2048]{1,0:T(1,128)S(1)} %bitcast.17, f32[8,4,512]{2,1,0:T(4,128)S(1)} %all-to-all-done.parts_ref, f32[16,1,256]{2,1,0:T(1,128)S(1)} %get-tuple-element.25.ids_ref), custom_call_target="tpu_custom_call" | custom-call | tf_op jit(solution)/shard_map/finish_tgt/pallas_call | solution.py:316
  (1 shorter events, 0.0 us)
Async XLA Ops:
  2.2 5.1 %copy-start.12 = (f32[4,2176]{1,0:T(4,128)S(1)}, f32[4,2176]{1,0:T(4,128)}, u32[]{:S(2)}) copy-start(f32[4,2176]{1,0:T(4,128)} %get-tuple-element.17) | copy-start | bytes 104452
  2.2 5.1 %collective-permute-start.3 = (f32[4,2176]{1,0:T(4,128)}, f32[4,2176]{1,0:T(4,128)S(1)}, u32[]{:S(2)}, u32[]{:S(2)}) collective-permute-start(f32[4,2176]{1,0:T(4,128)} %get-tuple-element.17), channel_id=1, source_target_pairs={{0,4},{4,0},{8,12},{12,8},{16,20},{20,16},{24,28},{28,24},{1,5},{5... | collective-permute-start | bytes 104456 | tf_op jit(solution)/shard_map/ppermute | solution.py:53
  5.1 6.4 %collective-permute-start.2 = (f32[4,2048]{1,0:T(4,128)}, f32[4,2048]{1,0:T(4,128)S(1)}, u32[]{:S(2)}, u32[]{:S(2)}) collective-permute-start(f32[4,2048]{1,0:T(4,128)} %get-tuple-element.16.refs_0_), channel_id=1, source_target_pairs={{0,3},{1,2},{2,1},{3,0},{4,7},{5,6},{6,5},{7,4},{8,11},{9,10},{10,... | collective-permute-start | bytes 98312 | tf_op jit(solution)/shard_map/ppermute | solution.py:41
  5.8 7.1 %collective-permute-start.1 = (f32[4,2048]{1,0:T(4,128)}, f32[4,2048]{1,0:T(4,128)S(1)}, u32[]{:S(2)}, u32[]{:S(2)}) collective-permute-start(f32[4,2048]{1,0:T(4,128)} %get-tuple-element.16.refs_0_), channel_id=1, source_target_pairs={{0,2},{1,3},{2,0},{3,1},{4,6},{5,7},{6,4},{7,5},{8,10},{9,11},{10,... | collective-permute-start | bytes 98312 | tf_op jit(solution)/shard_map/ppermute | solution.py:41
  6.7 6.2 %collective-permute-start = (f32[4,2048]{1,0:T(4,128)}, f32[4,2048]{1,0:T(4,128)S(1)}, u32[]{:S(2)}, u32[]{:S(2)}) collective-permute-start(f32[4,2048]{1,0:T(4,128)} %get-tuple-element.16.refs_0_), channel_id=1, source_target_pairs={{0,1},{1,0},{2,3},{3,2},{4,5},{5,4},{6,7},{7,6},{8,9},{9,8},{10,11... | collective-permute-start | bytes 98312 | tf_op jit(solution)/shard_map/ppermute | solution.py:41
  7.0 10.1 %copy-start.4 = (f32[4,2048]{1,0:T(4,128)S(1)}, f32[4,2048]{1,0:T(4,128)}, u32[]{:S(2)}) copy-start(f32[4,2048]{1,0:T(4,128)} %get-tuple-element.16.refs_0_) | copy-start | bytes 98308
  7.3 7.2 %collective-permute-start.6 = (f32[8,2176]{1,0:T(8,128)S(1)}, f32[8,2176]{1,0:T(8,128)S(1)}, u32[]{:S(2)}, u32[]{:S(2)}) collective-permute-start(f32[8,2176]{1,0:T(8,128)S(1)} %pad_maximum_fusion.refs_4_), channel_id=1, source_target_pairs={{0,24},{4,28},{8,16},{12,20},{16,8},{20,12},{24,0},{28,4},{1,25},{... | collective-permute-start | bytes 208904 | tf_op jit(solution)/shard_map/ppermute | solution.py:47
  11.5 5.5 %collective-permute-start.5 = (f32[8,2176]{1,0:T(8,128)S(1)}, f32[8,2176]{1,0:T(8,128)S(1)}, u32[]{:S(2)}, u32[]{:S(2)}) collective-permute-start(f32[8,2176]{1,0:T(8,128)S(1)} %pad_maximum_fusion.refs_4_), channel_id=1, source_target_pairs={{0,16},{4,20},{8,24},{12,28},{16,0},{20,4},{24,8},{28,12},{1,17},{... | collective-permute-start | bytes 208904 | tf_op jit(solution)/shard_map/ppermute | solution.py:47
  11.5 5.6 %collective-permute-start.4 = (f32[8,2176]{1,0:T(8,128)S(1)}, f32[8,2176]{1,0:T(8,128)S(1)}, u32[]{:S(2)}, u32[]{:S(2)}) collective-permute-start(f32[8,2176]{1,0:T(8,128)S(1)} %pad_maximum_fusion.refs_4_), channel_id=1, source_target_pairs={{0,8},{4,12},{8,0},{12,4},{16,24},{20,28},{24,16},{28,20},{1,9},{5... | collective-permute-start | bytes 208904 | tf_op jit(solution)/shard_map/ppermute | solution.py:47
  12.1 5.0 %copy-start.11 = (s32[32]{0:T(128)S(1)}, s32[32]{0:T(128)}, u32[]{:S(2)}) copy-start(s32[32]{0:T(128)} %pq_ref.1) | copy-start | bytes 388
  12.2 4.9 %copy-start.7 = (s32[8,2]{0,1:T(2,128)S(1)}, s32[8,2]{0,1:T(2,128)}, u32[]{:S(2)}) copy-start(s32[8,2]{0,1:T(2,128)} %param.20) | copy-start | bytes 196
  12.2 4.9 %copy-start.10 = (s32[32]{0:T(128)S(1)}, s32[32]{0:T(128)}, u32[]{:S(2)}) copy-start(s32[32]{0:T(128)} %ps_ref.1) | copy-start | bytes 388
  23.3 8.9 %copy-start = (f32[3,2048]{1,0:T(4,128)S(1)}, f32[3,2048]{1,0:T(4,128)}, u32[]{:S(2)}) copy-start(f32[3,2048]{1,0:T(4,128)} %pos_ref.2) | copy-start | bytes 73732
  23.3 8.9 %copy-start.2 = (f32[2048]{0:T(1024)S(1)}, f32[2048]{0:T(1024)}, u32[]{:S(2)}) copy-start(f32[2048]{0:T(1024)} %param.13) | copy-start | bytes 24580
  23.3 8.9 %copy-start.3 = (f32[2048]{0:T(1024)S(1)}, f32[2048]{0:T(1024)}, u32[]{:S(2)}) copy-start(f32[2048]{0:T(1024)} %param.14) | copy-start | bytes 24580
  23.3 10.9 %all-to-all-start = ((f32[8,4,512]{2,1,0:T(4,128)}), f32[8,4,512]{2,1,0:T(4,128)S(1)}, u32[]{:S(2)}, u32[]{:S(2)}) async-start(f32[8,4,512]{2,1,0:T(4,128)} %get-tuple-element.24), calls=%async_computation | async-start | bytes 131072 | tf_op jit(solution)/shard_map/all_to_all | solution.py:302
  27.3 1.9 %collective-permute-start.7 = (f32[4,2048]{1,0:T(4,128)S(1)}, f32[4,2048]{1,0:T(4,128)S(1)}, u32[]{:S(2)}, u32[]{:S(2)}) collective-permute-start(f32[4,2048]{1,0:T(4,128)S(1)} %get-tuple-element.19), channel_id=1, source_target_pairs={{0,1},{1,0},{2,3},{3,2},{4,5},{5,4},{6,7},{7,6},{8,9},{9,8},{10,11... | collective-permute-start | bytes 98312 | tf_op jit(solution)/shard_map/ppermute | solution.py:41
  27.3 4.0 %collective-permute-start.8 = (f32[4,2048]{1,0:T(4,128)S(1)}, f32[4,2048]{1,0:T(4,128)S(1)}, u32[]{:S(2)}, u32[]{:S(2)}) collective-permute-start(f32[4,2048]{1,0:T(4,128)S(1)} %get-tuple-element.20), channel_id=1, source_target_pairs={{0,2},{1,3},{2,0},{3,1},{4,6},{5,7},{6,4},{7,5},{8,10},{9,11},{10,... | collective-permute-start | bytes 98312 | tf_op jit(solution)/shard_map/ppermute | solution.py:41
  28.9 3.4 %copy-start.8 = (s32[8]{0:T(128)S(1)}, s32[8]{0:T(128)}, u32[]{:S(2)}) copy-start(s32[8]{0:T(128)} %count_ref.2) | copy-start | bytes 100
  28.9 3.4 %collective-permute-start.9 = (f32[4,2048]{1,0:T(4,128)S(1)}, f32[4,2048]{1,0:T(4,128)S(1)}, u32[]{:S(2)}, u32[]{:S(2)}) collective-permute-start(f32[4,2048]{1,0:T(4,128)S(1)} %get-tuple-element.21), channel_id=1, source_target_pairs={{0,3},{1,2},{2,1},{3,0},{4,7},{5,6},{6,5},{7,4},{8,11},{9,10},{10,... | collective-permute-start | bytes 98312 | tf_op jit(solution)/shard_map/ppermute | solution.py:41
  32.2 2.0 %copy-start.1 = (f32[3,2048]{1,0:T(4,128)S(1)}, f32[3,2048]{1,0:T(4,128)}, u32[]{:S(2)}) copy-start(f32[3,2048]{1,0:T(4,128)} %pos_ref.3) | copy-start | bytes 73732
  32.3 2.0 %copy-start.5 = (f32[2048]{0:T(1024)S(1)}, f32[2048]{0:T(1024)}, u32[]{:S(2)}) copy-start(f32[2048]{0:T(1024)} %param.17) | copy-start | bytes 24580
  32.3 2.0 %copy-start.6 = (f32[2048]{0:T(1024)S(1)}, f32[2048]{0:T(1024)}, u32[]{:S(2)}) copy-start(f32[2048]{0:T(1024)} %param.18) | copy-start | bytes 24580
  33.5 0.7 %copy-start.9 = (s32[8]{0:T(128)S(1)}, s32[8]{0:T(128)}, u32[]{:S(2)}) copy-start(s32[8]{0:T(128)} %count_ref.3) | copy-start | bytes 100

commit v3 on v2

--- a/solution.py
+++ b/solution.py
@@ -10,7 +10,8 @@
 
 BLK = 256
 LANES = 128
-GROUP = 4
+GROUP = 2
+BUFS = 4
 
 entropic = 0.05
 LOG2E = math.log2(math.e)
@@ -89,21 +90,26 @@
     return high, mid, rest - mid
 
 
-def main_kernel(n_tgt, n_clus, me_ref, req_ref, ps_ref, pq_ref, pc_ref, *refs):
-    outer, inner = split_axis(n_clus)
-    src_in, refs = refs[:n_tgt], refs[n_tgt:]
-    tgt_in, refs = refs[:outer], refs[outer:]
-    src_out, refs = refs[:n_tgt], refs[n_tgt:]
-    tgt_out, left, right, src_rows, tgt_rows, src_acc, tgt_acc, *kern_bufs = refs
-    tgt_me, outer_me, inner_me = me_ref[0], me_ref[1], me_ref[2]
-    per_dev = src_in[0].shape[1] // BLK
-    n_src = n_tgt * per_dev
-    per_req = req_ref.shape[0]
+def stages(outer):
+    cuts = sorted({0, min(1, outer), min(2, outer), outer})
+    return list(zip(cuts[:-1], cuts[1:]))
+
+
+def dot(x, y):
+    return jnp.dot(x, y, preferred_element_type=jnp.float32)
+
+
+def dot_t(x, y):
+    return lax.dot_general(x, y, (((1,), (1,)), ((), ())), preferred_element_type=jnp.float32)
+
+
+def prepare_src(tgt_me, src_in, left, src_rows):
     last = lax.broadcasted_iota(jnp.int32, (4, BLK), 0) == 3
     pad = jnp.zeros((8, BLK), jnp.float32)
-
-    for k in range(n_tgt):
-        base = back(tgt_me, k, n_tgt) * per_dev
+    per_dev = src_in[0].shape[1] // BLK
+    n_src = len(src_in) * per_dev
+    for k in range(len(src_in)):
+        base = back(tgt_me, k, len(src_in)) * per_dev
         for b in range(per_dev):
             high, mid, low = split3(src_in[k][:, b * BLK : (b + 1) * BLK])
             high1, mid1 = jnp.where(last, 1.0, high), jnp.where(last, 1.0, mid)
@@ -112,46 +118,89 @@
     dead = lax.broadcasted_iota(jnp.int32, (32, BLK), 0) == 3
     left[n_src] = jnp.where(dead, DEAD, 0.0).astype(jnp.bfloat16)
     src_rows[n_src] = pad
-    src_acc[...] = jnp.zeros_like(src_acc)
+
+
+def prepare_tgt(owner, rows, req_ref, tgt_in, right, tgt_rows):
+    last = lax.broadcasted_iota(jnp.int32, (4, BLK), 0) == 3
+    pad = jnp.zeros((8, BLK), jnp.float32)
+    per_req = req_ref.shape[0]
+    for m in range(per_req):
+        block = req_ref[m, owner]
+        raw = tgt_in[rows, pl.ds(pl.multiple_of(block * BLK, BLK), BLK)]
+        high, mid, _ = split3(raw)
+        tgt_rows[owner * per_req + m] = jnp.concatenate(
+            [jnp.where(last, 1.0, high), jnp.where(last, 0.0, mid)], 0
+        )
+        high, mid, low = split3(jnp.where(last, raw, raw * SCALE))
+        high1 = jnp.where(last, 1.0, high)
+        wide = jnp.concatenate([high1, mid, low, high1, jnp.where(last, high, mid), high1, pad], 0)
+        right[owner * per_req + m] = wide.T.astype(jnp.bfloat16)
+
+
+def pairs_kernel(n_tgt, n_clus, first, stop, me_ref, req_ref, ps_ref, pq_ref, pc_ref, *refs):
+    outer, inner = split_axis(n_clus)
+    per_req = req_ref.shape[0]
+    begins, ends = first == 0, stop == outer
+    refs = list(refs)
+    take = lambda n: [refs.pop(0) for _ in range(n)]
+    if begins:
+        src_in = take(n_tgt)
+    else:
+        left, src_rows, src_sums = take(3)
+    tgt_in = take(stop - first)
+    if ends:
+        done = take(len(stages(outer)) - 1)
+        src_out, (tgt_out,) = take(n_tgt), take(1)
+        (src_acc,) = take(1)
+    else:
+        if begins:
+            left, src_rows = take(2)
+        src_acc, tgt_out = take(2)
+    if begins and ends:
+        left, src_rows = take(2)
+    right, tgt_rows, tgt_acc, chosen, *kern_bufs = refs
+    tgt_me, outer_me, inner_me = me_ref[0], me_ref[1], me_ref[2]
+    n_src = left.shape[0] - 1
+
+    count = pc_ref[0]
+    total = 0
+    for pair in range(ps_ref.shape[0]):
+        place = lax.div(pq_ref[pair], per_req * inner)
+        away = (place ^ outer_me) if outer & (outer - 1) == 0 else lax.rem(outer_me - place + outer, outer)
+        chosen[total] = pair
+        total = total + ((pair < count) & (away >= first) & (away < stop)).astype(jnp.int32)
+
+    if begins:
+        prepare_src(tgt_me, src_in, left, src_rows)
+        src_acc[...] = jnp.zeros_like(src_acc)
+    else:
+        src_acc[...] = src_sums[...]
     tgt_acc[...] = jnp.zeros_like(tgt_acc)
-
-    for k in range(outer):
+    owners = []
+    for k in range(first, stop):
         for i in range(inner):
             owner = back(outer_me, k, outer) * inner + back(inner_me, i, inner)
-            for m in range(per_req):
-                block = req_ref[m, owner]
-                raw = tgt_in[k][4 * i : 4 * i + 4, pl.ds(pl.multiple_of(block * BLK, BLK), BLK)]
-                high, mid, _ = split3(raw)
-                tgt_rows[owner * per_req + m] = jnp.concatenate(
-                    [jnp.where(last, 1.0, high), jnp.where(last, 0.0, mid)], 0
-                )
-                high, mid, low = split3(jnp.where(last, raw, raw * SCALE))
-                high1 = jnp.where(last, 1.0, high)
-                wide = jnp.concatenate([high1, mid, low, high1, jnp.where(last, high, mid), high1, pad], 0)
-                right[owner * per_req + m] = wide.T.astype(jnp.bfloat16)
-
-    count = pc_ref[0]
-
-    def pair_ids(pair):
-        inside = jnp.minimum(pair, ps_ref.shape[0] - 1)
-        return jnp.where(pair < count, ps_ref[inside], n_src), pq_ref[inside]
-
-    def weigh(pair, buf, g):
-        s, q = pair_ids(pair)
-        kern = jnp.exp2(jnp.dot(right[q], left[s], preferred_element_type=jnp.float32))
+            owners.append(owner)
+            prepare_tgt(owner, slice(4 * i, 4 * i + 4), req_ref, tgt_in[k - first], right, tgt_rows)
+
+    def pair_ids(entry):
+        pair = chosen[jnp.clip(entry, 0, jnp.maximum(total - 1, 0))]
+        return jnp.where(entry < total, ps_ref[pair], n_src), pq_ref[pair]
+
+    def weigh(entry, buf, g):
+        s, q = pair_ids(entry)
+        q = jnp.where(entry < total, q, owners[0] * per_req)
+        kern = jnp.exp2(dot(right[q], left[s]))
         high = kern.astype(jnp.bfloat16)
         buf[g, 0] = high
         buf[g, 1] = (kern - high.astype(jnp.float32)).astype(jnp.bfloat16)
 
-    def reduce(pair, buf, g):
-        s, q = pair_ids(pair)
+    def reduce(entry, buf, g):
+        s, q = pair_ids(entry)
+        q = jnp.where(entry < total, q, owners[0] * per_req)
         high, low = buf[g, 0], buf[g, 1]
         y = tgt_rows[q].astype(jnp.bfloat16)
         x = src_rows[s].astype(jnp.bfloat16)
-        dot = functools.partial(jnp.dot, preferred_element_type=jnp.float32)
-        dot_t = functools.partial(
-            lax.dot_general, dimension_numbers=(((1,), (1,)), ((), ())), preferred_element_type=jnp.float32
-        )
         return s, q, dot(y, high) + dot(y, low), dot_t(x, high) + dot_t(x, low)
 
     bufs = len(kern_bufs)
@@ -159,28 +208,36 @@
         weigh(g, kern_bufs[0], g)
 
     def body(turn, carry):
-        first = turn * bufs * GROUP
+        start = turn * bufs * GROUP
         for u in range(bufs):
             parts = []
             for g in range(GROUP):
-                weigh(first + (u + 1) * GROUP + g, kern_bufs[(u + 1) % bufs], g)
-                parts.append(reduce(first + u * GROUP + g, kern_bufs[u], g))
+                weigh(start + (u + 1) * GROUP + g, kern_bufs[(u + 1) % bufs], g)
+                parts.append(reduce(start + u * GROUP + g, kern_bufs[u], g))
             for s, q, src_part, tgt_part in parts:
                 src_acc[s] += src_part
                 tgt_acc[q] += tgt_part
         return carry
 
-    lax.fori_loop(0, (count + GROUP * bufs - 1) // (GROUP * bufs), body, 0)
-
-    for k in range(n_tgt):
-        base = step(tgt_me, k, n_tgt) * per_dev
-        for b in range(per_dev):
-            total = src_acc[base + b]
-            src_out[k][:, b * BLK : (b + 1) * BLK] = total[0:4] + total[4:8]
-    for r in range(n_clus):
+    lax.fori_loop(0, lax.div(total + GROUP * bufs - 1, GROUP * bufs), body, 0)
+
+    for place, owner in enumerate(owners):
+        row = owner if ends else place
         for m in range(per_req):
-            total = tgt_acc[r * per_req + m]
-            tgt_out[r, :, m * BLK : (m + 1) * BLK] = total[0:4] + total[4:8]
+            part = tgt_acc[owner * per_req + m]
+            tgt_out[row, :, m * BLK : (m + 1) * BLK] = part[0:4] + part[4:8]
+    if ends:
+        for (begin, end), part in zip(stages(outer), done):
+            for k in range(begin, end):
+                for i in range(inner):
+                    owner = back(outer_me, k, outer) * inner + back(inner_me, i, inner)
+                    tgt_out[owner] = part[(k - begin) * inner + i]
+        per_dev = n_src // n_tgt
+        for k in range(n_tgt):
+            base = step(tgt_me, k, n_tgt) * per_dev
+            for b in range(per_dev):
+                part = src_acc[base + b]
+                src_out[k][:, b * BLK : (b + 1) * BLK] = part[0:4] + part[4:8]
 
 
 def finish_side(pos_ref, weight_ref, pot_ref, count_ref, sums, grad_pos_ref, grad_weight_ref):
@@ -278,25 +335,51 @@
     near = jnp.concatenate([tgt_pack] + [moved_inner(tgt_pack, "clus", k) for k in range(1, inner)], 0)
     tgt_in = [near] + [moved_outer(near, "clus", k) for k in range(1, outer)]
 
-    *src_out, tgt_out = pl.pallas_call(
-        functools.partial(main_kernel, n_tgt, n_clus),
-        name="pairs",
-        out_shape=[jax.ShapeDtypeStruct((4, ns), f32)] * n_tgt
-        + [jax.ShapeDtypeStruct((n_clus, 4, per_req * BLK), f32)],
-        in_specs=[SMEM] * 5 + [VMEM] * (n_tgt + outer),
-        out_specs=[VMEM] * (n_tgt + 1),
-        scratch_shapes=[
-            pltpu.VMEM((n_src + 1, 32, BLK), jnp.bfloat16),
-            pltpu.VMEM((slots, BLK, 32), jnp.bfloat16),
-            pltpu.VMEM((n_src + 1, 8, BLK), f32),
-            pltpu.VMEM((slots, 8, BLK), f32),
-            pltpu.VMEM((n_src + 1, 8, BLK), f32),
-            pltpu.VMEM((slots, 8, BLK), f32),
-            pltpu.VMEM((GROUP, 2, BLK, BLK), jnp.bfloat16),
-            pltpu.VMEM((GROUP, 2, BLK, BLK), jnp.bfloat16),
-        ],
-        compiler_params=small,
-    )(me, asked, pair_src, pair_slot, pair_count, *src_in, *tgt_in)
+    block_rows = jax.ShapeDtypeStruct((n_src + 1, 8, BLK), f32)
+    left_side = jax.ShapeDtypeStruct((n_src + 1, 32, BLK), jnp.bfloat16)
+    scratch = [
+        pltpu.VMEM((slots, BLK, 32), jnp.bfloat16),
+        pltpu.VMEM((slots, 8, BLK), f32),
+        pltpu.VMEM((slots, 8, BLK), f32),
+        pltpu.SMEM((pair_src.shape[0] + 1,), jnp.int32),
+    ] + [pltpu.VMEM((GROUP, 2, BLK, BLK), jnp.bfloat16)] * BUFS
+    lists = (me, asked, pair_src, pair_slot, pair_count)
+    state, done = (), []
+    for first, stop in stages(outer):
+        begins, ends = first == 0, stop == outer
+        args = (src_in if begins else list(state)) + tgt_in[first:stop] + (done if ends else [])
+        outs = []
+        if begins and not ends:
+            outs += [left_side, block_rows]
+        if ends:
+            outs += [jax.ShapeDtypeStruct((4, ns), f32)] * n_tgt
+            outs += [jax.ShapeDtypeStruct((n_clus, 4, per_req * BLK), f32)]
+        else:
+            outs += [block_rows, jax.ShapeDtypeStruct(((stop - first) * inner, 4, per_req * BLK), f32)]
+        extra = [pltpu.VMEM(block_rows.shape, f32)] if ends else []
+        if begins and ends:
+            extra += [pltpu.VMEM(left_side.shape, jnp.bfloat16), pltpu.VMEM(block_rows.shape, f32)]
+        share = pair_src.shape[0] * (stop - first) // outer
+        res = pl.pallas_call(
+            functools.partial(pairs_kernel, n_tgt, n_clus, first, stop),
+            name=f"pairs_{first}_{stop}",
+            out_shape=outs,
+            in_specs=[SMEM] * 5 + [VMEM] * len(args),
+            out_specs=[VMEM] * len(outs),
+            scratch_shapes=extra + scratch,
+            compiler_params=small,
+            cost_estimate=pl.CostEstimate(
+                flops=share * 10 * BLK**3, bytes_accessed=2**20, transcendentals=share * BLK**2
+            ),
+        )(*lists, *args)
+        if ends:
+            *src_out, tgt_out = res
+        else:
+            if begins:
+                state = res[:3]
+            else:
+                state = (state[0], state[1], res[0])
+            done = done + [res[-1]]
 
     src_parts = [src_out[0]] + [moved(src_out[k], "tgt", k) for k in range(1, n_tgt)]
     tgt_parts = lax.all_to_all(tgt_out, "clus", split_axis=0, concat_axis=0, tiled=True)

time: 36.1 us -> 37.1 us (1.028)
  Pallas kernels: 10.3 us -> 12.4 us
  waiting for transfers between devices: 8.28 us -> 7.04 us
    ppermute x3, waiting for transfers between devices: 4.17 us -> 1.58 us  [moved_outer(): return lax.ppermute(x, axis, pairs)]
    pallas_call x1 -> x3, Pallas kernels: 6.21 us -> 8.29 us  [shards(): pl.pallas_call(functools.partial(pairs_kernel, n_tgt, n_clus, first, stop...]
    ppermute x1, waiting for transfers between devices: 0.33 us -> 1.68 us  [moved_inner(): return lax.ppermute(x, axis, pairs)]
    ppermute x1, starting transfers between devices: 2.94 us -> 1.68 us  [moved_inner(): return lax.ppermute(x, axis, pairs)]
    ppermute x6, starting transfers between devices: 3.72 us -> 4.97 us  [moved(): return lax.ppermute(x, axis, [(i, step(i, k, n)) for i in range(n)])]
    all_to_all x1, starting transfers between devices: 4.02 us -> 4.58 us  [shards(): lax.all_to_all(tgt_out, 'clus', split_axis=0, concat_axis=0, tiled=True)]
  transfers between devices with their start and end apart: 11 -> 11, of which waited for: 7 -> 5; matrix products, arithmetic and copies ran while one was open for 0% -> 0% of each run, Pallas kernels for 3% -> 15%
where the time goes in v3:
time: 37.1 us; the launch traced here: 36.8 us
  starting transfers between devices  15.7 us (42%)
  Pallas kernels  12.4 us (33%)
  waiting for transfers between devices  7.04 us (19%)
  between operations  1.45 us (4%)
    pallas_call x3, Pallas kernels, shards(): pl.pallas_call(functools.partial(pairs_kernel, n_tgt, n_clus, first, stop...  8.29 us
    ppermute x6, starting transfers between devices, moved(): return lax.ppermute(x, axis, [(i, step(i, k, n)) for i in range(n)])  4.97 us
    all_to_all x1, starting transfers between devices, shards(): lax.all_to_all(tgt_out, 'clus', split_axis=0, concat_axis=0, tiled=True)  4.58 us
    ppermute x3, starting transfers between devices, moved_outer(): return lax.ppermute(x, axis, pairs)  4.45 us
    ppermute x6, waiting for transfers between devices, moved(): return lax.ppermute(x, axis, [(i, step(i, k, n)) for i in range(n)])  3.09 us
    ppermute x1, waiting for transfers between devices, moved_inner(): return lax.ppermute(x, axis, pairs)  1.68 us
    ppermute x1, starting transfers between devices, moved_inner(): return lax.ppermute(x, axis, pairs)  1.68 us
    ppermute x3, waiting for transfers between devices, moved_outer(): return lax.ppermute(x, axis, pairs)  1.58 us
  transfers between devices with their start and end apart: 11, of which 5 were waited for; matrix products, arithmetic and copies ran while one was open for 0% of the time, Pallas kernels for 15%

profile of v3, /device:TPU:0, one launch (start us, length us, event | category | flops | bytes accessed | tf_op | source)
XLA Modules:
  0.0 36.8 jit_solution(13611298035863772119)
XLA Ops:
  0.6 1.5 %pack.1 = (f32[4,2048]{1,0:T(4,128)}, f32[4,2176]{1,0:T(4,128)}) custom-call(s32[2,8]{1,0:T(2,128)} %bitcast.18, s32[8]{0:T(128)} %count_ref.2, s32[8]{0:T(128)} %count_ref.3, f32[3,2048]{1,0:T(4,128)} %pos_ref.2, f32[1,2048]{1,0:T(1,128)} %bitcast.10, f32[1,2048]{1,0:T(1,128)} %bitcast.12, f32[3,2048]{1,0:T(4,128)} %pos_ref.3, f32[1,2048]{1,0:T(1,128)} %bitcast.14, ...), custom_call_target="tpu_custom_call" | custom-call | tf_op jit(solution)/shard_map/pack/pallas_call | solution.py:325
  2.2 0.0 copy-start.12
  2.2 0.5 %collective-permute-start = (f32[4,2048]{1,0:T(4,128)}, f32[4,2048]{1,0:T(4,128)S(1)}, u32[]{:S(2)}, u32[]{:S(2)}) collective-permute-start(f32[4,2048]{1,0:T(4,128)} %get-tuple-element.22.refs_0_), channel_id=1, source_target_pairs={{0,1},{1,0},{2,3},{3,2},{4,5},{5,4},{6,7},{7,6},{8,9},{9,8},{10,11... | collective-permute-start | bytes 98312 | tf_op jit(solution)/shard_map/ppermute | solution.py:42
  2.6 2.6 %collective-permute-start.1 = (f32[4,2048]{1,0:T(4,128)}, f32[4,2048]{1,0:T(4,128)S(1)}, u32[]{:S(2)}, u32[]{:S(2)}) collective-permute-start(f32[4,2048]{1,0:T(4,128)} %get-tuple-element.22.refs_0_), channel_id=1, source_target_pairs={{0,2},{1,3},{2,0},{3,1},{4,6},{5,7},{6,4},{7,5},{8,10},{9,11},{10,... | collective-permute-start | bytes 98312 | tf_op jit(solution)/shard_map/ppermute | solution.py:42
  5.2 0.1 collective-permute-start.2
  5.3 1.7 %collective-permute-start.3 = (f32[4,2176]{1,0:T(4,128)}, f32[4,2176]{1,0:T(4,128)S(1)}, u32[]{:S(2)}, u32[]{:S(2)}) collective-permute-start(f32[4,2176]{1,0:T(4,128)} %get-tuple-element.23), channel_id=1, source_target_pairs={{0,4},{4,0},{8,12},{12,8},{16,20},{20,16},{24,28},{28,24},{1,5},{5... | collective-permute-start | bytes 104456 | tf_op jit(solution)/shard_map/ppermute | solution.py:54
  7.0 0.1 pad_add_fusion.me_ref
  7.7 0.0 copy-start.8
  7.7 0.0 copy-start.9
  7.7 0.0 copy-start.10
  7.7 0.0 copy-start.11
  7.8 1.7 %collective-permute-done.3 = f32[4,2176]{1,0:T(4,128)S(1)} collective-permute-done((f32[4,2176]{1,0:T(4,128)}, f32[4,2176]{1,0:T(4,128)S(1)}, u32[]{:S(2)}, u32[]{:S(2)}) %collective-permute-start.3) | collective-permute-done | bytes 34848 | tf_op jit(solution)/shard_map/ppermute | solution.py:54
  9.4 0.0 copy-done.12
  9.5 1.8 %collective-permute-start.4 = (f32[8,2176]{1,0:T(8,128)S(1)}, f32[8,2176]{1,0:T(8,128)S(1)}, u32[]{:S(2)}, u32[]{:S(2)}) collective-permute-start(f32[8,2176]{1,0:T(8,128)S(1)} %pad_maximum_fusion.refs_4_), channel_id=1, source_target_pairs={{0,8},{4,12},{8,0},{12,4},{16,24},{20,28},{24,16},{28,20},{1,9},{5... | collective-permute-start | bytes 208904 | tf_op jit(solution)/shard_map/ppermute | solution.py:48
  11.3 2.6 %collective-permute-start.5 = (f32[8,2176]{1,0:T(8,128)S(1)}, f32[8,2176]{1,0:T(8,128)S(1)}, u32[]{:S(2)}, u32[]{:S(2)}) collective-permute-start(f32[8,2176]{1,0:T(8,128)S(1)} %pad_maximum_fusion.refs_4_), channel_id=1, source_target_pairs={{0,16},{4,20},{8,24},{12,28},{16,0},{20,4},{24,8},{28,12},{1,17},{... | collective-permute-start | bytes 208904 | tf_op jit(solution)/shard_map/ppermute | solution.py:48
  13.9 0.0 collective-permute-done.refs_1_
  13.9 0.0 collective-permute-start.6
  13.9 0.0 collective-permute-done.1.refs_2_
  13.9 0.0 collective-permute-done.2.refs_3_
  13.9 0.0 copy-done.8
  13.9 0.0 copy-done.9
  13.9 0.0 copy-done.10
  14.0 0.0 copy-done.11
  14.0 2.3 %pairs_0_1.1 = (bf16[33,32,256]{2,1,0:T(8,128)(2,1)S(1)}, f32[33,8,256]{2,1,0:T(8,128)S(1)}, f32[33,8,256]{2,1,0:T(8,128)S(1)}, f32[2,4,512]{2,1,0:T(4,128)S(1)}) custom-call(s32[3]{0:T(128)S(1)} %pad_add_fusion.me_ref, s32[2,8]{1,0:T(2,128)S(1)} %bitcast.19, s32[32]{0:T(128)S(1)} %copy-done.10, s32[32]{0:T(128)S(1)} %copy-done.11, s32[1]{0:T(128)S(6)} %copy.16.pc_ref, ...), custom_call_target="tpu_custom_call" | custom-call | flops 1342177280 | bytes 1048576 | tf_op jit(solution)/shard_map/pairs_0_1/pallas_call | solution.py:363
  16.3 0.0 collective-permute-done.4.refs_3_.refs_5_
  16.3 2.1 %pairs_1_2.1 = (f32[33,8,256]{2,1,0:T(8,128)S(1)}, f32[2,4,512]{2,1,0:T(4,128)S(1)}) custom-call(s32[3]{0:T(128)S(1)} %pad_add_fusion.me_ref, s32[2,8]{1,0:T(2,128)S(1)} %bitcast.20, s32[32]{0:T(128)S(1)} %copy-done.10, s32[32]{0:T(128)S(1)} %copy-done.11, s32[1]{0:T(128)S(6)} %copy.16.pc_ref, bf16[33,32,256]{2,1,0:T(8,128)(2,1)S(1)} %get-tuple-element.24.refs_0_, ...), custom_call_target="tpu_custom_call" | custom-call | flops 1342177280 | bytes 1048576 | tf_op jit(solution)/shard_map/pairs_1_2/pallas_call | solution.py:363
  18.4 0.0 collective-permute-done.5.refs_3_.refs_6_
  18.4 1.6 %collective-permute-done.6.refs_4_.refs_7_ = f32[8,2176]{1,0:T(8,128)S(1)} collective-permute-done((f32[8,2176]{1,0:T(8,128)S(1)}, f32[8,2176]{1,0:T(8,128)S(1)}, u32[]{:S(2)}, u32[]{:S(2)}) %collective-permute-start.6) | collective-permute-done | bytes 69664 | tf_op jit(solution)/shard_map/ppermute | solution.py:48
  20.0 3.9 %pairs_2_4.1 = (f32[4,2048]{1,0:T(4,128)S(1)}, f32[4,2048]{1,0:T(4,128)S(1)}, f32[4,2048]{1,0:T(4,128)S(1)}, f32[4,2048]{1,0:T(4,128)S(1)}, f32[8,4,512]{2,1,0:T(4,128)}) custom-call(s32[3]{0:T(128)S(1)} %pad_add_fusion.me_ref, s32[2,8]{1,0:T(2,128)S(1)} %bitcast.21, s32[32]{0:T(128)S(1)} %copy-done.10, s32[32]{0:T(128)S(1)} %copy-done.11, ...), custom_call_target="tpu_custom_call" | custom-call | flops 2684354560 | bytes 1048576 | tf_op jit(solution)/shard_map/pairs_2_4/pallas_call | solution.py:363
  23.9 0.0 copy-start
  23.9 0.0 copy-start.2
  23.9 0.0 copy-start.3
  23.9 4.6 %all-to-all-start = ((f32[8,4,512]{2,1,0:T(4,128)}), f32[8,4,512]{2,1,0:T(4,128)S(1)}, u32[]{:S(2)}, u32[]{:S(2)}) async-start(f32[8,4,512]{2,1,0:T(4,128)} %get-tuple-element.36), calls=%async_computation | async-start | bytes 131072 | tf_op jit(solution)/shard_map/all_to_all | solution.py:385
  28.5 0.0 collective-permute-start.7
  28.5 1.6 %collective-permute-start.8 = (f32[4,2048]{1,0:T(4,128)S(1)}, f32[4,2048]{1,0:T(4,128)S(1)}, u32[]{:S(2)}, u32[]{:S(2)}) collective-permute-start(f32[4,2048]{1,0:T(4,128)S(1)} %get-tuple-element.32), channel_id=1, source_target_pairs={{0,2},{1,3},{2,0},{3,1},{4,6},{5,7},{6,4},{7,5},{8,10},{9,11},{10,... | collective-permute-start | bytes 98312 | tf_op jit(solution)/shard_map/ppermute | solution.py:42
  30.1 0.0 copy-start.6
  30.1 0.3 collective-permute-start.9
  30.3 0.0 collective-permute-done.7.refs_1_
  30.3 2.1 %collective-permute-done.8.refs_2_ = f32[4,2048]{1,0:T(4,128)S(1)} collective-permute-done((f32[4,2048]{1,0:T(4,128)S(1)}, f32[4,2048]{1,0:T(4,128)S(1)}, u32[]{:S(2)}, u32[]{:S(2)}) %collective-permute-start.8) | collective-permute-done | bytes 32800 | tf_op jit(solution)/shard_map/ppermute | solution.py:42
  32.4 1.0 %collective-permute-done.9.refs_3_ = f32[4,2048]{1,0:T(4,128)S(1)} collective-permute-done((f32[4,2048]{1,0:T(4,128)S(1)}, f32[4,2048]{1,0:T(4,128)S(1)}, u32[]{:S(2)}, u32[]{:S(2)}) %collective-permute-start.9) | collective-permute-done | bytes 32800 | tf_op jit(solution)/shard_map/ppermute | solution.py:42
  33.4 0.0 copy-done
  33.4 0.0 copy-done.2
  33.4 0.0 copy-done.3
  33.4 0.0 copy-done.6
  33.4 0.0 copy-start.1
  33.4 0.0 copy-start.4
  33.4 0.0 copy-start.5
  33.5 1.2 %finish_src.1 = (f32[3,2048]{1,0:T(4,128)}, f32[1,2048]{1,0:T(1,128)}, f32[16,1,256]{2,1,0:T(1,128)S(1)}) custom-call(s32[3]{0:T(128)S(1)} %pad_add_fusion.me_ref, s32[8]{0:T(128)S(1)} %copy-done.6, f32[3,2048]{1,0:T(4,128)S(1)} %copy-done, f32[1,2048]{1,0:T(1,128)S(1)} %bitcast.11, f32[1,2048]{1,0:T(1,128)S(1)} %bitcast.13, ...), custom_call_target="tpu_custom_call" | custom-call | tf_op jit(solution)/shard_map/finish_src/pallas_call | solution.py:387
  34.7 0.0 copy-start.7
  34.7 0.7 %all-to-all-done.parts_ref = f32[8,4,512]{2,1,0:T(4,128)S(1)} async-done(((f32[8,4,512]{2,1,0:T(4,128)}), f32[8,4,512]{2,1,0:T(4,128)S(1)}, u32[]{:S(2)}, u32[]{:S(2)}) %all-to-all-start) | async-done | bytes 65568 | tf_op jit(solution)/shard_map/all_to_all | solution.py:385
  35.4 0.0 copy-done.1
  35.4 0.0 copy-done.4
  35.4 0.0 copy-done.5
  35.4 0.0 copy-done.7
  35.4 1.4 %finish_tgt.1 = (f32[3,2048]{1,0:T(4,128)}, f32[1,2048]{1,0:T(1,128)}) custom-call(s32[8]{0:T(128)S(1)} %copy-done.7, f32[3,2048]{1,0:T(4,128)S(1)} %copy-done.1, f32[1,2048]{1,0:T(1,128)S(1)} %bitcast.15, f32[1,2048]{1,0:T(1,128)S(1)} %bitcast.17, f32[8,4,512]{2,1,0:T(4,128)S(1)} %all-to-all-done.parts_ref, f32[16,1,256]{2,1,0:T(1,128)S(1)} %get-tuple-element.37.ids_ref), custom_call_target="tpu_custom_call" | custom-call | tf_op jit(solution)/shard_map/finish_tgt/pallas_call | solution.py:399
  (1 shorter events, 0.0 us)
Async XLA Ops:
  2.2 7.3 %copy-start.12 = (f32[4,2176]{1,0:T(4,128)S(1)}, f32[4,2176]{1,0:T(4,128)}, u32[]{:S(2)}) copy-start(f32[4,2176]{1,0:T(4,128)} %get-tuple-element.23) | copy-start | bytes 104452
  2.2 11.7 %collective-permute-start = (f32[4,2048]{1,0:T(4,128)}, f32[4,2048]{1,0:T(4,128)S(1)}, u32[]{:S(2)}, u32[]{:S(2)}) collective-permute-start(f32[4,2048]{1,0:T(4,128)} %get-tuple-element.22.refs_0_), channel_id=1, source_target_pairs={{0,1},{1,0},{2,3},{3,2},{4,5},{5,4},{6,7},{7,6},{8,9},{9,8},{10,11... | collective-permute-start | bytes 98312 | tf_op jit(solution)/shard_map/ppermute | solution.py:42
  2.6 11.3 %collective-permute-start.1 = (f32[4,2048]{1,0:T(4,128)}, f32[4,2048]{1,0:T(4,128)S(1)}, u32[]{:S(2)}, u32[]{:S(2)}) collective-permute-start(f32[4,2048]{1,0:T(4,128)} %get-tuple-element.22.refs_0_), channel_id=1, source_target_pairs={{0,2},{1,3},{2,0},{3,1},{4,6},{5,7},{6,4},{7,5},{8,10},{9,11},{10,... | collective-permute-start | bytes 98312 | tf_op jit(solution)/shard_map/ppermute | solution.py:42
  5.2 8.7 %collective-permute-start.2 = (f32[4,2048]{1,0:T(4,128)}, f32[4,2048]{1,0:T(4,128)S(1)}, u32[]{:S(2)}, u32[]{:S(2)}) collective-permute-start(f32[4,2048]{1,0:T(4,128)} %get-tuple-element.22.refs_0_), channel_id=1, source_target_pairs={{0,3},{1,2},{2,1},{3,0},{4,7},{5,6},{6,5},{7,4},{8,11},{9,10},{10,... | collective-permute-start | bytes 98312 | tf_op jit(solution)/shard_map/ppermute | solution.py:42
  5.3 4.1 %collective-permute-start.3 = (f32[4,2176]{1,0:T(4,128)}, f32[4,2176]{1,0:T(4,128)S(1)}, u32[]{:S(2)}, u32[]{:S(2)}) collective-permute-start(f32[4,2176]{1,0:T(4,128)} %get-tuple-element.23), channel_id=1, source_target_pairs={{0,4},{4,0},{8,12},{12,8},{16,20},{20,16},{24,28},{28,24},{1,5},{5... | collective-permute-start | bytes 104456 | tf_op jit(solution)/shard_map/ppermute | solution.py:54
  7.7 6.2 %copy-start.8 = (s32[8,2]{0,1:T(2,128)S(1)}, s32[8,2]{0,1:T(2,128)}, u32[]{:S(2)}) copy-start(s32[8,2]{0,1:T(2,128)} %param.20) | copy-start | bytes 196
  7.7 6.2 %copy-start.9 = (f32[4,2048]{1,0:T(4,128)S(1)}, f32[4,2048]{1,0:T(4,128)}, u32[]{:S(2)}) copy-start(f32[4,2048]{1,0:T(4,128)} %get-tuple-element.22.refs_0_) | copy-start | bytes 98308
  7.7 6.2 %copy-start.10 = (s32[32]{0:T(128)S(1)}, s32[32]{0:T(128)}, u32[]{:S(2)}) copy-start(s32[32]{0:T(128)} %ps_ref.5) | copy-start | bytes 388
  7.7 6.2 %copy-start.11 = (s32[32]{0:T(128)S(1)}, s32[32]{0:T(128)}, u32[]{:S(2)}) copy-start(s32[32]{0:T(128)} %pq_ref.5) | copy-start | bytes 388
  9.5 6.8 %collective-permute-start.4 = (f32[8,2176]{1,0:T(8,128)S(1)}, f32[8,2176]{1,0:T(8,128)S(1)}, u32[]{:S(2)}, u32[]{:S(2)}) collective-permute-start(f32[8,2176]{1,0:T(8,128)S(1)} %pad_maximum_fusion.refs_4_), channel_id=1, source_target_pairs={{0,8},{4,12},{8,0},{12,4},{16,24},{20,28},{24,16},{28,20},{1,9},{5... | collective-permute-start | bytes 208904 | tf_op jit(solution)/shard_map/ppermute | solution.py:48
  11.3 7.1 %collective-permute-start.5 = (f32[8,2176]{1,0:T(8,128)S(1)}, f32[8,2176]{1,0:T(8,128)S(1)}, u32[]{:S(2)}, u32[]{:S(2)}) collective-permute-start(f32[8,2176]{1,0:T(8,128)S(1)} %pad_maximum_fusion.refs_4_), channel_id=1, source_target_pairs={{0,16},{4,20},{8,24},{12,28},{16,0},{20,4},{24,8},{28,12},{1,17},{... | collective-permute-start | bytes 208904 | tf_op jit(solution)/shard_map/ppermute | solution.py:48
  13.9 6.1 %collective-permute-start.6 = (f32[8,2176]{1,0:T(8,128)S(1)}, f32[8,2176]{1,0:T(8,128)S(1)}, u32[]{:S(2)}, u32[]{:S(2)}) collective-permute-start(f32[8,2176]{1,0:T(8,128)S(1)} %pad_maximum_fusion.refs_4_), channel_id=1, source_target_pairs={{0,24},{4,28},{8,16},{12,20},{16,8},{20,12},{24,0},{28,4},{1,25},{... | collective-permute-start | bytes 208904 | tf_op jit(solution)/shard_map/ppermute | solution.py:48
  23.9 9.5 %copy-start = (f32[3,2048]{1,0:T(4,128)S(1)}, f32[3,2048]{1,0:T(4,128)}, u32[]{:S(2)}) copy-start(f32[3,2048]{1,0:T(4,128)} %pos_ref.2) | copy-start | bytes 73732
  23.9 9.5 %copy-start.2 = (f32[2048]{0:T(1024)S(1)}, f32[2048]{0:T(1024)}, u32[]{:S(2)}) copy-start(f32[2048]{0:T(1024)} %param.13) | copy-start | bytes 24580
  23.9 9.5 %copy-start.3 = (f32[2048]{0:T(1024)S(1)}, f32[2048]{0:T(1024)}, u32[]{:S(2)}) copy-start(f32[2048]{0:T(1024)} %param.14) | copy-start | bytes 24580
  23.9 11.5 %all-to-all-start = ((f32[8,4,512]{2,1,0:T(4,128)}), f32[8,4,512]{2,1,0:T(4,128)S(1)}, u32[]{:S(2)}, u32[]{:S(2)}) async-start(f32[8,4,512]{2,1,0:T(4,128)} %get-tuple-element.36), calls=%async_computation | async-start | bytes 131072 | tf_op jit(solution)/shard_map/all_to_all | solution.py:385
  28.5 1.9 %collective-permute-start.7 = (f32[4,2048]{1,0:T(4,128)S(1)}, f32[4,2048]{1,0:T(4,128)S(1)}, u32[]{:S(2)}, u32[]{:S(2)}) collective-permute-start(f32[4,2048]{1,0:T(4,128)S(1)} %get-tuple-element.31), channel_id=1, source_target_pairs={{0,1},{1,0},{2,3},{3,2},{4,5},{5,4},{6,7},{7,6},{8,9},{9,8},{10,11... | collective-permute-start | bytes 98312 | tf_op jit(solution)/shard_map/ppermute | solution.py:42
  28.5 4.0 %collective-permute-start.8 = (f32[4,2048]{1,0:T(4,128)S(1)}, f32[4,2048]{1,0:T(4,128)S(1)}, u32[]{:S(2)}, u32[]{:S(2)}) collective-permute-start(f32[4,2048]{1,0:T(4,128)S(1)} %get-tuple-element.32), channel_id=1, source_target_pairs={{0,2},{1,3},{2,0},{3,1},{4,6},{5,7},{6,4},{7,5},{8,10},{9,11},{10,... | collective-permute-start | bytes 98312 | tf_op jit(solution)/shard_map/ppermute | solution.py:42
  30.1 3.4 %copy-start.6 = (s32[8]{0:T(128)S(1)}, s32[8]{0:T(128)}, u32[]{:S(2)}) copy-start(s32[8]{0:T(128)} %count_ref.2) | copy-start | bytes 100
  30.1 3.4 %collective-permute-start.9 = (f32[4,2048]{1,0:T(4,128)S(1)}, f32[4,2048]{1,0:T(4,128)S(1)}, u32[]{:S(2)}, u32[]{:S(2)}) collective-permute-start(f32[4,2048]{1,0:T(4,128)S(1)} %get-tuple-element.33), channel_id=1, source_target_pairs={{0,3},{1,2},{2,1},{3,0},{4,7},{5,6},{6,5},{7,4},{8,11},{9,10},{10,... | collective-permute-start | bytes 98312 | tf_op jit(solution)/shard_map/ppermute | solution.py:42
  33.4 1.9 %copy-start.1 = (f32[3,2048]{1,0:T(4,128)S(1)}, f32[3,2048]{1,0:T(4,128)}, u32[]{:S(2)}) copy-start(f32[3,2048]{1,0:T(4,128)} %pos_ref.3) | copy-start | bytes 73732
  33.4 1.9 %copy-start.4 = (f32[2048]{0:T(1024)S(1)}, f32[2048]{0:T(1024)}, u32[]{:S(2)}) copy-start(f32[2048]{0:T(1024)} %param.17) | copy-start | bytes 24580
  33.4 1.9 %copy-start.5 = (f32[2048]{0:T(1024)S(1)}, f32[2048]{0:T(1024)}, u32[]{:S(2)}) copy-start(f32[2048]{0:T(1024)} %param.18) | copy-start | bytes 24580
  34.7 0.7 %copy-start.7 = (s32[8]{0:T(128)S(1)}, s32[8]{0:T(128)}, u32[]{:S(2)}) copy-start(s32[8]{0:T(128)} %count_ref.3) | copy-start | bytes 100

commit v4 on v3

v4 whole, which is shorter than its diff:
```python
import functools
import math

import jax
import jax.numpy as jnp
from jax import lax
from jax.experimental import pallas as pl
from jax.experimental.pallas import tpu as pltpu
from jax.sharding import PartitionSpec as P

BLK = 256
LANES = 128
GROUP = 2
BUFS = 4

entropic = 0.05
LOG2E = math.log2(math.e)
SCALE = LOG2E / entropic
DEAD = -4096.0
PACK_VMEM = 60 * 2**20
MAIN_VMEM = 24 * 2**20

VMEM = pl.BlockSpec(memory_space=pltpu.VMEM)
SMEM = pl.BlockSpec(memory_space=pltpu.SMEM)
ANY = pl.BlockSpec(memory_space=pl.ANY)


def divide(x, n):
    shift = n.bit_length() - 1
    return lax.shift_right_logical(x, jnp.int32(shift)) if n == 1 << shift else lax.div(x, jnp.int32(n))


def step(i, k, n):
    return i ^ k if n & (n - 1) == 0 else (i + k) % n


def back(i, k, n):
    return i ^ k if n & (n - 1) == 0 else (i + n - k) % n


def flip(k, n):
    return k if n & (n - 1) == 0 else (n - k) % n


def split_axis(n):
    inner = 2 if n % 2 == 0 else 1
    return n // inner, inner


def moved(x, axis, k):
    n = lax.axis_size(axis)
    return lax.ppermute(x, axis, [(i, step(i, k, n)) for i in range(n)])


def moved_outer(x, axis, k):
    outer, inner = split_axis(lax.axis_size(axis))
    pairs = [(o * inner + i, step(o, k, outer) * inner + i) for o in range(outer) for i in range(inner)]
    return lax.ppermute(x, axis, pairs)


def moved_inner(x, axis, k):
    outer, inner = split_axis(lax.axis_size(axis))
    pairs = [(o * inner + i, o * inner + step(i, k, inner)) for o in range(outer) for i in range(inner)]
    return lax.ppermute(x, axis, pairs)


def live_row(count_ref, block):
    lane = lax.broadcasted_iota(jnp.int32, (1, BLK), 1)
    return lane < count_ref[block]


def pack_side(pos_ref, weight_ref, pot_ref, count_ref, out_ref):
    for b in range(count_ref.shape[0]):
        cols = slice(b * BLK, (b + 1) * BLK)
        pos = pos_ref[:, cols]
        norm = jnp.sum(pos * pos, axis=0, keepdims=True)
        expo = (pot_ref[:, cols] - 0.5 * norm) * SCALE + jnp.log(weight_ref[:, cols]) * LOG2E
        out_ref[0:3, cols] = pos
        out_ref[3:4, cols] = jnp.where(live_row(count_ref, b), expo, DEAD)


def pack_kernel(
    req_ref, ps_ref, pq_ref, sc_ref, tc_ref, sp_ref, sw_ref, so_ref, tp_ref, tw_ref, to_ref, src_ref, tgt_ref, plan_ref
):
    pairs = ps_ref.shape[0]
    for pair in range(pairs):
        plan_ref[req_ref.size + pair] = ps_ref[pair]
        plan_ref[req_ref.size + pairs + pair] = pq_ref[pair]
    pack_side(sp_ref, sw_ref, so_ref, sc_ref, src_ref)
    pack_side(tp_ref, tw_ref, to_ref, tc_ref, tgt_ref)
    per, rows = req_ref.shape
    own = tp_ref.shape[1]
    width = tgt_ref.shape[1] - own
    lane = lax.broadcasted_iota(jnp.int32, (4, width), 1)
    ids = jnp.zeros((4, width), jnp.float32)
    for r in range(rows):
        for m in range(per):
            block = req_ref[m, r]
            plan_ref[r * per + m] = block
            ids = jnp.where(lane == r * per + m, block.astype(jnp.float32), ids)
    tgt_ref[:, own:] = ids


def split3(x):
    high = x.astype(jnp.bfloat16).astype(jnp.float32)
    rest = x - high
    mid = rest.astype(jnp.bfloat16).astype(jnp.float32)
    return high, mid, rest - mid


def stages(outer):
    cuts = [(0, 1), (outer - 1, outer), (1, outer - 1)]
    return [(first, stop) for i, (first, stop) in enumerate(cuts) if first < stop and (i == 0 or first > 0)]


def dot(x, y):
    return jnp.dot(x, y, preferred_element_type=jnp.float32)


def dot_t(x, y):
    return lax.dot_general(x, y, (((1,), (1,)), ((), ())), preferred_element_type=jnp.float32)


def away(i, me, n):
    return i ^ me if n & (n - 1) == 0 else lax.rem(me - i + n, n)


def is_power(n):
    return n & (n - 1) == 0


def local_block(s, me, n, per_dev):
    if is_power(n) and is_power(per_dev):
        return s ^ (me * per_dev)
    dev = divide(s, per_dev)
    return s + (away(dev, me, n) - dev) * per_dev


def local_slot(q, outer_me, inner_me, outer, inner, per_req):
    if is_power(outer) and is_power(inner) and is_power(per_req):
        return q ^ ((outer_me * inner + inner_me) * per_req)
    clus = divide(q, per_req)
    place = divide(clus, inner)
    side = away(clus - place * inner, inner_me, inner)
    return (away(place, outer_me, outer) * inner + side - clus) * per_req + q


def prepare_src(src_in, left, src_rows):
    last = lax.broadcasted_iota(jnp.int32, (4, BLK), 0) == 3
    pad = jnp.zeros((8, BLK), jnp.float32)
    per_dev = src_in[0].shape[1] // BLK
    for k, part in enumerate(src_in):
        for b in range(per_dev):
            high, mid, low = split3(part[:, b * BLK : (b + 1) * BLK])
            high1, mid1 = jnp.where(last, 1.0, high), jnp.where(last, 1.0, mid)
            place = k * per_dev + b
            left[place] = jnp.concatenate([high, high1, high1, mid, mid1, low, pad], 0).astype(jnp.bfloat16)
            src_rows[place] = jnp.concatenate([high1, jnp.where(last, 0.0, mid)], 0)
    dead = lax.broadcasted_iota(jnp.int32, (32, BLK), 0) == 3
    left[len(src_in) * per_dev] = jnp.where(dead, DEAD, 0.0).astype(jnp.bfloat16)
    src_rows[len(src_in) * per_dev] = pad


def prepare_tgt(slot, block, rows, tgt_in, right, tgt_rows):
    last = lax.broadcasted_iota(jnp.int32, (4, BLK), 0) == 3
    pad = jnp.zeros((8, BLK), jnp.float32)
    raw = tgt_in[rows, pl.ds(pl.multiple_of(block * BLK, BLK), BLK)]
    high, mid, _ = split3(raw)
    tgt_rows[slot] = jnp.concatenate([jnp.where(last, 1.0, high), jnp.where(last, 0.0, mid)], 0)
    high, mid, low = split3(jnp.where(last, raw, raw * SCALE))
    high1 = jnp.where(last, 1.0, high)
    wide = jnp.concatenate([high1, mid, low, high1, jnp.where(last, high, mid), high1, pad], 0)
    right[slot] = wide.T.astype(jnp.bfloat16)


def pairs_kernel(n_tgt, n_clus, per_req, turn, *refs):
    outer, inner = split_axis(n_clus)
    first, stop = stages(outer)[turn]
    begins, ends = turn == 0, turn == len(stages(outer)) - 1
    refs = list(refs)
    take = lambda n: [refs.pop(0) for _ in range(n)]
    far_lists = take(2)
    if begins:
        src_in = take(n_tgt)
    else:
        left, src_rows, src_sums = take(3)
    tgt_in = take(stop - first)
    held = [k for cut in stages(outer)[1:turn] for k in range(*cut)] if ends else []
    held_in = take(len(held))
    if begins and not ends:
        left, src_rows = take(2)
    src_out = take(n_tgt if ends else 1)
    tgt_out = take(stop - first)
    for far, near in zip(held_in, take(len(held))):
        near[...] = far[...]
    src_acc = take(1)[0] if ends else src_out[0]
    if begins and ends:
        left, src_rows = take(2)
    right, tgt_rows, tgt_acc, chosen_src, chosen_slot, sems, *refs = refs
    lists, kern_bufs = refs[:2], refs[2:]
    copies = [pltpu.make_async_copy(far, near, sems.at[i]) for i, (far, near) in enumerate(zip(far_lists, lists))]
    for copy in copies:
        copy.start()
    n_src = left.shape[0] - 1
    per_dev = n_src // n_tgt
    if begins:
        prepare_src(src_in, left, src_rows)
        src_acc[...] = jnp.zeros_like(src_acc)
    else:
        src_acc[...] = src_sums[...]
    tgt_acc[...] = jnp.zeros_like(tgt_acc)
    for copy in copies:
        copy.wait()

    me_ref, plan_ref = lists
    slots = n_clus * per_req
    pairs = (plan_ref.shape[0] - slots) // 2
    tgt_me, outer_me, inner_me, count = (me_ref[i] for i in range(4))
    owners = []
    for k in range(first, stop):
        for i in range(inner):
            owner = back(outer_me, k, outer) * inner + back(inner_me, i, inner)
            for m in range(per_req):
                slot = len(owners) * per_req + m
                prepare_tgt(slot, plan_ref[owner * per_req + m], slice(4 * i, 4 * i + 4), tgt_in[k - first], right, tgt_rows)
            owners.append(owner)

    total = jnp.int32(0)
    for pair in range(pairs):
        chosen_src[total] = local_block(plan_ref[slots + pair], tgt_me, n_tgt, per_dev)
        slot = local_slot(plan_ref[slots + pairs + pair], outer_me, inner_me, outer, inner, per_req) - first * inner * per_req
        chosen_slot[total] = slot
        total = total + ((pair < count) & (slot >= 0) & (slot < len(owners) * per_req)).astype(jnp.int32)

    def pair_ids(entry):
        inside = jnp.minimum(entry, pairs - 1)
        live = entry < total
        return jnp.where(live, chosen_src[inside], n_src), jnp.where(live, chosen_slot[inside], 0)

    def weigh(entry, buf, g):
        s, q = pair_ids(entry)
        kern = jnp.exp2(dot(right[q], left[s]))
        high = kern.astype(jnp.bfloat16)
        buf[g, 0] = high
        buf[g, 1] = (kern - high.astype(jnp.float32)).astype(jnp.bfloat16)

    def reduce(entry, buf, g):
        s, q = pair_ids(entry)
        high, low = buf[g, 0], buf[g, 1]
        y = tgt_rows[q].astype(jnp.bfloat16)
        x = src_rows[s].astype(jnp.bfloat16)
        return s, q, dot(y, high) + dot(y, low), dot_t(x, high) + dot_t(x, low)

    bufs = len(kern_bufs)
    for g in range(GROUP):
        weigh(g, kern_bufs[0], g)

    def body(trip, carry):
        start = trip * bufs * GROUP
        for u in range(bufs):
            parts = []
            for g in range(GROUP):
                weigh(start + (u + 1) * GROUP + g, kern_bufs[(u + 1) % bufs], g)
                parts.append(reduce(start + u * GROUP + g, kern_bufs[u], g))
            for s, q, src_part, tgt_part in parts:
                src_acc[s] += src_part
                tgt_acc[q] += tgt_part
        return carry

    lax.fori_loop(0, divide(total + GROUP * bufs - 1, GROUP * bufs), body, 0)

    for place in range(len(owners)):
        for m in range(per_req):
            part = tgt_acc[place * per_req + m]
            tgt_out[place // inner][place % inner, :, m * BLK : (m + 1) * BLK] = part[0:4] + part[4:8]
    if ends:
        for k in range(n_tgt):
            base = flip(k, n_tgt) * per_dev
            for b in range(per_dev):
                part = src_acc[base + b]
                src_out[k][:, b * BLK : (b + 1) * BLK] = part[0:4] + part[4:8]


def join_kernel(*refs):
    *parts, out_ref = refs
    for k, part in enumerate(parts):
        out_ref[4 * k : 4 * k + 4] = part[...]


def keep_kernel(*refs):
    refs[-1][...] = refs[0][...]


def pick_kernel(*refs):
    *parts, out_ref = refs
    for k, part in enumerate(parts):
        out_ref[k] = part[1]


def finish_side(pos, weight, pot, live, total):
    mass = total[3:4]
    return pos * mass - total[0:3], jnp.where(live, pot - entropic * mass / weight, 0.0)


def src_kernel(n_tgt, per_req, me_ref, src_count_ref, tgt_count_ref, pos_ref, weight_ref, pot_ref, *refs):
    parts, refs = refs[:n_tgt], refs[n_tgt:]
    *tgt_in, grad_pos_ref, grad_weight_ref, ids_ref, live_ref = refs
    for b in range(src_count_ref.shape[0]):
        cols = slice(b * BLK, (b + 1) * BLK)
        grad_pos_ref[:, cols], grad_weight_ref[:, cols] = finish_side(
            pos_ref[:, cols],
            weight_ref[:, cols],
            pot_ref[:, cols],
            live_row(src_count_ref, b),
            sum(p[:, cols] for p in parts),
        )
    for b in range(tgt_count_ref.shape[0]):
        live_ref[:, b * BLK : (b + 1) * BLK] = live_row(tgt_count_ref, b).astype(jnp.float32)
    outer = len(tgt_in)
    inner = tgt_in[0].shape[0] // 4
    outer_me, inner_me = me_ref[1], me_ref[2]
    me = outer_me * inner + inner_me
    own = tgt_count_ref.shape[0] * BLK
    width = tgt_in[0].shape[1] - own
    lane = lax.broadcasted_iota(jnp.int32, (1, width), 1)
    for k in range(outer):
        for i in range(inner):
            row = tgt_in[flip(k, outer)][4 * i : 4 * i + 1, own:]
            for m in range(per_req):
                block = jnp.sum(jnp.where(lane == me * per_req + m, row, 0.0), axis=1, keepdims=True)
                ids_ref[(k * inner + i) * per_req + m] = jnp.broadcast_to(block, (4, BLK))


def tgt_kernel(outer, inner, pos_ref, weight_ref, pot_ref, live_ref, ids_ref, *refs):
    *parts, grad_pos_ref, grad_weight_ref = refs
    own, side = parts[:outer], parts[outer:]
    per_req = ids_ref.shape[0] // (outer * inner)
    for b in range(pos_ref.shape[1] // BLK):
        cols = slice(b * BLK, (b + 1) * BLK)
        total = jnp.zeros((4, BLK), jnp.float32)
        for k in range(outer):
            for i in range(inner):
                for m in range(per_req):
                    wide = slice(m * BLK, (m + 1) * BLK)
                    part = own[k][0, :, wide] if i == 0 else side[i - 1][k, :, wide]
                    total += jnp.where(ids_ref[(k * inner + i) * per_req + m] == b, part, 0.0)
        grad_pos_ref[:, cols], grad_weight_ref[:, cols] = finish_side(
            pos_ref[:, cols], weight_ref[:, cols], pot_ref[:, cols], live_ref[:, cols] > 0.0, total
        )


def shards(
    src_pos,
    src_weight,
    src_pot,
    src_count,
    tgt_pos,
    tgt_weight,
    tgt_pot,
    tgt_count,
    requests,
    pair_src,
    pair_slot,
    pair_count,
):
    f32 = jnp.float32
    n_tgt, n_clus = lax.axis_size("tgt"), lax.axis_size("clus")
    outer, inner = split_axis(n_clus)
    ns, nt = src_pos.shape[1], tgt_pos.shape[1]
    n_src = n_tgt * (ns // BLK)
    per_req = requests.shape[1]
    slots = n_clus * per_req
    width = -(-slots // LANES) * LANES
    asked = requests.T
    small = pltpu.CompilerParams(vmem_limit_bytes=MAIN_VMEM)
    clus_me = lax.axis_index("clus")
    me = jnp.stack([lax.axis_index("tgt"), clus_me // inner, clus_me % inner, pair_count[0]]).astype(jnp.int32)
    src_side = (src_pos, src_weight.reshape(1, -1), src_pot.reshape(1, -1))
    tgt_side = (tgt_pos, tgt_weight.reshape(1, -1), tgt_pot.reshape(1, -1))

    src_pack, tgt_pack, plan = pl.pallas_call(
        pack_kernel,
        name="pack",
        out_shape=(
            jax.ShapeDtypeStruct((4, ns), f32),
            jax.ShapeDtypeStruct((4, nt + width), f32),
            jax.ShapeDtypeStruct((slots + 2 * pair_src.shape[0],), jnp.int32),
        ),
        in_specs=[SMEM] * 5 + [VMEM] * 6,
        out_specs=(VMEM, VMEM, SMEM),
        compiler_params=pltpu.CompilerParams(vmem_limit_bytes=PACK_VMEM),
    )(asked, pair_src, pair_slot, src_count, tgt_count, *src_side, *tgt_side)

    src_in = [src_pack] + [moved(src_pack, "tgt", k) for k in range(1, n_tgt)]
    near = [tgt_pack] + [moved_inner(tgt_pack, "clus", k) for k in range(1, inner)]
    near = pl.pallas_call(
        join_kernel,
        name="join",
        out_shape=jax.ShapeDtypeStruct((4 * inner, nt + width), f32),
        in_specs=[VMEM] * inner,
        out_specs=VMEM,
        compiler_params=small,
    )(*near)
    tgt_in = [near] + [moved_outer(near, "clus", k) for k in range(1, outer)]

    block_rows = jax.ShapeDtypeStruct((n_src + 1, 8, BLK), f32)
    left_side = jax.ShapeDtypeStruct((n_src + 1, 32, BLK), jnp.bfloat16)
    lists = (me, plan)
    scratch = (
        [pltpu.SMEM((pair_src.shape[0] + 1,), jnp.int32)] * 2
        + [pltpu.SemaphoreType.DMA((len(lists),))]
        + [pltpu.SMEM(a.shape, jnp.int32) for a in lists]
        + [pltpu.VMEM((GROUP, 2, BLK, BLK), jnp.bfloat16)] * BUFS
    )
    part_shape = jax.ShapeDtypeStruct((inner, 4, per_req * BLK), f32)
    state, sums = (), {}
    for turn, (first, stop) in enumerate(stages(outer)):
        begins, ends = turn == 0, turn == len(stages(outer)) - 1
        held = [k for cut in stages(outer)[1:turn] for k in range(*cut)] if ends else []
        args = (src_in if begins else list(state)) + tgt_in[first:stop] + [sums[k] for k in held]
        outs = [left_side, block_rows] if begins and not ends else []
        outs += [jax.ShapeDtypeStruct((4, ns), f32)] * n_tgt if ends else [block_rows]
        outs += [part_shape] * (stop - first + len(held))
        extra = [pltpu.VMEM(block_rows.shape, f32)] if ends else []
        if begins and ends:
            extra += [pltpu.VMEM(left_side.shape, jnp.bfloat16), pltpu.VMEM(block_rows.shape, f32)]
        near = (stop - first) * inner * per_req
        extra += [
            pltpu.VMEM((near, BLK, 32), jnp.bfloat16),
            pltpu.VMEM((near, 8, BLK), f32),
            pltpu.VMEM((near, 8, BLK), f32),
        ]
        res = pl.pallas_call(
            functools.partial(pairs_kernel, n_tgt, n_clus, per_req, turn),
            name=f"pairs_{first}_{stop}",
            out_shape=outs,
            in_specs=[ANY] * len(lists) + [VMEM] * len(args),
            out_specs=[VMEM] * len(outs),
            scratch_shapes=extra + scratch,
            compiler_params=small,
            cost_estimate=pl.CostEstimate(flops=4*10**8 if begins else 0, bytes_accessed=2**20, transcendentals=0),
        )(*lists, *args)
        made = list(range(first, stop)) + held
        sums.update(zip(made, res[len(res) - len(made) :]))
        if ends:
            src_out = res[:n_tgt]
        else:
            state = tuple(res[:3]) if begins else (state[0], state[1], res[0])

    src_parts = [src_out[0]] + [moved(src_out[k], "tgt", k) for k in range(1, n_tgt)]
    tgt_parts = [sums[0]] + [moved_outer(sums[k], "clus", flip(k, outer)) for k in range(1, outer)]
    part_keep = functools.partial(
        pl.pallas_call,
        keep_kernel,
        name="keep",
        out_shape=part_shape,
        out_specs=VMEM,
        compiler_params=small,
    )
    for k in reversed(range(2, outer)):
        late = tgt_parts[k + 1 : k + 2]
        tgt_parts[k] = part_keep(in_specs=[VMEM] * (1 + len(late)))(tgt_parts[k], *late)
    if inner == 2:
        beside = pl.pallas_call(
            pick_kernel,
            name="pick",
            out_shape=jax.ShapeDtypeStruct((outer, 4, per_req * BLK), f32),
            in_specs=[VMEM] * outer,
            out_specs=VMEM,
            compiler_params=small,
        )(*tgt_parts)
        tgt_parts.append(moved_inner(beside, "clus", 1))

    grad_src_pos, grad_src_weight, ids, live = pl.pallas_call(
        functools.partial(src_kernel, n_tgt, per_req),
        name="finish_src",
        out_shape=(
            jax.ShapeDtypeStruct((3, ns), f32),
            jax.ShapeDtypeStruct((1, ns), f32),
            jax.ShapeDtypeStruct((slots, 4, BLK), f32),
            jax.ShapeDtypeStruct((1, nt), f32),
        ),
        in_specs=[SMEM] * 3 + [VMEM] * (3 + n_tgt + outer),
        out_specs=(VMEM,) * 4,
        compiler_params=small,
    )(me, src_count, tgt_count, *src_side, *src_parts, *tgt_in)
    grad_tgt_pos, grad_tgt_weight = pl.pallas_call(
        functools.partial(tgt_kernel, outer, inner),
        name="finish_tgt",
        out_shape=(jax.ShapeDtypeStruct((3, nt), f32), jax.ShapeDtypeStruct((1, nt), f32)),
        in_specs=[VMEM] * (5 + len(tgt_parts)),
        out_specs=(VMEM,) * 2,
        compiler_params=small,
    )(*tgt_side, live, ids, *tgt_parts)
    return grad_src_pos, grad_src_weight.reshape(-1), grad_tgt_pos, grad_tgt_weight.reshape(-1)


def solution(mesh):
    placed = (
        P(None, ("clus", "tgt")),
        P(("clus", "tgt")),
        P(("clus", "tgt")),
        P(("clus", "tgt")),
        P(None, ("clus", "tgt")),
        P(("clus", "tgt")),
        P(("clus", "tgt")),
        P(("clus", "tgt")),
        P(("clus", "tgt"), None),
        P(("clus", "tgt")),
        P(("clus", "tgt")),
        P(("clus", "tgt")),
    )
    return jax.shard_map(
        shards,
        mesh=mesh,
        in_specs=placed,
        out_specs=(
            P(None, ("clus", "tgt")),
            P(("clus", "tgt")),
            P(None, ("clus", "tgt")),
            P(("clus", "tgt")),
        ),
        check_vma=False,
    )
```

time: 37.1 us -> 33.4 us (0.900)
  waiting for transfers between devices: 7.04 us -> 1.82 us
  starting transfers between devices: 15.7 us -> 18.1 us
  Pallas kernels: 12.4 us -> 10.7 us
  local copies, waits for them, and re-layouts: 0.07 us -> 0.71 us
    all_to_all x1 -> x0, starting transfers between devices: 4.58 us -> none  [shards(): lax.all_to_all(tgt_out, 'clus', split_axis=0, concat_axis=0, tiled=True)]
    ppermute x3 -> x6, starting transfers between devices: 4.45 us -> 8.91 us  [moved_outer(): return lax.ppermute(x, axis, pairs)]
    ppermute x1 -> x2, starting transfers between devices: 1.68 us -> 5.46 us  [moved_inner(): return lax.ppermute(x, axis, pairs)]
    ppermute x6, waiting for transfers between devices: 3.09 us -> 0.02 us  [moved(): return lax.ppermute(x, axis, [(i, step(i, k, n)) for i in range(n)])]
    pallas_call x4 -> x8, Pallas kernels: 9.67 us -> 7.88 us  [the longest x3 7.16 us: shards(): pl.pallas_call(functools.partial(pairs_kernel, n_tgt, n_clus, per_req, tu...]
    ppermute x6, starting transfers between devices: 4.97 us -> 3.72 us  [moved(): return lax.ppermute(x, axis, [(i, step(i, k, n)) for i in range(n)])]
    ppermute x1 -> x2, waiting for transfers between devices: 1.68 us -> 0.59 us  [moved_inner(): return lax.ppermute(x, axis, pairs)]
    all_to_all x1 -> x0, waiting for transfers between devices: 0.69 us -> none  [shards(): lax.all_to_all(tgt_out, 'clus', split_axis=0, concat_axis=0, tiled=True)]
  transfers between devices with their start and end apart: 11 -> 14, of which waited for: 5 -> 3; matrix products, arithmetic and copies ran while one was open for 0% -> 0% of each run, Pallas kernels for 15% -> 16%
where the time goes in v4:
time: 33.4 us; the launch traced here: 32.9 us
  starting transfers between devices  18.1 us (54%)
  Pallas kernels  10.7 us (32%)
  waiting for transfers between devices  1.82 us (5%)
  between operations  1.52 us (5%)
  local copies, waits for them, and re-layouts  0.71 us (2%)
    ppermute x6, starting transfers between devices, moved_outer(): return lax.ppermute(x, axis, pairs)  8.91 us
    pallas_call x3, Pallas kernels, shards(): pl.pallas_call(functools.partial(pairs_kernel, n_tgt, n_clus, per_req, tu...  7.16 us
    ppermute x2, starting transfers between devices, moved_inner(): return lax.ppermute(x, axis, pairs)  5.46 us
    ppermute x6, starting transfers between devices, moved(): return lax.ppermute(x, axis, [(i, step(i, k, n)) for i in range(n)])  3.72 us
    pallas_call x1, Pallas kernels, shards(): pl.pallas_call(pack_kernel, name='pack', out_shape=(jax.ShapeDtypeStruct(...  1.57 us
    ppermute x6, waiting for transfers between devices, moved_outer(): return lax.ppermute(x, axis, pairs)  1.22 us
    pallas_call x1, Pallas kernels, shards(): pl.pallas_call(functools.partial(src_kernel, n_tgt, per_req), name='finis...  1.21 us
    unnamed x22, local copies, waits for them, and re-layouts  0.71 us
  transfers between devices with their start and end apart: 14, of which 3 were waited for; matrix products, arithmetic and copies ran while one was open for 0% of the time, Pallas kernels for 16%

profile of v4, /device:TPU:0, one launch (start us, length us, event | category | flops | bytes accessed | tf_op | source)
XLA Modules:
  0.0 32.9 jit_solution(17084671598220903067)
XLA Ops:
  0.6 1.6 %pack.1 = (f32[4,2048]{1,0:T(4,128)}, f32[4,2176]{1,0:T(4,128)}, s32[80]{0:T(128)}) custom-call(s32[2,8]{1,0:T(2,128)} %bitcast.18, s32[32]{0:T(128)} %ps_ref.1, s32[32]{0:T(128)} %pq_ref.1, s32[8]{0:T(128)} %src_count_ref.1, s32[8]{0:T(128)} %tgt_count_ref.1, f32[3,2048]{1,0:T(4,128)} %pos_ref.2, f32[1,2048]{1,0:T(1,128)} %bitcast.10, f32[1,2048]{1,0:T(1,128)} %bitcast.12, ...), custom_call_target="tpu_custom_call" | custom-call | tf_op jit(solution)/shard_map/pack/pallas_call | solution.py:381
  2.2 0.0 copy-start.2
  2.2 3.0 %collective-permute-start.3 = (f32[4,2176]{1,0:T(4,128)}, f32[4,2176]{1,0:T(4,128)S(1)}, u32[]{:S(2)}, u32[]{:S(2)}) collective-permute-start(f32[4,2176]{1,0:T(4,128)} %get-tuple-element.28.refs_0_), channel_id=1, source_target_pairs={{0,4},{4,0},{8,12},{12,8},{16,20},{20,16},{24,28},{28,24},{1,5},{5... | collective-permute-start | bytes 104456 | tf_op jit(solution)/shard_map/ppermute | solution.py:64
  5.2 0.0 collective-permute-start
  5.2 1.5 %collective-permute-start.1 = (f32[4,2048]{1,0:T(4,128)}, f32[4,2048]{1,0:T(4,128)S(1)}, u32[]{:S(2)}, u32[]{:S(2)}) collective-permute-start(f32[4,2048]{1,0:T(4,128)} %get-tuple-element.27.refs_2_), channel_id=1, source_target_pairs={{0,2},{1,3},{2,0},{3,1},{4,6},{5,7},{6,4},{7,5},{8,10},{9,11},{10,... | collective-permute-start | bytes 98312 | tf_op jit(solution)/shard_map/ppermute | solution.py:52
  6.7 0.3 %collective-permute-start.2 = (f32[4,2048]{1,0:T(4,128)}, f32[4,2048]{1,0:T(4,128)S(1)}, u32[]{:S(2)}, u32[]{:S(2)}) collective-permute-start(f32[4,2048]{1,0:T(4,128)} %get-tuple-element.27.refs_2_), channel_id=1, source_target_pairs={{0,3},{1,2},{2,1},{3,0},{4,7},{5,6},{6,5},{7,4},{8,11},{9,10},{10,... | collective-permute-start | bytes 98312 | tf_op jit(solution)/shard_map/ppermute | solution.py:52
  7.7 0.0 copy-start.10
  7.8 0.0 collective-permute-done.3.refs_1_
  7.8 0.0 copy-done.2
  7.8 3.8 %collective-permute-start.4 = (f32[8,2176]{1,0:T(8,128)S(1)}, f32[8,2176]{1,0:T(8,128)S(1)}, u32[]{:S(2)}, u32[]{:S(2)}) collective-permute-start(f32[8,2176]{1,0:T(8,128)S(1)} %join.1.refs_6_.refs_4_), channel_id=1, source_target_pairs={{0,24},{4,28},{8,16},{12,20},{16,8},{20,12},{24,0},{28,4},{1,25},{... | collective-permute-start | bytes 208904 | tf_op jit(solution)/shard_map/ppermute | solution.py:58
  11.6 0.0 collective-permute-start.5
  11.6 0.0 collective-permute-done.refs_3_
  11.6 0.7 %collective-permute-start.6 = (f32[8,2176]{1,0:T(8,128)S(1)}, f32[8,2176]{1,0:T(8,128)S(1)}, u32[]{:S(2)}, u32[]{:S(2)}) collective-permute-start(f32[8,2176]{1,0:T(8,128)S(1)} %join.1.refs_6_.refs_4_), channel_id=1, source_target_pairs={{0,16},{4,20},{8,24},{12,28},{16,0},{20,4},{24,8},{28,12},{1,17},{... | collective-permute-start | bytes 208904 | tf_op jit(solution)/shard_map/ppermute | solution.py:58
  12.2 0.1 pad_add_fusion.refs_0_.me_ref
  12.3 0.0 copy-start.7
  12.3 0.0 collective-permute-done.1.refs_4_
  12.3 0.0 collective-permute-done.2.refs_5_
  12.3 0.0 copy-done.10
  12.3 0.7 %copy-done.7 = s32[80]{0:T(128)S(1)} copy-done((s32[80]{0:T(128)S(1)}, s32[80]{0:T(128)}, u32[]{:S(2)}) %copy-start.7) | copy-done | bytes 344
  13.0 2.0 %pairs_0_1.1 = (bf16[33,32,256]{2,1,0:T(8,128)(2,1)S(1)}, f32[33,8,256]{2,1,0:T(8,128)S(1)}, f32[33,8,256]{2,1,0:T(8,128)S(1)}, f32[2,4,512]{2,1,0:T(4,128)S(1)}) custom-call(s32[4]{0:T(128)S(1)} %pad_add_fusion.refs_0_.me_ref, s32[80]{0:T(128)S(1)} %copy-done.7, f32[4,2048]{1,0:T(4,128)S(1)} %copy-done.10, f32[4,2048]{1,0:T(4,128)S(1)} %collective-permute-done.refs_3_, ...), custom_call_target="tpu_custom_call" | custom-call | flops 400000000 | bytes 1048576 | tf_op jit(solution)/shard_map/pairs_0_1/pallas_call | solution.py:433
  15.0 0.0 collective-permute-done.4.refs_5_.refs_7_
  15.0 2.0 %pairs_3_4.1 = (f32[33,8,256]{2,1,0:T(8,128)S(1)}, f32[2,4,512]{2,1,0:T(4,128)S(1)}) custom-call(s32[4]{0:T(128)S(1)} %pad_add_fusion.refs_0_.me_ref, s32[80]{0:T(128)S(1)} %copy-done.7, bf16[33,32,256]{2,1,0:T(8,128)(2,1)S(1)} %get-tuple-element.29.refs_2_, f32[33,8,256]{2,1,0:T(8,128)S(1)} %get-tuple-element.30.refs_3_, ...), custom_call_target="tpu_custom_call" | custom-call | bytes 1048576 | tf_op jit(solution)/shard_map/pairs_3_4/pallas_call | solution.py:433
  17.0 0.0 collective-permute-done.5.refs_5_
  17.1 0.5 %collective-permute-done.6.refs_6_ = f32[8,2176]{1,0:T(8,128)S(1)} collective-permute-done((f32[8,2176]{1,0:T(8,128)S(1)}, f32[8,2176]{1,0:T(8,128)S(1)}, u32[]{:S(2)}, u32[]{:S(2)}) %collective-permute-start.6) | collective-permute-done | bytes 69664 | tf_op jit(solution)/shard_map/ppermute | solution.py:58
  17.5 3.1 %pairs_1_3.1 = (f32[4,2048]{1,0:T(4,128)S(1)}, f32[4,2048]{1,0:T(4,128)S(1)}, f32[4,2048]{1,0:T(4,128)S(1)}, f32[4,2048]{1,0:T(4,128)S(1)}, f32[2,4,512]{2,1,0:T...) custom-call(s32[4]{0:T(128)S(1)} %pad_add_fusion.refs_0_.me_ref, s32[80]{0:T(128)S(1)} %copy-done.7, ...), custom_call_target="tpu_custom_call" | custom-call | bytes 1048576 | tf_op jit(solution)/shard_map/pairs_1_3/pallas_call | solution.py:433
  20.7 2.3 %collective-permute-start.12 = (f32[2,4,512]{2,1,0:T(4,128)S(1)}, f32[2,4,512]{2,1,0:T(4,128)S(1)}, u32[]{:S(2)}, u32[]{:S(2)}) collective-permute-start(f32[2,4,512]{2,1,0:T(4,128)S(1)} %get-tuple-element.45), channel_id=1, source_target_pairs={{0,24},{4,28},{8,16},{12,20},{16,8},{20,12},{24,0},{28,4},{1,25},{... | collective-permute-start | bytes 49160 | tf_op jit(solution)/shard_map/ppermute | solution.py:58
  23.0 0.5 %collective-permute-start.11 = (f32[2,4,512]{2,1,0:T(4,128)S(1)}, f32[2,4,512]{2,1,0:T(4,128)S(1)}, u32[]{:S(2)}, u32[]{:S(2)}) collective-permute-start(f32[2,4,512]{2,1,0:T(4,128)S(1)} %get-tuple-element.44), channel_id=1, source_target_pairs={{0,16},{4,20},{8,24},{12,28},{16,0},{20,4},{24,8},{28,12},{1,17},{... | collective-permute-start | bytes 49160 | tf_op jit(solution)/shard_map/ppermute | solution.py:58
  23.5 1.6 %collective-permute-start.10 = (f32[2,4,512]{2,1,0:T(4,128)S(1)}, f32[2,4,512]{2,1,0:T(4,128)S(1)}, u32[]{:S(2)}, u32[]{:S(2)}) collective-permute-start(f32[2,4,512]{2,1,0:T(4,128)S(1)} %get-tuple-element.43), channel_id=1, source_target_pairs={{0,8},{4,12},{8,0},{12,4},{16,24},{20,28},{24,16},{28,20},{1,9},{5... | collective-permute-start | bytes 49160 | tf_op jit(solution)/shard_map/ppermute | solution.py:58
  25.1 0.0 collective-permute-start.7
  25.1 1.5 %collective-permute-start.8 = (f32[4,2048]{1,0:T(4,128)S(1)}, f32[4,2048]{1,0:T(4,128)S(1)}, u32[]{:S(2)}, u32[]{:S(2)}) collective-permute-start(f32[4,2048]{1,0:T(4,128)S(1)} %get-tuple-element.36), channel_id=1, source_target_pairs={{0,2},{1,3},{2,0},{3,1},{4,6},{5,7},{6,4},{7,5},{8,10},{9,11},{10,... | collective-permute-start | bytes 98312 | tf_op jit(solution)/shard_map/ppermute | solution.py:52
  26.7 0.0 collective-permute-done.12.refs_0_
  26.7 0.3 %collective-permute-start.9 = (f32[4,2048]{1,0:T(4,128)S(1)}, f32[4,2048]{1,0:T(4,128)S(1)}, u32[]{:S(2)}, u32[]{:S(2)}) collective-permute-start(f32[4,2048]{1,0:T(4,128)S(1)} %get-tuple-element.37), channel_id=1, source_target_pairs={{0,3},{1,2},{2,1},{3,0},{4,7},{5,6},{6,5},{7,4},{8,11},{9,10},{10,... | collective-permute-start | bytes 98312 | tf_op jit(solution)/shard_map/ppermute | solution.py:52
  27.0 0.7 %collective-permute-done.11.refs_0_ = f32[2,4,512]{2,1,0:T(4,128)S(1)} collective-permute-done((f32[2,4,512]{2,1,0:T(4,128)S(1)}, f32[2,4,512]{2,1,0:T(4,128)S(1)}, u32[]{:S(2)}, u32[]{:S(2)}) %collective-permute-start.11) | collective-permute-done | bytes 16416 | tf_op jit(solution)/shard_map/ppermute | solution.py:58
  27.7 0.0 collective-permute-done.10.refs_1_
  27.7 0.0 copy-start
  27.7 0.0 copy-start.3
  27.8 0.0 copy-start.4
  27.8 0.0 copy-start.8
  27.8 0.0 copy-start.9
  27.8 2.5 %collective-permute-start.13 = (f32[4,4,512]{2,1,0:T(4,128)S(1)}, f32[4,4,512]{2,1,0:T(4,128)S(1)}, u32[]{:S(2)}, u32[]{:S(2)}) collective-permute-start(f32[4,4,512]{2,1,0:T(4,128)S(1)} %pick.1), channel_id=1, source_target_pairs={{0,4},{4,0},{8,12},{12,8},{16,20},{20,16},{24,28},{28,24},{1,5},{5... | collective-permute-start | bytes 98312 | tf_op jit(solution)/shard_map/ppermute | solution.py:64
  30.3 0.0 collective-permute-done.7.refs_1_
  30.3 0.0 collective-permute-done.8.refs_2_
  30.3 0.0 collective-permute-done.9.refs_3_
  30.3 0.0 copy-done
  30.3 0.0 copy-done.3
  30.3 0.0 copy-done.4
  30.3 0.0 copy-done.8
  30.3 0.0 copy-done.9
  30.3 0.0 copy-start.1
  30.3 0.0 copy-start.5
  30.3 0.0 copy-start.6
  30.4 1.2 %finish_src.1 = (f32[3,2048]{1,0:T(4,128)}, f32[1,2048]{1,0:T(1,128)}, f32[16,4,256]{2,1,0:T(4,128)S(1)}, f32[1,2048]{1,0:T(1,128)S(1)}) custom-call(s32[4]{0:T(128)S(1)} %pad_add_fusion.refs_0_.me_ref, s32[8]{0:T(128)S(1)} %copy-done.8, s32[8]{0:T(128)S(1)} %copy-done.9, f32[3,2048]{1,0:T(4,128)S(1)} %copy-done, f32[1,2048]{1,0:T(1,128)S(1)} %bitcast.11, ...), custom_call_target="tpu_custom_call" | custom-call | tf_op jit(solution)/shard_map/finish_src/pallas_call | solution.py:474
  31.6 0.6 %collective-permute-done.13.refs_4_ = f32[4,4,512]{2,1,0:T(4,128)S(1)} collective-permute-done((f32[4,4,512]{2,1,0:T(4,128)S(1)}, f32[4,4,512]{2,1,0:T(4,128)S(1)}, u32[]{:S(2)}, u32[]{:S(2)}) %collective-permute-start.13) | collective-permute-done | bytes 32800 | tf_op jit(solution)/shard_map/ppermute | solution.py:64
  32.1 0.0 copy-done.1
  32.2 0.0 copy-done.5
  32.2 0.0 copy-done.6
  32.2 0.7 %finish_tgt.1 = (f32[3,2048]{1,0:T(4,128)}, f32[1,2048]{1,0:T(1,128)}) custom-call(f32[3,2048]{1,0:T(4,128)S(1)} %copy-done.1, f32[1,2048]{1,0:T(1,128)S(1)} %bitcast.15, f32[1,2048]{1,0:T(1,128)S(1)} %bitcast.17, f32[1,2048]{1,0:T(1,128)S(1)} %get-tuple-element.40.live_ref, f32[16,4,256]{2,1,0:T(4,128)S(1)} %get-tuple-element.41.ids_ref, ...), custom_call_target="tpu_custom_call" | custom-call | tf_op jit(solution)/shard_map/finish_tgt/pallas_call | solution.py:487
  (4 shorter events, 0.0 us)
Async XLA Ops:
  2.2 5.6 %copy-start.2 = (f32[4,2176]{1,0:T(4,128)S(1)}, f32[4,2176]{1,0:T(4,128)}, u32[]{:S(2)}) copy-start(f32[4,2176]{1,0:T(4,128)} %get-tuple-element.28.refs_0_) | copy-start | bytes 104452
  2.2 5.5 %collective-permute-start.3 = (f32[4,2176]{1,0:T(4,128)}, f32[4,2176]{1,0:T(4,128)S(1)}, u32[]{:S(2)}, u32[]{:S(2)}) collective-permute-start(f32[4,2176]{1,0:T(4,128)} %get-tuple-element.28.refs_0_), channel_id=1, source_target_pairs={{0,4},{4,0},{8,12},{12,8},{16,20},{20,16},{24,28},{28,24},{1,5},{5... | collective-permute-start | bytes 104456 | tf_op jit(solution)/shard_map/ppermute | solution.py:64
  5.2 6.3 %collective-permute-start = (f32[4,2048]{1,0:T(4,128)}, f32[4,2048]{1,0:T(4,128)S(1)}, u32[]{:S(2)}, u32[]{:S(2)}) collective-permute-start(f32[4,2048]{1,0:T(4,128)} %get-tuple-element.27.refs_2_), channel_id=1, source_target_pairs={{0,1},{1,0},{2,3},{3,2},{4,5},{5,4},{6,7},{7,6},{8,9},{9,8},{10,11... | collective-permute-start | bytes 98312 | tf_op jit(solution)/shard_map/ppermute | solution.py:52
  5.2 7.1 %collective-permute-start.1 = (f32[4,2048]{1,0:T(4,128)}, f32[4,2048]{1,0:T(4,128)S(1)}, u32[]{:S(2)}, u32[]{:S(2)}) collective-permute-start(f32[4,2048]{1,0:T(4,128)} %get-tuple-element.27.refs_2_), channel_id=1, source_target_pairs={{0,2},{1,3},{2,0},{3,1},{4,6},{5,7},{6,4},{7,5},{8,10},{9,11},{10,... | collective-permute-start | bytes 98312 | tf_op jit(solution)/shard_map/ppermute | solution.py:52
  6.7 5.6 %collective-permute-start.2 = (f32[4,2048]{1,0:T(4,128)}, f32[4,2048]{1,0:T(4,128)S(1)}, u32[]{:S(2)}, u32[]{:S(2)}) collective-permute-start(f32[4,2048]{1,0:T(4,128)} %get-tuple-element.27.refs_2_), channel_id=1, source_target_pairs={{0,3},{1,2},{2,1},{3,0},{4,7},{5,6},{6,5},{7,4},{8,11},{9,10},{10,... | collective-permute-start | bytes 98312 | tf_op jit(solution)/shard_map/ppermute | solution.py:52
  7.7 4.6 %copy-start.10 = (f32[4,2048]{1,0:T(4,128)S(1)}, f32[4,2048]{1,0:T(4,128)}, u32[]{:S(2)}) copy-start(f32[4,2048]{1,0:T(4,128)} %get-tuple-element.27.refs_2_) | copy-start | bytes 98308
  7.8 7.2 %collective-permute-start.4 = (f32[8,2176]{1,0:T(8,128)S(1)}, f32[8,2176]{1,0:T(8,128)S(1)}, u32[]{:S(2)}, u32[]{:S(2)}) collective-permute-start(f32[8,2176]{1,0:T(8,128)S(1)} %join.1.refs_6_.refs_4_), channel_id=1, source_target_pairs={{0,24},{4,28},{8,16},{12,20},{16,8},{20,12},{24,0},{28,4},{1,25},{... | collective-permute-start | bytes 208904 | tf_op jit(solution)/shard_map/ppermute | solution.py:58
  11.6 5.5 %collective-permute-start.5 = (f32[8,2176]{1,0:T(8,128)S(1)}, f32[8,2176]{1,0:T(8,128)S(1)}, u32[]{:S(2)}, u32[]{:S(2)}) collective-permute-start(f32[8,2176]{1,0:T(8,128)S(1)} %join.1.refs_6_.refs_4_), channel_id=1, source_target_pairs={{0,8},{4,12},{8,0},{12,4},{16,24},{20,28},{24,16},{28,20},{1,9},{5... | collective-permute-start | bytes 208904 | tf_op jit(solution)/shard_map/ppermute | solution.py:58
  11.6 6.0 %collective-permute-start.6 = (f32[8,2176]{1,0:T(8,128)S(1)}, f32[8,2176]{1,0:T(8,128)S(1)}, u32[]{:S(2)}, u32[]{:S(2)}) collective-permute-start(f32[8,2176]{1,0:T(8,128)S(1)} %join.1.refs_6_.refs_4_), channel_id=1, source_target_pairs={{0,16},{4,20},{8,24},{12,28},{16,0},{20,4},{24,8},{28,12},{1,17},{... | collective-permute-start | bytes 208904 | tf_op jit(solution)/shard_map/ppermute | solution.py:58
  12.3 0.7 %copy-start.7 = (s32[80]{0:T(128)S(1)}, s32[80]{0:T(128)}, u32[]{:S(2)}) copy-start(s32[80]{0:T(128)} %get-tuple-element.26.refs_1_) | copy-start | bytes 964
  20.7 6.0 %collective-permute-start.12 = (f32[2,4,512]{2,1,0:T(4,128)S(1)}, f32[2,4,512]{2,1,0:T(4,128)S(1)}, u32[]{:S(2)}, u32[]{:S(2)}) collective-permute-start(f32[2,4,512]{2,1,0:T(4,128)S(1)} %get-tuple-element.45), channel_id=1, source_target_pairs={{0,24},{4,28},{8,16},{12,20},{16,8},{20,12},{24,0},{28,4},{1,25},{... | collective-permute-start | bytes 49160 | tf_op jit(solution)/shard_map/ppermute | solution.py:58
  23.0 4.8 %collective-permute-start.11 = (f32[2,4,512]{2,1,0:T(4,128)S(1)}, f32[2,4,512]{2,1,0:T(4,128)S(1)}, u32[]{:S(2)}, u32[]{:S(2)}) collective-permute-start(f32[2,4,512]{2,1,0:T(4,128)S(1)} %get-tuple-element.44), channel_id=1, source_target_pairs={{0,16},{4,20},{8,24},{12,28},{16,0},{20,4},{24,8},{28,12},{1,17},{... | collective-permute-start | bytes 49160 | tf_op jit(solution)/shard_map/ppermute | solution.py:58
  23.5 4.2 %collective-permute-start.10 = (f32[2,4,512]{2,1,0:T(4,128)S(1)}, f32[2,4,512]{2,1,0:T(4,128)S(1)}, u32[]{:S(2)}, u32[]{:S(2)}) collective-permute-start(f32[2,4,512]{2,1,0:T(4,128)S(1)} %get-tuple-element.43), channel_id=1, source_target_pairs={{0,8},{4,12},{8,0},{12,4},{16,24},{20,28},{24,16},{28,20},{1,9},{5... | collective-permute-start | bytes 49160 | tf_op jit(solution)/shard_map/ppermute | solution.py:58
  25.1 5.1 %collective-permute-start.7 = (f32[4,2048]{1,0:T(4,128)S(1)}, f32[4,2048]{1,0:T(4,128)S(1)}, u32[]{:S(2)}, u32[]{:S(2)}) collective-permute-start(f32[4,2048]{1,0:T(4,128)S(1)} %get-tuple-element.35), channel_id=1, source_target_pairs={{0,1},{1,0},{2,3},{3,2},{4,5},{5,4},{6,7},{7,6},{8,9},{9,8},{10,11... | collective-permute-start | bytes 98312 | tf_op jit(solution)/shard_map/ppermute | solution.py:52
  25.1 5.1 %collective-permute-start.8 = (f32[4,2048]{1,0:T(4,128)S(1)}, f32[4,2048]{1,0:T(4,128)S(1)}, u32[]{:S(2)}, u32[]{:S(2)}) collective-permute-start(f32[4,2048]{1,0:T(4,128)S(1)} %get-tuple-element.36), channel_id=1, source_target_pairs={{0,2},{1,3},{2,0},{3,1},{4,6},{5,7},{6,4},{7,5},{8,10},{9,11},{10,... | collective-permute-start | bytes 98312 | tf_op jit(solution)/shard_map/ppermute | solution.py:52
  26.7 3.6 %collective-permute-start.9 = (f32[4,2048]{1,0:T(4,128)S(1)}, f32[4,2048]{1,0:T(4,128)S(1)}, u32[]{:S(2)}, u32[]{:S(2)}) collective-permute-start(f32[4,2048]{1,0:T(4,128)S(1)} %get-tuple-element.37), channel_id=1, source_target_pairs={{0,3},{1,2},{2,1},{3,0},{4,7},{5,6},{6,5},{7,4},{8,11},{9,10},{10,... | collective-permute-start | bytes 98312 | tf_op jit(solution)/shard_map/ppermute | solution.py:52
  27.7 2.5 %copy-start = (f32[3,2048]{1,0:T(4,128)S(1)}, f32[3,2048]{1,0:T(4,128)}, u32[]{:S(2)}) copy-start(f32[3,2048]{1,0:T(4,128)} %pos_ref.2) | copy-start | bytes 73732
  27.7 2.5 %copy-start.3 = (f32[2048]{0:T(1024)S(1)}, f32[2048]{0:T(1024)}, u32[]{:S(2)}) copy-start(f32[2048]{0:T(1024)} %param.13) | copy-start | bytes 24580
  27.8 2.5 %copy-start.4 = (f32[2048]{0:T(1024)S(1)}, f32[2048]{0:T(1024)}, u32[]{:S(2)}) copy-start(f32[2048]{0:T(1024)} %param.14) | copy-start | bytes 24580
  27.8 2.5 %copy-start.8 = (s32[8]{0:T(128)S(1)}, s32[8]{0:T(128)}, u32[]{:S(2)}) copy-start(s32[8]{0:T(128)} %src_count_ref.1) | copy-start | bytes 100
  27.8 2.5 %copy-start.9 = (s32[8]{0:T(128)S(1)}, s32[8]{0:T(128)}, u32[]{:S(2)}) copy-start(s32[8]{0:T(128)} %tgt_count_ref.1) | copy-start | bytes 100
  27.8 4.3 %collective-permute-start.13 = (f32[4,4,512]{2,1,0:T(4,128)S(1)}, f32[4,4,512]{2,1,0:T(4,128)S(1)}, u32[]{:S(2)}, u32[]{:S(2)}) collective-permute-start(f32[4,4,512]{2,1,0:T(4,128)S(1)} %pick.1), channel_id=1, source_target_pairs={{0,4},{4,0},{8,12},{12,8},{16,20},{20,16},{24,28},{28,24},{1,5},{5... | collective-permute-start | bytes 98312 | tf_op jit(solution)/shard_map/ppermute | solution.py:64
  30.3 1.8 %copy-start.1 = (f32[3,2048]{1,0:T(4,128)S(1)}, f32[3,2048]{1,0:T(4,128)}, u32[]{:S(2)}) copy-start(f32[3,2048]{1,0:T(4,128)} %pos_ref.3) | copy-start | bytes 73732
  30.3 1.8 %copy-start.5 = (f32[2048]{0:T(1024)S(1)}, f32[2048]{0:T(1024)}, u32[]{:S(2)}) copy-start(f32[2048]{0:T(1024)} %param.17) | copy-start | bytes 24580
  30.3 1.8 %copy-start.6 = (f32[2048]{0:T(1024)S(1)}, f32[2048]{0:T(1024)}, u32[]{:S(2)}) copy-start(f32[2048]{0:T(1024)} %param.18) | copy-start | bytes 24580

commit v5 on v4

--- a/solution.py
+++ b/solution.py
@@ -79,26 +79,20 @@
         out_ref[3:4, cols] = jnp.where(live_row(count_ref, b), expo, DEAD)
 
 
-def pack_kernel(
-    req_ref, ps_ref, pq_ref, sc_ref, tc_ref, sp_ref, sw_ref, so_ref, tp_ref, tw_ref, to_ref, src_ref, tgt_ref, plan_ref
-):
-    pairs = ps_ref.shape[0]
-    for pair in range(pairs):
-        plan_ref[req_ref.size + pair] = ps_ref[pair]
-        plan_ref[req_ref.size + pairs + pair] = pq_ref[pair]
+def pack_kernel(req_ref, sc_ref, tc_ref, ps_ref, pq_ref, sp_ref, sw_ref, so_ref, tp_ref, tw_ref, to_ref, src_ref, tgt_ref):
     pack_side(sp_ref, sw_ref, so_ref, sc_ref, src_ref)
     pack_side(tp_ref, tw_ref, to_ref, tc_ref, tgt_ref)
     per, rows = req_ref.shape
     own = tp_ref.shape[1]
-    width = tgt_ref.shape[1] - own
-    lane = lax.broadcasted_iota(jnp.int32, (4, width), 1)
-    ids = jnp.zeros((4, width), jnp.float32)
+    lane = lax.broadcasted_iota(jnp.int32, (1, tgt_ref.shape[1] - own), 1)
+    ids = jnp.zeros(lane.shape, jnp.float32)
     for r in range(rows):
         for m in range(per):
-            block = req_ref[m, r]
-            plan_ref[r * per + m] = block
-            ids = jnp.where(lane == r * per + m, block.astype(jnp.float32), ids)
-    tgt_ref[:, own:] = ids
+            ids = jnp.where(lane == r * per + m, req_ref[m, r].astype(jnp.float32), ids)
+    tgt_ref[:, own:] = jnp.zeros((4,) + lane.shape[1:], jnp.float32)
+    tgt_ref[0:1, own:] = ids
+    tgt_ref[1:2, own : own + ps_ref.shape[1]] = ps_ref[...].astype(jnp.float32)
+    tgt_ref[2:3, own : own + pq_ref.shape[1]] = pq_ref[...].astype(jnp.float32)
 
 
 def split3(x):
@@ -175,32 +169,37 @@
 
 def pairs_kernel(n_tgt, n_clus, per_req, turn, *refs):
     outer, inner = split_axis(n_clus)
-    first, stop = stages(outer)[turn]
-    begins, ends = turn == 0, turn == len(stages(outer)) - 1
+    cuts = stages(outer)
+    first, stop = cuts[turn]
+    begins, ends = turn == 0, turn == len(cuts) - 1
+    slots = n_clus * per_req
     refs = list(refs)
     take = lambda n: [refs.pop(0) for _ in range(n)]
-    far_lists = take(2)
     if begins:
+        (far_me,) = take(1)
         src_in = take(n_tgt)
     else:
-        left, src_rows, src_sums = take(3)
+        memo, left, src_rows, src_sums = take(4)
     tgt_in = take(stop - first)
-    held = [k for cut in stages(outer)[1:turn] for k in range(*cut)] if ends else []
+    held = [k for cut in cuts[1:turn] for k in range(*cut)] if ends else []
     held_in = take(len(held))
     if begins and not ends:
-        left, src_rows = take(2)
+        memo, left, src_rows = take(3)
     src_out = take(n_tgt if ends else 1)
     tgt_out = take(stop - first)
     for far, near in zip(held_in, take(len(held))):
         near[...] = far[...]
     src_acc = take(1)[0] if ends else src_out[0]
     if begins and ends:
-        left, src_rows = take(2)
-    right, tgt_rows, tgt_acc, chosen_src, chosen_slot, sems, *refs = refs
-    lists, kern_bufs = refs[:2], refs[2:]
-    copies = [pltpu.make_async_copy(far, near, sems.at[i]) for i, (far, near) in enumerate(zip(far_lists, lists))]
-    for copy in copies:
+        memo, left, src_rows = take(3)
+    right, tgt_rows, tgt_acc, *refs = refs
+    if begins:
+        (chosen_src, chosen_slot, sem, me_ref, head), kern_bufs = refs[:5], refs[5:]
+        copy = pltpu.make_async_copy(far_me, me_ref, sem)
         copy.start()
+        head[...] = tgt_in[0][0:4, tgt_in[0].shape[1] - head.shape[1] :].astype(jnp.int32)
+    else:
+        kern_bufs = refs
     n_src = left.shape[0] - 1
     per_dev = n_src // n_tgt
     if begins:
@@ -209,33 +208,50 @@
     else:
         src_acc[...] = src_sums[...]
     tgt_acc[...] = jnp.zeros_like(tgt_acc)
-    for copy in copies:
+
+    pairs = (memo.shape[0] - len(cuts) - slots) // (2 * len(cuts))
+    tops = [len(cuts) + slots + 2 * pairs * i for i in range(len(cuts))]
+
+    def note(row, value):
+        memo[pl.ds(row, 1), :] = jnp.full((1, LANES), value, jnp.int32)
+
+    if begins:
         copy.wait()
-
-    me_ref, plan_ref = lists
-    slots = n_clus * per_req
-    pairs = (plan_ref.shape[0] - slots) // 2
-    tgt_me, outer_me, inner_me, count = (me_ref[i] for i in range(4))
-    owners = []
-    for k in range(first, stop):
-        for i in range(inner):
-            owner = back(outer_me, k, outer) * inner + back(inner_me, i, inner)
-            for m in range(per_req):
-                slot = len(owners) * per_req + m
-                prepare_tgt(slot, plan_ref[owner * per_req + m], slice(4 * i, 4 * i + 4), tgt_in[k - first], right, tgt_rows)
-            owners.append(owner)
-
-    total = jnp.int32(0)
-    for pair in range(pairs):
-        chosen_src[total] = local_block(plan_ref[slots + pair], tgt_me, n_tgt, per_dev)
-        slot = local_slot(plan_ref[slots + pairs + pair], outer_me, inner_me, outer, inner, per_req) - first * inner * per_req
-        chosen_slot[total] = slot
-        total = total + ((pair < count) & (slot >= 0) & (slot < len(owners) * per_req)).astype(jnp.int32)
+        tgt_me, outer_me, inner_me, count = (me_ref[i] for i in range(4))
+        for slot in range(slots):
+            note(len(cuts) + local_slot(slot, outer_me, inner_me, outer, inner, per_req), head[0, slot])
+        totals = [jnp.int32(0)] * len(cuts)
+        for pair in range(pairs):
+            s = local_block(head[1, pair], tgt_me, n_tgt, per_dev)
+            slot = local_slot(head[2, pair], outer_me, inner_me, outer, inner, per_req)
+            for i, (low, high) in enumerate(cuts):
+                inside = slot - low * inner * per_req
+                if i == 0:
+                    chosen_src[totals[0]] = s
+                    chosen_slot[totals[0]] = inside
+                else:
+                    note(tops[i] + totals[i], s)
+                    note(tops[i] + pairs + totals[i], inside)
+                hit = (pair < count) & (inside >= 0) & (inside < (high - low) * inner * per_req)
+                totals[i] = totals[i] + hit.astype(jnp.int32)
+        for i in range(1, len(cuts)):
+            note(i, totals[i])
+        total = totals[0]
+    else:
+        total = memo[turn, 0]
+    for slot in range((stop - first) * inner * per_req):
+        i = slot // per_req % inner
+        block = memo[len(cuts) + first * inner * per_req + slot, 0]
+        prepare_tgt(slot, block, slice(4 * i, 4 * i + 4), tgt_in[slot // (inner * per_req)], right, tgt_rows)
 
     def pair_ids(entry):
         inside = jnp.minimum(entry, pairs - 1)
         live = entry < total
-        return jnp.where(live, chosen_src[inside], n_src), jnp.where(live, chosen_slot[inside], 0)
+        if begins:
+            s, q = chosen_src[inside], chosen_slot[inside]
+        else:
+            s, q = memo[tops[turn] + inside, 0], memo[tops[turn] + pairs + inside, 0]
+        return jnp.where(live, s, n_src), jnp.where(live, q, 0)
 
     def weigh(entry, buf, g):
         s, q = pair_ids(entry)
@@ -269,7 +285,7 @@
 
     lax.fori_loop(0, divide(total + GROUP * bufs - 1, GROUP * bufs), body, 0)
 
-    for place in range(len(owners)):
+    for place in range((stop - first) * inner):
         for m in range(per_req):
             part = tgt_acc[place * per_req + m]
             tgt_out[place // inner][place % inner, :, m * BLK : (m + 1) * BLK] = part[0:4] + part[4:8]
@@ -370,7 +386,7 @@
     n_src = n_tgt * (ns // BLK)
     per_req = requests.shape[1]
     slots = n_clus * per_req
-    width = -(-slots // LANES) * LANES
+    width = -(-max(slots, pair_src.shape[0]) // LANES) * LANES
     asked = requests.T
     small = pltpu.CompilerParams(vmem_limit_bytes=MAIN_VMEM)
     clus_me = lax.axis_index("clus")
@@ -378,18 +394,14 @@
     src_side = (src_pos, src_weight.reshape(1, -1), src_pot.reshape(1, -1))
     tgt_side = (tgt_pos, tgt_weight.reshape(1, -1), tgt_pot.reshape(1, -1))
 
-    src_pack, tgt_pack, plan = pl.pallas_call(
+    src_pack, tgt_pack = pl.pallas_call(
         pack_kernel,
         name="pack",
-        out_shape=(
-            jax.ShapeDtypeStruct((4, ns), f32),
-            jax.ShapeDtypeStruct((4, nt + width), f32),
-            jax.ShapeDtypeStruct((slots + 2 * pair_src.shape[0],), jnp.int32),
-        ),
-        in_specs=[SMEM] * 5 + [VMEM] * 6,
-        out_specs=(VMEM, VMEM, SMEM),
+        out_shape=(jax.ShapeDtypeStruct((4, ns), f32), jax.ShapeDtypeStruct((4, nt + width), f32)),
+        in_specs=[SMEM] * 3 + [VMEM] * 8,
+        out_specs=(VMEM, VMEM),
         compiler_params=pltpu.CompilerParams(vmem_limit_bytes=PACK_VMEM),
-    )(asked, pair_src, pair_slot, src_count, tgt_count, *src_side, *tgt_side)
+    )(asked, src_count, tgt_count, pair_src.reshape(1, -1), pair_slot.reshape(1, -1), *src_side, *tgt_side)
 
     src_in = [src_pack] + [moved(src_pack, "tgt", k) for k in range(1, n_tgt)]
     near = [tgt_pack] + [moved_inner(tgt_pack, "clus", k) for k in range(1, inner)]
@@ -405,24 +417,26 @@
 
     block_rows = jax.ShapeDtypeStruct((n_src + 1, 8, BLK), f32)
     left_side = jax.ShapeDtypeStruct((n_src + 1, 32, BLK), jnp.bfloat16)
-    lists = (me, plan)
-    scratch = (
-        [pltpu.SMEM((pair_src.shape[0] + 1,), jnp.int32)] * 2
-        + [pltpu.SemaphoreType.DMA((len(lists),))]
-        + [pltpu.SMEM(a.shape, jnp.int32) for a in lists]
-        + [pltpu.VMEM((GROUP, 2, BLK, BLK), jnp.bfloat16)] * BUFS
+    n_pairs = pair_src.shape[0]
+    memo_rows = jax.ShapeDtypeStruct((len(stages(outer)) * (1 + 2 * n_pairs) + slots, LANES), jnp.int32)
+    list_scratch = (
+        [pltpu.SMEM((n_pairs + 1,), jnp.int32)] * 2
+        + [pltpu.SemaphoreType.DMA, pltpu.SMEM(me.shape, jnp.int32)]
+        + [pltpu.VMEM((4, width), jnp.int32)]
     )
+    kern_bufs = [pltpu.VMEM((GROUP, 2, BLK, BLK), jnp.bfloat16)] * BUFS
     part_shape = jax.ShapeDtypeStruct((inner, 4, per_req * BLK), f32)
     state, sums = (), {}
     for turn, (first, stop) in enumerate(stages(outer)):
         begins, ends = turn == 0, turn == len(stages(outer)) - 1
         held = [k for cut in stages(outer)[1:turn] for k in range(*cut)] if ends else []
-        args = (src_in if begins else list(state)) + tgt_in[first:stop] + [sums[k] for k in held]
-        outs = [left_side, block_rows] if begins and not ends else []
+        args = ([me] + src_in if begins else list(state)) + tgt_in[first:stop] + [sums[k] for k in held]
+        outs = [memo_rows, left_side, block_rows] if begins and not ends else []
         outs += [jax.ShapeDtypeStruct((4, ns), f32)] * n_tgt if ends else [block_rows]
         outs += [part_shape] * (stop - first + len(held))
         extra = [pltpu.VMEM(block_rows.shape, f32)] if ends else []
         if begins and ends:
+            extra += [pltpu.VMEM(memo_rows.shape, jnp.int32)]
             extra += [pltpu.VMEM(left_side.shape, jnp.bfloat16), pltpu.VMEM(block_rows.shape, f32)]
         near = (stop - first) * inner * per_req
         extra += [
@@ -434,18 +448,18 @@
             functools.partial(pairs_kernel, n_tgt, n_clus, per_req, turn),
             name=f"pairs_{first}_{stop}",
             out_shape=outs,
-            in_specs=[ANY] * len(lists) + [VMEM] * len(args),
+            in_specs=[ANY if begins and a is me else VMEM for a in args],
             out_specs=[VMEM] * len(outs),
-            scratch_shapes=extra + scratch,
+            scratch_shapes=extra + (list_scratch if begins else []) + kern_bufs,
             compiler_params=small,
             cost_estimate=pl.CostEstimate(flops=4*10**8 if begins else 0, bytes_accessed=2**20, transcendentals=0),
-        )(*lists, *args)
+        )(*args)
         made = list(range(first, stop)) + held
         sums.update(zip(made, res[len(res) - len(made) :]))
         if ends:
             src_out = res[:n_tgt]
         else:
-            state = tuple(res[:3]) if begins else (state[0], state[1], res[0])
+            state = tuple(res[:4]) if begins else state[:3] + (res[0],)
 
     src_parts = [src_out[0]] + [moved(src_out[k], "tgt", k) for k in range(1, n_tgt)]
     tgt_parts = [sums[0]] + [moved_outer(sums[k], "clus", flip(k, outer)) for k in range(1, outer)]

time: 33.4 us -> 32.5 us (0.973); the launches traced: 32.9 us -> 32.3 us
  waiting for transfers between devices: 1.82 us -> 3.13 us
  starting transfers between devices: 18.1 us -> 17.3 us
  local copies, waits for them, and re-layouts: 0.71 us -> 0.06 us
  Pallas kernels: 10.7 us -> 10.3 us
    ppermute x6, waiting for transfers between devices: 1.22 us -> 2.11 us  [moved_outer(): return lax.ppermute(x, axis, pairs)]
    ppermute x2, starting transfers between devices: 5.46 us -> 4.64 us  [moved_inner(): return lax.ppermute(x, axis, pairs)]
    unnamed x22 -> x20, local copies, waits for them, and re-layouts: 0.71 us -> 0.06 us
  transfers between devices with their start and end apart: 14 -> 14, of which waited for: 3 -> 5; matrix products, arithmetic and copies ran while one was open for 0% -> 0% of each run, Pallas kernels for 16% -> 16%
where the time goes in v5:
time: 32.5 us; the launch traced here: 32.3 us
  starting transfers between devices  17.3 us (53%)
  Pallas kernels  10.3 us (32%)
  waiting for transfers between devices  3.13 us (10%)
  between operations  1.46 us (4%)
    ppermute x6, starting transfers between devices, moved_outer(): return lax.ppermute(x, axis, pairs)  8.91 us
    pallas_call x3, Pallas kernels, shards(): pl.pallas_call(functools.partial(pairs_kernel, n_tgt, n_clus, per_req, tu...  6.84 us
    ppermute x2, starting transfers between devices, moved_inner(): return lax.ppermute(x, axis, pairs)  4.64 us
    ppermute x6, starting transfers between devices, moved(): return lax.ppermute(x, axis, [(i, step(i, k, n)) for i in range(n)])  3.72 us
    ppermute x6, waiting for transfers between devices, moved_outer(): return lax.ppermute(x, axis, pairs)  2.11 us
    pallas_call x1, Pallas kernels, shards(): pl.pallas_call(pack_kernel, name='pack', out_shape=(jax.ShapeDtypeStruct(...  1.55 us
    pallas_call x1, Pallas kernels, shards(): pl.pallas_call(functools.partial(src_kernel, n_tgt, per_req), name='finis...  1.21 us
    ppermute x2, waiting for transfers between devices, moved_inner(): return lax.ppermute(x, axis, pairs)  0.72 us
  transfers between devices with their start and end apart: 14, of which 5 were waited for; matrix products, arithmetic and copies ran while one was open for 0% of the time, Pallas kernels for 16%

profile of v5, /device:TPU:0, one launch (start us, length us, event | category | flops | bytes accessed | tf_op | source)
XLA Modules:
  0.0 32.3 jit_solution(6146298554236209639)
XLA Ops:
  0.6 1.5 %pack.1 = (f32[4,2048]{1,0:T(4,128)}, f32[4,2176]{1,0:T(4,128)}) custom-call(s32[2,8]{1,0:T(2,128)} %bitcast.20, s32[8]{0:T(128)} %src_count_ref.1, s32[8]{0:T(128)} %tgt_count_ref.1, s32[1,32]{1,0:T(1,128)} %bitcast.21, s32[1,32]{1,0:T(1,128)} %bitcast.22, f32[3,2048]{1,0:T(4,128)} %pos_ref.2, f32[1,2048]{1,0:T(1,128)} %bitcast.12, f32[1,2048]{1,0:T(1,128)} %bitcast.14, ...), custom_call_target="tpu_custom_call" | custom-call | tf_op jit(solution)/shard_map/pack/pallas_call | solution.py:397
  2.2 0.0 copy-start.2
  2.2 2.9 %collective-permute-start.3 = (f32[4,2176]{1,0:T(4,128)}, f32[4,2176]{1,0:T(4,128)S(1)}, u32[]{:S(2)}, u32[]{:S(2)}) collective-permute-start(f32[4,2176]{1,0:T(4,128)} %get-tuple-element.27.refs_0_), channel_id=1, source_target_pairs={{0,4},{4,0},{8,12},{12,8},{16,20},{20,16},{24,28},{28,24},{1,5},{5... | collective-permute-start | bytes 104456 | tf_op jit(solution)/shard_map/ppermute | solution.py:64
  5.1 0.0 collective-permute-start
  5.1 1.5 %collective-permute-start.1 = (f32[4,2048]{1,0:T(4,128)}, f32[4,2048]{1,0:T(4,128)S(1)}, u32[]{:S(2)}, u32[]{:S(2)}) collective-permute-start(f32[4,2048]{1,0:T(4,128)} %get-tuple-element.26.refs_1_), channel_id=1, source_target_pairs={{0,2},{1,3},{2,0},{3,1},{4,6},{5,7},{6,4},{7,5},{8,10},{9,11},{10,... | collective-permute-start | bytes 98312 | tf_op jit(solution)/shard_map/ppermute | solution.py:52
  6.6 0.3 %collective-permute-start.2 = (f32[4,2048]{1,0:T(4,128)}, f32[4,2048]{1,0:T(4,128)S(1)}, u32[]{:S(2)}, u32[]{:S(2)}) collective-permute-start(f32[4,2048]{1,0:T(4,128)} %get-tuple-element.26.refs_1_), channel_id=1, source_target_pairs={{0,3},{1,2},{2,1},{3,0},{4,7},{5,6},{6,5},{7,4},{8,11},{9,10},{10,... | collective-permute-start | bytes 98312 | tf_op jit(solution)/shard_map/ppermute | solution.py:52
  7.6 0.0 copy-start.9
  7.7 0.0 collective-permute-done.3.refs_1_
  7.7 0.0 copy-done.2
  7.7 3.8 %collective-permute-start.4 = (f32[8,2176]{1,0:T(8,128)S(1)}, f32[8,2176]{1,0:T(8,128)S(1)}, u32[]{:S(2)}, u32[]{:S(2)}) collective-permute-start(f32[8,2176]{1,0:T(8,128)S(1)} %join.1.refs_5_.refs_4_), channel_id=1, source_target_pairs={{0,24},{4,28},{8,16},{12,20},{16,8},{20,12},{24,0},{28,4},{1,25},{... | collective-permute-start | bytes 208904 | tf_op jit(solution)/shard_map/ppermute | solution.py:58
  11.5 0.0 collective-permute-start.5
  11.5 0.0 collective-permute-done.refs_2_
  11.5 0.7 %collective-permute-start.6 = (f32[8,2176]{1,0:T(8,128)S(1)}, f32[8,2176]{1,0:T(8,128)S(1)}, u32[]{:S(2)}, u32[]{:S(2)}) collective-permute-start(f32[8,2176]{1,0:T(8,128)S(1)} %join.1.refs_5_.refs_4_), channel_id=1, source_target_pairs={{0,16},{4,20},{8,24},{12,28},{16,0},{20,4},{24,8},{28,12},{1,17},{... | collective-permute-start | bytes 208904 | tf_op jit(solution)/shard_map/ppermute | solution.py:58
  12.1 0.1 pad_add_fusion.refs_0_.me_ref
  12.2 0.0 collective-permute-done.1.refs_3_
  12.2 0.0 collective-permute-done.2.refs_4_
  12.2 0.0 copy-done.9
  12.2 2.4 %pairs_0_1.1 = (s32[211,128]{1,0:T(8,128)S(1)}, bf16[33,32,256]{2,1,0:T(8,128)(2,1)S(1)}, f32[33,8,256]{2,1,0:T(8,128)S(1)}, f32[33,8,256]{2,1,0:T(8,128)S(1)}, f32[2,4,512]{2,1,0:T(4,128)S(1)}) custom-call(s32[4]{0:T(128)S(1)} %pad_add_fusion.refs_0_.me_ref, f32[4,2048]{1,0:T(4,128)S(1)} %copy-done.9, f32[4,2048]{1,0:T(4,128)S(1)} %collective-permute-done.refs_2_, ...), custom_call_target="tpu_custom_call" | custom-call | flops 400000000 | bytes 1048576 | tf_op jit(solution)/shard_map/pairs_0_1/pallas_call | solution.py:447
  14.7 0.0 collective-permute-done.4.refs_4_.refs_7_
  14.7 1.6 %pairs_3_4.1 = (f32[33,8,256]{2,1,0:T(8,128)S(1)}, f32[2,4,512]{2,1,0:T(4,128)S(1)}) custom-call(s32[211,128]{1,0:T(8,128)S(1)} %get-tuple-element.28.refs_0_, bf16[33,32,256]{2,1,0:T(8,128)(2,1)S(1)} %get-tuple-element.29.refs_1_, f32[33,8,256]{2,1,0:T(8,128)S(1)} %get-tuple-element.30.refs_2_, f32[33,8,256]{2,1,0:T(8,128)S(1)} %get-tuple-element.31.refs_3_, ...), custom_call_target="tpu_custom_call" | custom-call | bytes 1048576 | tf_op jit(solution)/shard_map/pairs_3_4/pallas_call | solution.py:447
  16.3 0.4 %collective-permute-done.5.refs_4_.refs_5_ = f32[8,2176]{1,0:T(8,128)S(1)} collective-permute-done((f32[8,2176]{1,0:T(8,128)S(1)}, f32[8,2176]{1,0:T(8,128)S(1)}, u32[]{:S(2)}, u32[]{:S(2)}) %collective-permute-start.5) | collective-permute-done | bytes 69664 | tf_op jit(solution)/shard_map/ppermute | solution.py:58
  16.7 0.7 %collective-permute-done.6.refs_5_.refs_6_ = f32[8,2176]{1,0:T(8,128)S(1)} collective-permute-done((f32[8,2176]{1,0:T(8,128)S(1)}, f32[8,2176]{1,0:T(8,128)S(1)}, u32[]{:S(2)}, u32[]{:S(2)}) %collective-permute-start.6) | collective-permute-done | bytes 69664 | tf_op jit(solution)/shard_map/ppermute | solution.py:58
  17.4 2.8 %pairs_1_3.1 = (f32[4,2048]{1,0:T(4,128)S(1)}, f32[4,2048]{1,0:T(4,128)S(1)}, f32[4,2048]{1,0:T(4,128)S(1)}, f32[4,2048]{1,0:T(4,128)S(1)}, f32[2,4,512]{2,1,0:T...) custom-call(s32[211,128]{1,0:T(8,128)S(1)} %get-tuple-element.28.refs_0_, ...), custom_call_target="tpu_custom_call" | custom-call | bytes 1048576 | tf_op jit(solution)/shard_map/pairs_1_3/pallas_call | solution.py:447
  20.3 2.6 %collective-permute-start.12 = (f32[2,4,512]{2,1,0:T(4,128)S(1)}, f32[2,4,512]{2,1,0:T(4,128)S(1)}, u32[]{:S(2)}, u32[]{:S(2)}) collective-permute-start(f32[2,4,512]{2,1,0:T(4,128)S(1)} %get-tuple-element.45), channel_id=1, source_target_pairs={{0,24},{4,28},{8,16},{12,20},{16,8},{20,12},{24,0},{28,4},{1,25},{... | collective-permute-start | bytes 49160 | tf_op jit(solution)/shard_map/ppermute | solution.py:58
  22.9 0.2 collective-permute-start.11
  23.1 1.6 %collective-permute-start.10 = (f32[2,4,512]{2,1,0:T(4,128)S(1)}, f32[2,4,512]{2,1,0:T(4,128)S(1)}, u32[]{:S(2)}, u32[]{:S(2)}) collective-permute-start(f32[2,4,512]{2,1,0:T(4,128)S(1)} %get-tuple-element.43), channel_id=1, source_target_pairs={{0,8},{4,12},{8,0},{12,4},{16,24},{20,28},{24,16},{28,20},{1,9},{5... | collective-permute-start | bytes 49160 | tf_op jit(solution)/shard_map/ppermute | solution.py:58
  24.7 0.0 collective-permute-start.7
  24.7 1.5 %collective-permute-start.8 = (f32[4,2048]{1,0:T(4,128)S(1)}, f32[4,2048]{1,0:T(4,128)S(1)}, u32[]{:S(2)}, u32[]{:S(2)}) collective-permute-start(f32[4,2048]{1,0:T(4,128)S(1)} %get-tuple-element.36), channel_id=1, source_target_pairs={{0,2},{1,3},{2,0},{3,1},{4,6},{5,7},{6,4},{7,5},{8,10},{9,11},{10,... | collective-permute-start | bytes 98312 | tf_op jit(solution)/shard_map/ppermute | solution.py:52
  26.3 0.0 collective-permute-done.12.refs_0_
  26.3 0.3 %collective-permute-start.9 = (f32[4,2048]{1,0:T(4,128)S(1)}, f32[4,2048]{1,0:T(4,128)S(1)}, u32[]{:S(2)}, u32[]{:S(2)}) collective-permute-start(f32[4,2048]{1,0:T(4,128)S(1)} %get-tuple-element.37), channel_id=1, source_target_pairs={{0,3},{1,2},{2,1},{3,0},{4,7},{5,6},{6,5},{7,4},{8,11},{9,10},{10,... | collective-permute-start | bytes 98312 | tf_op jit(solution)/shard_map/ppermute | solution.py:52
  26.6 0.9 %collective-permute-done.11.refs_0_ = f32[2,4,512]{2,1,0:T(4,128)S(1)} collective-permute-done((f32[2,4,512]{2,1,0:T(4,128)S(1)}, f32[2,4,512]{2,1,0:T(4,128)S(1)}, u32[]{:S(2)}, u32[]{:S(2)}) %collective-permute-start.11) | collective-permute-done | bytes 16416 | tf_op jit(solution)/shard_map/ppermute | solution.py:58
  27.5 0.0 collective-permute-done.10.refs_1_
  27.5 0.0 copy-start
  27.6 0.0 copy-start.3
  27.6 0.0 copy-start.4
  27.6 0.0 copy-start.7
  27.6 0.0 copy-start.8
  27.6 1.7 %collective-permute-start.13 = (f32[4,4,512]{2,1,0:T(4,128)S(1)}, f32[4,4,512]{2,1,0:T(4,128)S(1)}, u32[]{:S(2)}, u32[]{:S(2)}) collective-permute-start(f32[4,4,512]{2,1,0:T(4,128)S(1)} %pick.1), channel_id=1, source_target_pairs={{0,4},{4,0},{8,12},{12,8},{16,20},{20,16},{24,28},{28,24},{1,5},{5... | collective-permute-start | bytes 98312 | tf_op jit(solution)/shard_map/ppermute | solution.py:64
  29.3 0.0 collective-permute-done.7.refs_1_
  29.3 0.0 collective-permute-done.8.refs_2_
  29.3 0.3 collective-permute-done.9.refs_3_
  29.6 0.0 copy-done
  29.6 0.0 copy-done.3
  29.6 0.0 copy-done.4
  29.6 0.0 copy-done.7
  29.6 0.0 copy-done.8
  29.6 0.0 copy-start.1
  29.6 0.0 copy-start.5
  29.7 0.0 copy-start.6
  29.7 1.2 %finish_src.1 = (f32[3,2048]{1,0:T(4,128)}, f32[1,2048]{1,0:T(1,128)}, f32[16,4,256]{2,1,0:T(4,128)S(1)}, f32[1,2048]{1,0:T(1,128)S(1)}) custom-call(s32[4]{0:T(128)S(1)} %pad_add_fusion.refs_0_.me_ref, s32[8]{0:T(128)S(1)} %copy-done.7, s32[8]{0:T(128)S(1)} %copy-done.8, f32[3,2048]{1,0:T(4,128)S(1)} %copy-done, f32[1,2048]{1,0:T(1,128)S(1)} %bitcast.13, ...), custom_call_target="tpu_custom_call" | custom-call | tf_op jit(solution)/shard_map/finish_src/pallas_call | solution.py:488
  30.9 0.7 %collective-permute-done.13.refs_4_ = f32[4,4,512]{2,1,0:T(4,128)S(1)} collective-permute-done((f32[4,4,512]{2,1,0:T(4,128)S(1)}, f32[4,4,512]{2,1,0:T(4,128)S(1)}, u32[]{:S(2)}, u32[]{:S(2)}) %collective-permute-start.13) | collective-permute-done | bytes 32800 | tf_op jit(solution)/shard_map/ppermute | solution.py:64
  31.6 0.0 copy-done.1
  31.6 0.0 copy-done.5
  31.6 0.0 copy-done.6
  31.6 0.7 %finish_tgt.1 = (f32[3,2048]{1,0:T(4,128)}, f32[1,2048]{1,0:T(1,128)}) custom-call(f32[3,2048]{1,0:T(4,128)S(1)} %copy-done.1, f32[1,2048]{1,0:T(1,128)S(1)} %bitcast.17, f32[1,2048]{1,0:T(1,128)S(1)} %bitcast.19, f32[1,2048]{1,0:T(1,128)S(1)} %get-tuple-element.40.live_ref, f32[16,4,256]{2,1,0:T(4,128)S(1)} %get-tuple-element.41.ids_ref, ...), custom_call_target="tpu_custom_call" | custom-call | tf_op jit(solution)/shard_map/finish_tgt/pallas_call | solution.py:501
  (4 shorter events, 0.0 us)
Async XLA Ops:
  2.2 5.5 %copy-start.2 = (f32[4,2176]{1,0:T(4,128)S(1)}, f32[4,2176]{1,0:T(4,128)}, u32[]{:S(2)}) copy-start(f32[4,2176]{1,0:T(4,128)} %get-tuple-element.27.refs_0_) | copy-start | bytes 104452
  2.2 5.5 %collective-permute-start.3 = (f32[4,2176]{1,0:T(4,128)}, f32[4,2176]{1,0:T(4,128)S(1)}, u32[]{:S(2)}, u32[]{:S(2)}) collective-permute-start(f32[4,2176]{1,0:T(4,128)} %get-tuple-element.27.refs_0_), channel_id=1, source_target_pairs={{0,4},{4,0},{8,12},{12,8},{16,20},{20,16},{24,28},{28,24},{1,5},{5... | collective-permute-start | bytes 104456 | tf_op jit(solution)/shard_map/ppermute | solution.py:64
  5.1 6.3 %collective-permute-start = (f32[4,2048]{1,0:T(4,128)}, f32[4,2048]{1,0:T(4,128)S(1)}, u32[]{:S(2)}, u32[]{:S(2)}) collective-permute-start(f32[4,2048]{1,0:T(4,128)} %get-tuple-element.26.refs_1_), channel_id=1, source_target_pairs={{0,1},{1,0},{2,3},{3,2},{4,5},{5,4},{6,7},{7,6},{8,9},{9,8},{10,11... | collective-permute-start | bytes 98312 | tf_op jit(solution)/shard_map/ppermute | solution.py:52
  5.1 7.1 %collective-permute-start.1 = (f32[4,2048]{1,0:T(4,128)}, f32[4,2048]{1,0:T(4,128)S(1)}, u32[]{:S(2)}, u32[]{:S(2)}) collective-permute-start(f32[4,2048]{1,0:T(4,128)} %get-tuple-element.26.refs_1_), channel_id=1, source_target_pairs={{0,2},{1,3},{2,0},{3,1},{4,6},{5,7},{6,4},{7,5},{8,10},{9,11},{10,... | collective-permute-start | bytes 98312 | tf_op jit(solution)/shard_map/ppermute | solution.py:52
  6.6 5.6 %collective-permute-start.2 = (f32[4,2048]{1,0:T(4,128)}, f32[4,2048]{1,0:T(4,128)S(1)}, u32[]{:S(2)}, u32[]{:S(2)}) collective-permute-start(f32[4,2048]{1,0:T(4,128)} %get-tuple-element.26.refs_1_), channel_id=1, source_target_pairs={{0,3},{1,2},{2,1},{3,0},{4,7},{5,6},{6,5},{7,4},{8,11},{9,10},{10,... | collective-permute-start | bytes 98312 | tf_op jit(solution)/shard_map/ppermute | solution.py:52
  7.6 4.6 %copy-start.9 = (f32[4,2048]{1,0:T(4,128)S(1)}, f32[4,2048]{1,0:T(4,128)}, u32[]{:S(2)}) copy-start(f32[4,2048]{1,0:T(4,128)} %get-tuple-element.26.refs_1_) | copy-start | bytes 98308
  7.7 7.0 %collective-permute-start.4 = (f32[8,2176]{1,0:T(8,128)S(1)}, f32[8,2176]{1,0:T(8,128)S(1)}, u32[]{:S(2)}, u32[]{:S(2)}) collective-permute-start(f32[8,2176]{1,0:T(8,128)S(1)} %join.1.refs_5_.refs_4_), channel_id=1, source_target_pairs={{0,24},{4,28},{8,16},{12,20},{16,8},{20,12},{24,0},{28,4},{1,25},{... | collective-permute-start | bytes 208904 | tf_op jit(solution)/shard_map/ppermute | solution.py:58
  11.5 5.2 %collective-permute-start.5 = (f32[8,2176]{1,0:T(8,128)S(1)}, f32[8,2176]{1,0:T(8,128)S(1)}, u32[]{:S(2)}, u32[]{:S(2)}) collective-permute-start(f32[8,2176]{1,0:T(8,128)S(1)} %join.1.refs_5_.refs_4_), channel_id=1, source_target_pairs={{0,8},{4,12},{8,0},{12,4},{16,24},{20,28},{24,16},{28,20},{1,9},{5... | collective-permute-start | bytes 208904 | tf_op jit(solution)/shard_map/ppermute | solution.py:58
  11.5 6.0 %collective-permute-start.6 = (f32[8,2176]{1,0:T(8,128)S(1)}, f32[8,2176]{1,0:T(8,128)S(1)}, u32[]{:S(2)}, u32[]{:S(2)}) collective-permute-start(f32[8,2176]{1,0:T(8,128)S(1)} %join.1.refs_5_.refs_4_), channel_id=1, source_target_pairs={{0,16},{4,20},{8,24},{12,28},{16,0},{20,4},{24,8},{28,12},{1,17},{... | collective-permute-start | bytes 208904 | tf_op jit(solution)/shard_map/ppermute | solution.py:58
  20.3 6.0 %collective-permute-start.12 = (f32[2,4,512]{2,1,0:T(4,128)S(1)}, f32[2,4,512]{2,1,0:T(4,128)S(1)}, u32[]{:S(2)}, u32[]{:S(2)}) collective-permute-start(f32[2,4,512]{2,1,0:T(4,128)S(1)} %get-tuple-element.45), channel_id=1, source_target_pairs={{0,24},{4,28},{8,16},{12,20},{16,8},{20,12},{24,0},{28,4},{1,25},{... | collective-permute-start | bytes 49160 | tf_op jit(solution)/shard_map/ppermute | solution.py:58
  22.9 4.6 %collective-permute-start.11 = (f32[2,4,512]{2,1,0:T(4,128)S(1)}, f32[2,4,512]{2,1,0:T(4,128)S(1)}, u32[]{:S(2)}, u32[]{:S(2)}) collective-permute-start(f32[2,4,512]{2,1,0:T(4,128)S(1)} %get-tuple-element.44), channel_id=1, source_target_pairs={{0,16},{4,20},{8,24},{12,28},{16,0},{20,4},{24,8},{28,12},{1,17},{... | collective-permute-start | bytes 49160 | tf_op jit(solution)/shard_map/ppermute | solution.py:58
  23.1 4.4 %collective-permute-start.10 = (f32[2,4,512]{2,1,0:T(4,128)S(1)}, f32[2,4,512]{2,1,0:T(4,128)S(1)}, u32[]{:S(2)}, u32[]{:S(2)}) collective-permute-start(f32[2,4,512]{2,1,0:T(4,128)S(1)} %get-tuple-element.43), channel_id=1, source_target_pairs={{0,8},{4,12},{8,0},{12,4},{16,24},{20,28},{24,16},{28,20},{1,9},{5... | collective-permute-start | bytes 49160 | tf_op jit(solution)/shard_map/ppermute | solution.py:58
  24.7 4.6 %collective-permute-start.7 = (f32[4,2048]{1,0:T(4,128)S(1)}, f32[4,2048]{1,0:T(4,128)S(1)}, u32[]{:S(2)}, u32[]{:S(2)}) collective-permute-start(f32[4,2048]{1,0:T(4,128)S(1)} %get-tuple-element.35), channel_id=1, source_target_pairs={{0,1},{1,0},{2,3},{3,2},{4,5},{5,4},{6,7},{7,6},{8,9},{9,8},{10,11... | collective-permute-start | bytes 98312 | tf_op jit(solution)/shard_map/ppermute | solution.py:52
  24.7 4.6 %collective-permute-start.8 = (f32[4,2048]{1,0:T(4,128)S(1)}, f32[4,2048]{1,0:T(4,128)S(1)}, u32[]{:S(2)}, u32[]{:S(2)}) collective-permute-start(f32[4,2048]{1,0:T(4,128)S(1)} %get-tuple-element.36), channel_id=1, source_target_pairs={{0,2},{1,3},{2,0},{3,1},{4,6},{5,7},{6,4},{7,5},{8,10},{9,11},{10,... | collective-permute-start | bytes 98312 | tf_op jit(solution)/shard_map/ppermute | solution.py:52
  26.3 3.3 %collective-permute-start.9 = (f32[4,2048]{1,0:T(4,128)S(1)}, f32[4,2048]{1,0:T(4,128)S(1)}, u32[]{:S(2)}, u32[]{:S(2)}) collective-permute-start(f32[4,2048]{1,0:T(4,128)S(1)} %get-tuple-element.37), channel_id=1, source_target_pairs={{0,3},{1,2},{2,1},{3,0},{4,7},{5,6},{6,5},{7,4},{8,11},{9,10},{10,... | collective-permute-start | bytes 98312 | tf_op jit(solution)/shard_map/ppermute | solution.py:52
  27.5 2.1 %copy-start = (f32[3,2048]{1,0:T(4,128)S(1)}, f32[3,2048]{1,0:T(4,128)}, u32[]{:S(2)}) copy-start(f32[3,2048]{1,0:T(4,128)} %pos_ref.2) | copy-start | bytes 73732
  27.6 2.1 %copy-start.3 = (f32[2048]{0:T(1024)S(1)}, f32[2048]{0:T(1024)}, u32[]{:S(2)}) copy-start(f32[2048]{0:T(1024)} %param.13) | copy-start | bytes 24580
  27.6 2.0 %copy-start.4 = (f32[2048]{0:T(1024)S(1)}, f32[2048]{0:T(1024)}, u32[]{:S(2)}) copy-start(f32[2048]{0:T(1024)} %param.14) | copy-start | bytes 24580
  27.6 2.0 %copy-start.7 = (s32[8]{0:T(128)S(1)}, s32[8]{0:T(128)}, u32[]{:S(2)}) copy-start(s32[8]{0:T(128)} %src_count_ref.1) | copy-start | bytes 100
  27.6 2.0 %copy-start.8 = (s32[8]{0:T(128)S(1)}, s32[8]{0:T(128)}, u32[]{:S(2)}) copy-start(s32[8]{0:T(128)} %tgt_count_ref.1) | copy-start | bytes 100
  27.6 4.0 %collective-permute-start.13 = (f32[4,4,512]{2,1,0:T(4,128)S(1)}, f32[4,4,512]{2,1,0:T(4,128)S(1)}, u32[]{:S(2)}, u32[]{:S(2)}) collective-permute-start(f32[4,4,512]{2,1,0:T(4,128)S(1)} %pick.1), channel_id=1, source_target_pairs={{0,4},{4,0},{8,12},{12,8},{16,20},{20,16},{24,28},{28,24},{1,5},{5... | collective-permute-start | bytes 98312 | tf_op jit(solution)/shard_map/ppermute | solution.py:64
  29.6 2.0 %copy-start.1 = (f32[3,2048]{1,0:T(4,128)S(1)}, f32[3,2048]{1,0:T(4,128)}, u32[]{:S(2)}) copy-start(f32[3,2048]{1,0:T(4,128)} %pos_ref.3) | copy-start | bytes 73732
  29.6 2.0 %copy-start.5 = (f32[2048]{0:T(1024)S(1)}, f32[2048]{0:T(1024)}, u32[]{:S(2)}) copy-start(f32[2048]{0:T(1024)} %param.17) | copy-start | bytes 24580
  29.7 1.9 %copy-start.6 = (f32[2048]{0:T(1024)S(1)}, f32[2048]{0:T(1024)}, u32[]{:S(2)}) copy-start(f32[2048]{0:T(1024)} %param.18) | copy-start | bytes 24580

commit v6 on v5

--- a/solution.py
+++ b/solution.py
@@ -12,6 +12,7 @@
 LANES = 128
 GROUP = 2
 BUFS = 4
+MIX = 2**10
 
 entropic = 0.05
 LOG2E = math.log2(math.e)
@@ -91,8 +92,7 @@
             ids = jnp.where(lane == r * per + m, req_ref[m, r].astype(jnp.float32), ids)
     tgt_ref[:, own:] = jnp.zeros((4,) + lane.shape[1:], jnp.float32)
     tgt_ref[0:1, own:] = ids
-    tgt_ref[1:2, own : own + ps_ref.shape[1]] = ps_ref[...].astype(jnp.float32)
-    tgt_ref[2:3, own : own + pq_ref.shape[1]] = pq_ref[...].astype(jnp.float32)
+    tgt_ref[1:2, own : own + ps_ref.shape[1]] = (ps_ref[...] * MIX + pq_ref[...]).astype(jnp.float32)
 
 
 def split3(x):
@@ -103,8 +103,9 @@
 
 
 def stages(outer):
-    cuts = [(0, 1), (outer - 1, outer), (1, outer - 1)]
-    return [(first, stop) for i, (first, stop) in enumerate(cuts) if first < stop and (i == 0 or first > 0)]
+    halves = [outer - 1] if outer > 2 else []
+    rest = [k for k in reversed(range(1, outer)) if k not in halves]
+    return [cut for cut in ([0], halves, rest) if cut]
 
 
 def dot(x, y):
@@ -170,23 +171,24 @@
 def pairs_kernel(n_tgt, n_clus, per_req, turn, *refs):
     outer, inner = split_axis(n_clus)
     cuts = stages(outer)
-    first, stop = cuts[turn]
+    mine = cuts[turn]
+    wide = inner * per_req
     begins, ends = turn == 0, turn == len(cuts) - 1
     slots = n_clus * per_req
     refs = list(refs)
     take = lambda n: [refs.pop(0) for _ in range(n)]
     if begins:
-        (far_me,) = take(1)
+        count_ref, _ = take(2)
         src_in = take(n_tgt)
     else:
         memo, left, src_rows, src_sums = take(4)
-    tgt_in = take(stop - first)
-    held = [k for cut in cuts[1:turn] for k in range(*cut)] if ends else []
+    tgt_in = take(len(mine))
+    held = [k for cut in cuts[1:turn] for k in cut] if ends else []
     held_in = take(len(held))
     if begins and not ends:
         memo, left, src_rows = take(3)
     src_out = take(n_tgt if ends else 1)
-    tgt_out = take(stop - first)
+    tgt_out = take(len(mine))
     for far, near in zip(held_in, take(len(held))):
         near[...] = far[...]
     src_acc = take(1)[0] if ends else src_out[0]
@@ -194,9 +196,7 @@
         memo, left, src_rows = take(3)
     right, tgt_rows, tgt_acc, *refs = refs
     if begins:
-        (chosen_src, chosen_slot, sem, me_ref, head), kern_bufs = refs[:5], refs[5:]
-        copy = pltpu.make_async_copy(far_me, me_ref, sem)
-        copy.start()
+        (chosen_src, chosen_slot, head), kern_bufs = refs[:3], refs[3:]
         head[...] = tgt_in[0][0:4, tgt_in[0].shape[1] - head.shape[1] :].astype(jnp.int32)
     else:
         kern_bufs = refs
@@ -209,40 +209,43 @@
         src_acc[...] = src_sums[...]
     tgt_acc[...] = jnp.zeros_like(tgt_acc)
 
-    pairs = (memo.shape[0] - len(cuts) - slots) // (2 * len(cuts))
-    tops = [len(cuts) + slots + 2 * pairs * i for i in range(len(cuts))]
+    pairs = (memo.shape[0] - len(cuts) - slots) // len(cuts)
+    tops = [len(cuts) + slots + pairs * i for i in range(len(cuts))]
 
     def note(row, value):
         memo[pl.ds(row, 1), :] = jnp.full((1, LANES), value, jnp.int32)
 
     if begins:
-        copy.wait()
-        tgt_me, outer_me, inner_me, count = (me_ref[i] for i in range(4))
+        count, tgt_me, clus_me = count_ref[0], lax.axis_index("tgt"), lax.axis_index("clus")
+        outer_me = divide(clus_me, inner)
+        inner_me = clus_me - outer_me * inner
         for slot in range(slots):
             note(len(cuts) + local_slot(slot, outer_me, inner_me, outer, inner, per_req), head[0, slot])
         totals = [jnp.int32(0)] * len(cuts)
         for pair in range(pairs):
-            s = local_block(head[1, pair], tgt_me, n_tgt, per_dev)
-            slot = local_slot(head[2, pair], outer_me, inner_me, outer, inner, per_req)
-            for i, (low, high) in enumerate(cuts):
-                inside = slot - low * inner * per_req
+            both = head[1, pair]
+            s = local_block(divide(both, MIX), tgt_me, n_tgt, per_dev)
+            slot = local_slot(both & (MIX - 1), outer_me, inner_me, outer, inner, per_req)
+            k = divide(slot, wide)
+            for i, cut in enumerate(cuts):
                 if i == 0:
                     chosen_src[totals[0]] = s
-                    chosen_slot[totals[0]] = inside
+                    chosen_slot[totals[0]] = slot
                 else:
-                    note(tops[i] + totals[i], s)
-                    note(tops[i] + pairs + totals[i], inside)
-                hit = (pair < count) & (inside >= 0) & (inside < (high - low) * inner * per_req)
-                totals[i] = totals[i] + hit.astype(jnp.int32)
+                    note(tops[i] + totals[i], s * MIX + slot)
+                held_here = sum((k == far).astype(jnp.int32) for far in cut)
+                totals[i] = totals[i] + jnp.where(pair < count, held_here, 0)
         for i in range(1, len(cuts)):
             note(i, totals[i])
         total = totals[0]
     else:
         total = memo[turn, 0]
-    for slot in range((stop - first) * inner * per_req):
-        i = slot // per_req % inner
-        block = memo[len(cuts) + first * inner * per_req + slot, 0]
-        prepare_tgt(slot, block, slice(4 * i, 4 * i + 4), tgt_in[slot // (inner * per_req)], right, tgt_rows)
+    for place, k in enumerate(mine):
+        for i in range(inner):
+            for m in range(per_req):
+                slot = k * wide + i * per_req + m
+                block = memo[len(cuts) + slot, 0]
+                prepare_tgt(slot, block, slice(4 * i, 4 * i + 4), tgt_in[place], right, tgt_rows)
 
     def pair_ids(entry):
         inside = jnp.minimum(entry, pairs - 1)
@@ -250,8 +253,9 @@
         if begins:
             s, q = chosen_src[inside], chosen_slot[inside]
         else:
-            s, q = memo[tops[turn] + inside, 0], memo[tops[turn] + pairs + inside, 0]
-        return jnp.where(live, s, n_src), jnp.where(live, q, 0)
+            both = memo[tops[turn] + inside, 0]
+            s, q = divide(both, MIX), both & (MIX - 1)
+        return jnp.where(live, s, n_src), jnp.where(live, q, mine[0] * wide)
 
     def weigh(entry, buf, g):
         s, q = pair_ids(entry)
@@ -285,10 +289,11 @@
 
     lax.fori_loop(0, divide(total + GROUP * bufs - 1, GROUP * bufs), body, 0)
 
-    for place in range((stop - first) * inner):
-        for m in range(per_req):
-            part = tgt_acc[place * per_req + m]
-            tgt_out[place // inner][place % inner, :, m * BLK : (m + 1) * BLK] = part[0:4] + part[4:8]
+    for place, k in enumerate(mine):
+        for i in range(inner):
+            for m in range(per_req):
+                part = tgt_acc[k * wide + i * per_req + m]
+                tgt_out[place][i, :, m * BLK : (m + 1) * BLK] = part[0:4] + part[4:8]
     if ends:
         for k in range(n_tgt):
             base = flip(k, n_tgt) * per_dev
@@ -413,48 +418,46 @@
         out_specs=VMEM,
         compiler_params=small,
     )(*near)
-    tgt_in = [near] + [moved_outer(near, "clus", k) for k in range(1, outer)]
+    tgt_in = {0: near, **{k: moved_outer(near, "clus", k) for cut in stages(outer)[1:] for k in cut}}
 
     block_rows = jax.ShapeDtypeStruct((n_src + 1, 8, BLK), f32)
     left_side = jax.ShapeDtypeStruct((n_src + 1, 32, BLK), jnp.bfloat16)
     n_pairs = pair_src.shape[0]
-    memo_rows = jax.ShapeDtypeStruct((len(stages(outer)) * (1 + 2 * n_pairs) + slots, LANES), jnp.int32)
+    memo_rows = jax.ShapeDtypeStruct((len(stages(outer)) * (1 + n_pairs) + slots, LANES), jnp.int32)
     list_scratch = (
         [pltpu.SMEM((n_pairs + 1,), jnp.int32)] * 2
-        + [pltpu.SemaphoreType.DMA, pltpu.SMEM(me.shape, jnp.int32)]
         + [pltpu.VMEM((4, width), jnp.int32)]
     )
     kern_bufs = [pltpu.VMEM((GROUP, 2, BLK, BLK), jnp.bfloat16)] * BUFS
     part_shape = jax.ShapeDtypeStruct((inner, 4, per_req * BLK), f32)
     state, sums = (), {}
-    for turn, (first, stop) in enumerate(stages(outer)):
+    for turn, mine in enumerate(stages(outer)):
         begins, ends = turn == 0, turn == len(stages(outer)) - 1
-        held = [k for cut in stages(outer)[1:turn] for k in range(*cut)] if ends else []
-        args = ([me] + src_in if begins else list(state)) + tgt_in[first:stop] + [sums[k] for k in held]
+        held = [k for cut in stages(outer)[1:turn] for k in cut] if ends else []
+        args = ([pair_count, me] + src_in if begins else list(state)) + [tgt_in[k] for k in mine] + [sums[k] for k in held]
         outs = [memo_rows, left_side, block_rows] if begins and not ends else []
         outs += [jax.ShapeDtypeStruct((4, ns), f32)] * n_tgt if ends else [block_rows]
-        outs += [part_shape] * (stop - first + len(held))
+        outs += [part_shape] * (len(mine) + len(held))
         extra = [pltpu.VMEM(block_rows.shape, f32)] if ends else []
         if begins and ends:
             extra += [pltpu.VMEM(memo_rows.shape, jnp.int32)]
             extra += [pltpu.VMEM(left_side.shape, jnp.bfloat16), pltpu.VMEM(block_rows.shape, f32)]
-        near = (stop - first) * inner * per_req
         extra += [
-            pltpu.VMEM((near, BLK, 32), jnp.bfloat16),
-            pltpu.VMEM((near, 8, BLK), f32),
-            pltpu.VMEM((near, 8, BLK), f32),
+            pltpu.VMEM((slots, BLK, 32), jnp.bfloat16),
+            pltpu.VMEM((slots, 8, BLK), f32),
+            pltpu.VMEM((slots, 8, BLK), f32),
         ]
         res = pl.pallas_call(
             functools.partial(pairs_kernel, n_tgt, n_clus, per_req, turn),
-            name=f"pairs_{first}_{stop}",
+            name=f"pairs_{turn}",
             out_shape=outs,
-            in_specs=[ANY if begins and a is me else VMEM for a in args],
+            in_specs=[SMEM if a is pair_count else ANY if a is me else VMEM for a in args],
             out_specs=[VMEM] * len(outs),
             scratch_shapes=extra + (list_scratch if begins else []) + kern_bufs,
             compiler_params=small,
             cost_estimate=pl.CostEstimate(flops=4*10**8 if begins else 0, bytes_accessed=2**20, transcendentals=0),
         )(*args)
-        made = list(range(first, stop)) + held
+        made = list(mine) + held
         sums.update(zip(made, res[len(res) - len(made) :]))
         if ends:
             src_out = res[:n_tgt]
@@ -497,7 +500,7 @@
         in_specs=[SMEM] * 3 + [VMEM] * (3 + n_tgt + outer),
         out_specs=(VMEM,) * 4,
         compiler_params=small,
-    )(me, src_count, tgt_count, *src_side, *src_parts, *tgt_in)
+    )(me, src_count, tgt_count, *src_side, *src_parts, *(tgt_in[k] for k in range(outer)))
     grad_tgt_pos, grad_tgt_weight = pl.pallas_call(
         functools.partial(tgt_kernel, outer, inner),
         name="finish_tgt",

time: 32.5 us -> 32.4 us (level)
  waiting for transfers between devices: 3.13 us -> 4.24 us
  starting transfers between devices: 17.3 us -> 16.8 us
  Pallas kernels: 10.3 us -> 9.82 us
    ppermute x6, waiting for transfers between devices: 2.11 us -> 2.77 us  [moved_outer(): return lax.ppermute(x, axis, pairs)]
    ppermute x6, waiting for transfers between devices: 0.29 us -> 0.82 us  [moved(): return lax.ppermute(x, axis, [(i, step(i, k, n)) for i in range(n)])]
    pallas_call x3, Pallas kernels: 6.84 us -> 6.34 us  [shards(): pl.pallas_call(functools.partial(pairs_kernel, n_tgt, n_clus, per_req, tu...]
    ppermute x2, starting transfers between devices: 4.64 us -> 4.18 us  [moved_inner(): return lax.ppermute(x, axis, pairs)]
  transfers between devices with their start and end apart: 14 -> 14, of which waited for: 5 -> 5; matrix products, arithmetic and copies ran while one was open for 0% -> 0% of each run, Pallas kernels for 16% -> 15%
where the time goes in v6:
time: 32.4 us; the launch traced here: 32.5 us
  starting transfers between devices  16.8 us (52%)
  Pallas kernels  9.82 us (30%)
  waiting for transfers between devices  4.24 us (13%)
  between operations  1.45 us (4%)
    ppermute x6, starting transfers between devices, moved_outer(): return lax.ppermute(x, axis, pairs)  8.91 us
    pallas_call x3, Pallas kernels, shards(): pl.pallas_call(functools.partial(pairs_kernel, n_tgt, n_clus, per_req, tu...  6.34 us
    ppermute x2, starting transfers between devices, moved_inner(): return lax.ppermute(x, axis, pairs)  4.18 us
    ppermute x6, starting transfers between devices, moved(): return lax.ppermute(x, axis, [(i, step(i, k, n)) for i in range(n)])  3.72 us
    ppermute x6, waiting for transfers between devices, moved_outer(): return lax.ppermute(x, axis, pairs)  2.77 us
    pallas_call x1, Pallas kernels, shards(): pl.pallas_call(pack_kernel, name='pack', out_shape=(jax.ShapeDtypeStruct(...  1.55 us
    pallas_call x1, Pallas kernels, shards(): pl.pallas_call(functools.partial(src_kernel, n_tgt, per_req), name='finis...  1.21 us
    ppermute x6, waiting for transfers between devices, moved(): return lax.ppermute(x, axis, [(i, step(i, k, n)) for i in range(n)])  0.82 us
  transfers between devices with their start and end apart: 14, of which 5 were waited for; matrix products, arithmetic and copies ran while one was open for 0% of the time, Pallas kernels for 15%

profile of v6, /device:TPU:0, one launch (start us, length us, event | category | flops | bytes accessed | tf_op | source)
XLA Modules:
  0.0 32.5 jit_solution(12140190878596095717)
XLA Ops:
  0.6 1.5 %pack.1 = (f32[4,2048]{1,0:T(4,128)}, f32[4,2176]{1,0:T(4,128)}) custom-call(s32[2,8]{1,0:T(2,128)} %bitcast.20, s32[8]{0:T(128)} %src_count_ref.1, s32[8]{0:T(128)} %tgt_count_ref.1, s32[1,32]{1,0:T(1,128)} %bitcast.21, s32[1,32]{1,0:T(1,128)} %bitcast.22, f32[3,2048]{1,0:T(4,128)} %pos_ref.2, f32[1,2048]{1,0:T(1,128)} %bitcast.12, f32[1,2048]{1,0:T(1,128)} %bitcast.14, ...), custom_call_target="tpu_custom_call" | custom-call | tf_op jit(solution)/shard_map/pack/pallas_call | solution.py:402
  2.2 0.0 copy-start.2
  2.2 2.9 %collective-permute-start.3 = (f32[4,2176]{1,0:T(4,128)}, f32[4,2176]{1,0:T(4,128)S(1)}, u32[]{:S(2)}, u32[]{:S(2)}) collective-permute-start(f32[4,2176]{1,0:T(4,128)} %get-tuple-element.27.refs_0_), channel_id=1, source_target_pairs={{0,4},{4,0},{8,12},{12,8},{16,20},{20,16},{24,28},{28,24},{1,5},{5... | collective-permute-start | bytes 104456 | tf_op jit(solution)/shard_map/ppermute | solution.py:65
  5.1 0.0 collective-permute-start
  5.1 1.5 %collective-permute-start.1 = (f32[4,2048]{1,0:T(4,128)}, f32[4,2048]{1,0:T(4,128)S(1)}, u32[]{:S(2)}, u32[]{:S(2)}) collective-permute-start(f32[4,2048]{1,0:T(4,128)} %get-tuple-element.26.refs_2_), channel_id=1, source_target_pairs={{0,2},{1,3},{2,0},{3,1},{4,6},{5,7},{6,4},{7,5},{8,10},{9,11},{10,... | collective-permute-start | bytes 98312 | tf_op jit(solution)/shard_map/ppermute | solution.py:53
  6.6 0.3 %collective-permute-start.2 = (f32[4,2048]{1,0:T(4,128)}, f32[4,2048]{1,0:T(4,128)S(1)}, u32[]{:S(2)}, u32[]{:S(2)}) collective-permute-start(f32[4,2048]{1,0:T(4,128)} %get-tuple-element.26.refs_2_), channel_id=1, source_target_pairs={{0,3},{1,2},{2,1},{3,0},{4,7},{5,6},{6,5},{7,4},{8,11},{9,10},{10,... | collective-permute-start | bytes 98312 | tf_op jit(solution)/shard_map/ppermute | solution.py:53
  7.6 0.0 copy-start.9
  7.7 0.0 collective-permute-done.3.refs_1_
  7.7 0.0 copy-done.2
  7.7 3.8 %collective-permute-start.4 = (f32[8,2176]{1,0:T(8,128)S(1)}, f32[8,2176]{1,0:T(8,128)S(1)}, u32[]{:S(2)}, u32[]{:S(2)}) collective-permute-start(f32[8,2176]{1,0:T(8,128)S(1)} %join.1.refs_6_.refs_4_), channel_id=1, source_target_pairs={{0,24},{4,28},{8,16},{12,20},{16,8},{20,12},{24,0},{28,4},{1,25},{... | collective-permute-start | bytes 208904 | tf_op jit(solution)/shard_map/ppermute | solution.py:59
  11.5 0.0 collective-permute-start.5
  11.5 0.0 collective-permute-done.refs_3_
  11.5 0.7 %collective-permute-start.6 = (f32[8,2176]{1,0:T(8,128)S(1)}, f32[8,2176]{1,0:T(8,128)S(1)}, u32[]{:S(2)}, u32[]{:S(2)}) collective-permute-start(f32[8,2176]{1,0:T(8,128)S(1)} %join.1.refs_6_.refs_4_), channel_id=1, source_target_pairs={{0,8},{4,12},{8,0},{12,4},{16,24},{20,28},{24,16},{28,20},{1,9},{5... | collective-permute-start | bytes 208904 | tf_op jit(solution)/shard_map/ppermute | solution.py:59
  12.1 0.1 pad_add_fusion.refs_1_.me_ref
  12.2 0.0 collective-permute-done.1.refs_4_
  12.2 0.0 collective-permute-done.2.refs_5_
  12.2 0.0 copy-done.9
  12.2 1.9 %pairs_0.1 = (s32[115,128]{1,0:T(8,128)S(1)}, bf16[33,32,256]{2,1,0:T(8,128)(2,1)S(1)}, f32[33,8,256]{2,1,0:T(8,128)S(1)}, f32[33,8,256]{2,1,0:T(8,128)S(1)}, f32[2,4,512]{2,1,0:T(4,128)S(1)}) custom-call(s32[1]{0:T(128)S(6)} %copy.16.refs_0_, s32[4]{0:T(128)S(1)} %pad_add_fusion.refs_1_.me_ref, f32[4,2048]{1,0:T(4,128)S(1)} %copy-done.9, ...), custom_call_target="tpu_custom_call" | custom-call | flops 400000000 | bytes 1048576 | tf_op jit(solution)/shard_map/pairs_0/pallas_call | solution.py:450
  14.2 0.2 collective-permute-done.4.refs_4_.refs_7_
  14.3 1.6 %pairs_1.1 = (f32[33,8,256]{2,1,0:T(8,128)S(1)}, f32[2,4,512]{2,1,0:T(4,128)S(1)}) custom-call(s32[115,128]{1,0:T(8,128)S(1)} %get-tuple-element.28.refs_0_, bf16[33,32,256]{2,1,0:T(8,128)(2,1)S(1)} %get-tuple-element.29.refs_1_, f32[33,8,256]{2,1,0:T(8,128)S(1)} %get-tuple-element.30.refs_2_, f32[33,8,256]{2,1,0:T(8,128)S(1)} %get-tuple-element.31.refs_3_, ...), custom_call_target="tpu_custom_call" | custom-call | bytes 1048576 | tf_op jit(solution)/shard_map/pairs_1/pallas_call | solution.py:450
  15.9 1.7 %collective-permute-done.5.refs_4_.refs_6_ = f32[8,2176]{1,0:T(8,128)S(1)} collective-permute-done((f32[8,2176]{1,0:T(8,128)S(1)}, f32[8,2176]{1,0:T(8,128)S(1)}, u32[]{:S(2)}, u32[]{:S(2)}) %collective-permute-start.5) | collective-permute-done | bytes 69664 | tf_op jit(solution)/shard_map/ppermute | solution.py:59
  17.7 0.0 collective-permute-done.6.refs_5_
  17.7 2.8 %pairs_2.1 = (f32[4,2048]{1,0:T(4,128)S(1)}, f32[4,2048]{1,0:T(4,128)S(1)}, f32[4,2048]{1,0:T(4,128)S(1)}, f32[4,2048]{1,0:T(4,128)S(1)}, f32[2,4,512]{2,1,0:T(4...) custom-call(s32[115,128]{1,0:T(8,128)S(1)} %get-tuple-element.28.refs_0_, ...), custom_call_target="tpu_custom_call" | custom-call | bytes 1048576 | tf_op jit(solution)/shard_map/pairs_2/pallas_call | solution.py:450
  20.5 2.5 %collective-permute-start.12 = (f32[2,4,512]{2,1,0:T(4,128)S(1)}, f32[2,4,512]{2,1,0:T(4,128)S(1)}, u32[]{:S(2)}, u32[]{:S(2)}) collective-permute-start(f32[2,4,512]{2,1,0:T(4,128)S(1)} %get-tuple-element.45), channel_id=1, source_target_pairs={{0,24},{4,28},{8,16},{12,20},{16,8},{20,12},{24,0},{28,4},{1,25},{... | collective-permute-start | bytes 49160 | tf_op jit(solution)/shard_map/ppermute | solution.py:59
  23.0 0.2 collective-permute-start.11
  23.3 1.7 %collective-permute-start.10 = (f32[2,4,512]{2,1,0:T(4,128)S(1)}, f32[2,4,512]{2,1,0:T(4,128)S(1)}, u32[]{:S(2)}, u32[]{:S(2)}) collective-permute-start(f32[2,4,512]{2,1,0:T(4,128)S(1)} %get-tuple-element.43), channel_id=1, source_target_pairs={{0,8},{4,12},{8,0},{12,4},{16,24},{20,28},{24,16},{28,20},{1,9},{5... | collective-permute-start | bytes 49160 | tf_op jit(solution)/shard_map/ppermute | solution.py:59
  25.0 0.0 collective-permute-start.7
  25.0 1.5 %collective-permute-start.8 = (f32[4,2048]{1,0:T(4,128)S(1)}, f32[4,2048]{1,0:T(4,128)S(1)}, u32[]{:S(2)}, u32[]{:S(2)}) collective-permute-start(f32[4,2048]{1,0:T(4,128)S(1)} %get-tuple-element.36), channel_id=1, source_target_pairs={{0,2},{1,3},{2,0},{3,1},{4,6},{5,7},{6,4},{7,5},{8,10},{9,11},{10,... | collective-permute-start | bytes 98312 | tf_op jit(solution)/shard_map/ppermute | solution.py:53
  26.5 0.0 collective-permute-done.12.refs_0_
  26.5 0.3 %collective-permute-start.9 = (f32[4,2048]{1,0:T(4,128)S(1)}, f32[4,2048]{1,0:T(4,128)S(1)}, u32[]{:S(2)}, u32[]{:S(2)}) collective-permute-start(f32[4,2048]{1,0:T(4,128)S(1)} %get-tuple-element.37), channel_id=1, source_target_pairs={{0,3},{1,2},{2,1},{3,0},{4,7},{5,6},{6,5},{7,4},{8,11},{9,10},{10,... | collective-permute-start | bytes 98312 | tf_op jit(solution)/shard_map/ppermute | solution.py:53
  26.8 0.9 %collective-permute-done.11.refs_0_ = f32[2,4,512]{2,1,0:T(4,128)S(1)} collective-permute-done((f32[2,4,512]{2,1,0:T(4,128)S(1)}, f32[2,4,512]{2,1,0:T(4,128)S(1)}, u32[]{:S(2)}, u32[]{:S(2)}) %collective-permute-start.11) | collective-permute-done | bytes 16416 | tf_op jit(solution)/shard_map/ppermute | solution.py:59
  27.7 0.0 collective-permute-done.10.refs_1_
  27.7 0.0 copy-start
  27.7 0.0 copy-start.3
  27.7 0.0 copy-start.4
  27.7 0.0 copy-start.7
  27.7 0.0 copy-start.8
  27.8 1.2 %collective-permute-start.13 = (f32[4,4,512]{2,1,0:T(4,128)S(1)}, f32[4,4,512]{2,1,0:T(4,128)S(1)}, u32[]{:S(2)}, u32[]{:S(2)}) collective-permute-start(f32[4,4,512]{2,1,0:T(4,128)S(1)} %pick.1), channel_id=1, source_target_pairs={{0,4},{4,0},{8,12},{12,8},{16,20},{20,16},{24,28},{28,24},{1,5},{5... | collective-permute-start | bytes 98312 | tf_op jit(solution)/shard_map/ppermute | solution.py:65
  29.0 0.0 collective-permute-done.7.refs_1_
  29.0 0.0 collective-permute-done.8.refs_2_
  29.0 0.8 %collective-permute-done.9.refs_3_ = f32[4,2048]{1,0:T(4,128)S(1)} collective-permute-done((f32[4,2048]{1,0:T(4,128)S(1)}, f32[4,2048]{1,0:T(4,128)S(1)}, u32[]{:S(2)}, u32[]{:S(2)}) %collective-permute-start.9) | collective-permute-done | bytes 32800 | tf_op jit(solution)/shard_map/ppermute | solution.py:53
  29.8 0.0 copy-done
  29.8 0.0 copy-done.3
  29.8 0.0 copy-done.4
  29.8 0.0 copy-done.7
  29.8 0.0 copy-done.8
  29.8 0.0 copy-start.1
  29.9 0.0 copy-start.5
  29.9 0.0 copy-start.6
  29.9 1.2 %finish_src.1 = (f32[3,2048]{1,0:T(4,128)}, f32[1,2048]{1,0:T(1,128)}, f32[16,4,256]{2,1,0:T(4,128)S(1)}, f32[1,2048]{1,0:T(1,128)S(1)}) custom-call(s32[4]{0:T(128)S(1)} %pad_add_fusion.refs_1_.me_ref, s32[8]{0:T(128)S(1)} %copy-done.7, s32[8]{0:T(128)S(1)} %copy-done.8, f32[3,2048]{1,0:T(4,128)S(1)} %copy-done, f32[1,2048]{1,0:T(1,128)S(1)} %bitcast.13, ...), custom_call_target="tpu_custom_call" | custom-call | tf_op jit(solution)/shard_map/finish_src/pallas_call | solution.py:491
  31.1 0.6 %collective-permute-done.13.refs_4_ = f32[4,4,512]{2,1,0:T(4,128)S(1)} collective-permute-done((f32[4,4,512]{2,1,0:T(4,128)S(1)}, f32[4,4,512]{2,1,0:T(4,128)S(1)}, u32[]{:S(2)}, u32[]{:S(2)}) %collective-permute-start.13) | collective-permute-done | bytes 32800 | tf_op jit(solution)/shard_map/ppermute | solution.py:65
  31.7 0.0 copy-done.1
  31.7 0.0 copy-done.5
  31.7 0.0 copy-done.6
  31.7 0.7 %finish_tgt.1 = (f32[3,2048]{1,0:T(4,128)}, f32[1,2048]{1,0:T(1,128)}) custom-call(f32[3,2048]{1,0:T(4,128)S(1)} %copy-done.1, f32[1,2048]{1,0:T(1,128)S(1)} %bitcast.17, f32[1,2048]{1,0:T(1,128)S(1)} %bitcast.19, f32[1,2048]{1,0:T(1,128)S(1)} %get-tuple-element.40.live_ref, f32[16,4,256]{2,1,0:T(4,128)S(1)} %get-tuple-element.41.ids_ref, ...), custom_call_target="tpu_custom_call" | custom-call | tf_op jit(solution)/shard_map/finish_tgt/pallas_call | solution.py:504
  (4 shorter events, 0.0 us)
Async XLA Ops:
  2.2 5.5 %copy-start.2 = (f32[4,2176]{1,0:T(4,128)S(1)}, f32[4,2176]{1,0:T(4,128)}, u32[]{:S(2)}) copy-start(f32[4,2176]{1,0:T(4,128)} %get-tuple-element.27.refs_0_) | copy-start | bytes 104452
  2.2 5.5 %collective-permute-start.3 = (f32[4,2176]{1,0:T(4,128)}, f32[4,2176]{1,0:T(4,128)S(1)}, u32[]{:S(2)}, u32[]{:S(2)}) collective-permute-start(f32[4,2176]{1,0:T(4,128)} %get-tuple-element.27.refs_0_), channel_id=1, source_target_pairs={{0,4},{4,0},{8,12},{12,8},{16,20},{20,16},{24,28},{28,24},{1,5},{5... | collective-permute-start | bytes 104456 | tf_op jit(solution)/shard_map/ppermute | solution.py:65
  5.1 6.3 %collective-permute-start = (f32[4,2048]{1,0:T(4,128)}, f32[4,2048]{1,0:T(4,128)S(1)}, u32[]{:S(2)}, u32[]{:S(2)}) collective-permute-start(f32[4,2048]{1,0:T(4,128)} %get-tuple-element.26.refs_2_), channel_id=1, source_target_pairs={{0,1},{1,0},{2,3},{3,2},{4,5},{5,4},{6,7},{7,6},{8,9},{9,8},{10,11... | collective-permute-start | bytes 98312 | tf_op jit(solution)/shard_map/ppermute | solution.py:53
  5.1 7.1 %collective-permute-start.1 = (f32[4,2048]{1,0:T(4,128)}, f32[4,2048]{1,0:T(4,128)S(1)}, u32[]{:S(2)}, u32[]{:S(2)}) collective-permute-start(f32[4,2048]{1,0:T(4,128)} %get-tuple-element.26.refs_2_), channel_id=1, source_target_pairs={{0,2},{1,3},{2,0},{3,1},{4,6},{5,7},{6,4},{7,5},{8,10},{9,11},{10,... | collective-permute-start | bytes 98312 | tf_op jit(solution)/shard_map/ppermute | solution.py:53
  6.6 5.6 %collective-permute-start.2 = (f32[4,2048]{1,0:T(4,128)}, f32[4,2048]{1,0:T(4,128)S(1)}, u32[]{:S(2)}, u32[]{:S(2)}) collective-permute-start(f32[4,2048]{1,0:T(4,128)} %get-tuple-element.26.refs_2_), channel_id=1, source_target_pairs={{0,3},{1,2},{2,1},{3,0},{4,7},{5,6},{6,5},{7,4},{8,11},{9,10},{10,... | collective-permute-start | bytes 98312 | tf_op jit(solution)/shard_map/ppermute | solution.py:53
  7.6 4.6 %copy-start.9 = (f32[4,2048]{1,0:T(4,128)S(1)}, f32[4,2048]{1,0:T(4,128)}, u32[]{:S(2)}) copy-start(f32[4,2048]{1,0:T(4,128)} %get-tuple-element.26.refs_2_) | copy-start | bytes 98308
  7.7 6.6 %collective-permute-start.4 = (f32[8,2176]{1,0:T(8,128)S(1)}, f32[8,2176]{1,0:T(8,128)S(1)}, u32[]{:S(2)}, u32[]{:S(2)}) collective-permute-start(f32[8,2176]{1,0:T(8,128)S(1)} %join.1.refs_6_.refs_4_), channel_id=1, source_target_pairs={{0,24},{4,28},{8,16},{12,20},{16,8},{20,12},{24,0},{28,4},{1,25},{... | collective-permute-start | bytes 208904 | tf_op jit(solution)/shard_map/ppermute | solution.py:59
  11.5 6.2 %collective-permute-start.5 = (f32[8,2176]{1,0:T(8,128)S(1)}, f32[8,2176]{1,0:T(8,128)S(1)}, u32[]{:S(2)}, u32[]{:S(2)}) collective-permute-start(f32[8,2176]{1,0:T(8,128)S(1)} %join.1.refs_6_.refs_4_), channel_id=1, source_target_pairs={{0,16},{4,20},{8,24},{12,28},{16,0},{20,4},{24,8},{28,12},{1,17},{... | collective-permute-start | bytes 208904 | tf_op jit(solution)/shard_map/ppermute | solution.py:59
  11.5 6.2 %collective-permute-start.6 = (f32[8,2176]{1,0:T(8,128)S(1)}, f32[8,2176]{1,0:T(8,128)S(1)}, u32[]{:S(2)}, u32[]{:S(2)}) collective-permute-start(f32[8,2176]{1,0:T(8,128)S(1)} %join.1.refs_6_.refs_4_), channel_id=1, source_target_pairs={{0,8},{4,12},{8,0},{12,4},{16,24},{20,28},{24,16},{28,20},{1,9},{5... | collective-permute-start | bytes 208904 | tf_op jit(solution)/shard_map/ppermute | solution.py:59
  20.5 6.0 %collective-permute-start.12 = (f32[2,4,512]{2,1,0:T(4,128)S(1)}, f32[2,4,512]{2,1,0:T(4,128)S(1)}, u32[]{:S(2)}, u32[]{:S(2)}) collective-permute-start(f32[2,4,512]{2,1,0:T(4,128)S(1)} %get-tuple-element.45), channel_id=1, source_target_pairs={{0,24},{4,28},{8,16},{12,20},{16,8},{20,12},{24,0},{28,4},{1,25},{... | collective-permute-start | bytes 49160 | tf_op jit(solution)/shard_map/ppermute | solution.py:59
  23.0 4.6 %collective-permute-start.11 = (f32[2,4,512]{2,1,0:T(4,128)S(1)}, f32[2,4,512]{2,1,0:T(4,128)S(1)}, u32[]{:S(2)}, u32[]{:S(2)}) collective-permute-start(f32[2,4,512]{2,1,0:T(4,128)S(1)} %get-tuple-element.44), channel_id=1, source_target_pairs={{0,16},{4,20},{8,24},{12,28},{16,0},{20,4},{24,8},{28,12},{1,17},{... | collective-permute-start | bytes 49160 | tf_op jit(solution)/shard_map/ppermute | solution.py:59
  23.3 4.4 %collective-permute-start.10 = (f32[2,4,512]{2,1,0:T(4,128)S(1)}, f32[2,4,512]{2,1,0:T(4,128)S(1)}, u32[]{:S(2)}, u32[]{:S(2)}) collective-permute-start(f32[2,4,512]{2,1,0:T(4,128)S(1)} %get-tuple-element.43), channel_id=1, source_target_pairs={{0,8},{4,12},{8,0},{12,4},{16,24},{20,28},{24,16},{28,20},{1,9},{5... | collective-permute-start | bytes 49160 | tf_op jit(solution)/shard_map/ppermute | solution.py:59
  25.0 4.1 %collective-permute-start.7 = (f32[4,2048]{1,0:T(4,128)S(1)}, f32[4,2048]{1,0:T(4,128)S(1)}, u32[]{:S(2)}, u32[]{:S(2)}) collective-permute-start(f32[4,2048]{1,0:T(4,128)S(1)} %get-tuple-element.35), channel_id=1, source_target_pairs={{0,1},{1,0},{2,3},{3,2},{4,5},{5,4},{6,7},{7,6},{8,9},{9,8},{10,11... | collective-permute-start | bytes 98312 | tf_op jit(solution)/shard_map/ppermute | solution.py:53
  25.0 4.1 %collective-permute-start.8 = (f32[4,2048]{1,0:T(4,128)S(1)}, f32[4,2048]{1,0:T(4,128)S(1)}, u32[]{:S(2)}, u32[]{:S(2)}) collective-permute-start(f32[4,2048]{1,0:T(4,128)S(1)} %get-tuple-element.36), channel_id=1, source_target_pairs={{0,2},{1,3},{2,0},{3,1},{4,6},{5,7},{6,4},{7,5},{8,10},{9,11},{10,... | collective-permute-start | bytes 98312 | tf_op jit(solution)/shard_map/ppermute | solution.py:53
  26.5 3.3 %collective-permute-start.9 = (f32[4,2048]{1,0:T(4,128)S(1)}, f32[4,2048]{1,0:T(4,128)S(1)}, u32[]{:S(2)}, u32[]{:S(2)}) collective-permute-start(f32[4,2048]{1,0:T(4,128)S(1)} %get-tuple-element.37), channel_id=1, source_target_pairs={{0,3},{1,2},{2,1},{3,0},{4,7},{5,6},{6,5},{7,4},{8,11},{9,10},{10,... | collective-permute-start | bytes 98312 | tf_op jit(solution)/shard_map/ppermute | solution.py:53
  27.7 2.1 %copy-start = (f32[3,2048]{1,0:T(4,128)S(1)}, f32[3,2048]{1,0:T(4,128)}, u32[]{:S(2)}) copy-start(f32[3,2048]{1,0:T(4,128)} %pos_ref.2) | copy-start | bytes 73732
  27.7 2.1 %copy-start.3 = (f32[2048]{0:T(1024)S(1)}, f32[2048]{0:T(1024)}, u32[]{:S(2)}) copy-start(f32[2048]{0:T(1024)} %param.13) | copy-start | bytes 24580
  27.7 2.1 %copy-start.4 = (f32[2048]{0:T(1024)S(1)}, f32[2048]{0:T(1024)}, u32[]{:S(2)}) copy-start(f32[2048]{0:T(1024)} %param.14) | copy-start | bytes 24580
  27.7 2.1 %copy-start.7 = (s32[8]{0:T(128)S(1)}, s32[8]{0:T(128)}, u32[]{:S(2)}) copy-start(s32[8]{0:T(128)} %src_count_ref.1) | copy-start | bytes 100
  27.7 2.1 %copy-start.8 = (s32[8]{0:T(128)S(1)}, s32[8]{0:T(128)}, u32[]{:S(2)}) copy-start(s32[8]{0:T(128)} %tgt_count_ref.1) | copy-start | bytes 100
  27.8 4.0 %collective-permute-start.13 = (f32[4,4,512]{2,1,0:T(4,128)S(1)}, f32[4,4,512]{2,1,0:T(4,128)S(1)}, u32[]{:S(2)}, u32[]{:S(2)}) collective-permute-start(f32[4,4,512]{2,1,0:T(4,128)S(1)} %pick.1), channel_id=1, source_target_pairs={{0,4},{4,0},{8,12},{12,8},{16,20},{20,16},{24,28},{28,24},{1,5},{5... | collective-permute-start | bytes 98312 | tf_op jit(solution)/shard_map/ppermute | solution.py:65
  29.8 1.9 %copy-start.1 = (f32[3,2048]{1,0:T(4,128)S(1)}, f32[3,2048]{1,0:T(4,128)}, u32[]{:S(2)}) copy-start(f32[3,2048]{1,0:T(4,128)} %pos_ref.3) | copy-start | bytes 73732
  29.9 1.9 %copy-start.5 = (f32[2048]{0:T(1024)S(1)}, f32[2048]{0:T(1024)}, u32[]{:S(2)}) copy-start(f32[2048]{0:T(1024)} %param.17) | copy-start | bytes 24580
  29.9 1.9 %copy-start.6 = (f32[2048]{0:T(1024)S(1)}, f32[2048]{0:T(1024)}, u32[]{:S(2)}) copy-start(f32[2048]{0:T(1024)} %param.18) | copy-start | bytes 24580

commit v7 on v5

--- a/solution.py
+++ b/solution.py
@@ -265,7 +265,8 @@
         high, low = buf[g, 0], buf[g, 1]
         y = tgt_rows[q].astype(jnp.bfloat16)
         x = src_rows[s].astype(jnp.bfloat16)
-        return s, q, dot(y, high) + dot(y, low), dot_t(x, high) + dot_t(x, low)
+        tgt_part = dot_t(x, high) + dot_t(x, low)
+        return s, q, dot(y, high) + dot(y, low), tgt_part
 
     bufs = len(kern_bufs)
     for g in range(GROUP):

time: 32.5 us -> 32.5 us (level)
  no operation moved by 1% of the time
where the time goes in v7:
time: 32.5 us; the launch traced here: 32.2 us
  starting transfers between devices  17.3 us (53%)
  Pallas kernels  10.2 us (31%)
  waiting for transfers between devices  3.12 us (10%)
  between operations  1.46 us (4%)
    ppermute x6, starting transfers between devices, moved_outer(): return lax.ppermute(x, axis, pairs)  8.91 us
    pallas_call x3, Pallas kernels, shards(): pl.pallas_call(functools.partial(pairs_kernel, n_tgt, n_clus, per_req, tu...  6.73 us
    ppermute x2, starting transfers between devices, moved_inner(): return lax.ppermute(x, axis, pairs)  4.67 us
    ppermute x6, starting transfers between devices, moved(): return lax.ppermute(x, axis, [(i, step(i, k, n)) for i in range(n)])  3.72 us
    ppermute x6, waiting for transfers between devices, moved_outer(): return lax.ppermute(x, axis, pairs)  2.14 us
    pallas_call x1, Pallas kernels, shards(): pl.pallas_call(pack_kernel, name='pack', out_shape=(jax.ShapeDtypeStruct(...  1.55 us
    pallas_call x1, Pallas kernels, shards(): pl.pallas_call(functools.partial(src_kernel, n_tgt, per_req), name='finis...  1.21 us
    pallas_call x1, Pallas kernels, shards(): pl.pallas_call(functools.partial(tgt_kernel, outer, inner), name='finish_...  0.7 us
  transfers between devices with their start and end apart: 14, of which 5 were waited for; matrix products, arithmetic and copies ran while one was open for 0% of the time, Pallas kernels for 16%

profile of v7, /device:TPU:0, one launch (start us, length us, event | category | flops | bytes accessed | tf_op | source)
XLA Modules:
  0.0 32.2 jit_solution(1510481460160513133)
XLA Ops:
  0.6 1.5 %pack.1 = (f32[4,2048]{1,0:T(4,128)}, f32[4,2176]{1,0:T(4,128)}) custom-call(s32[2,8]{1,0:T(2,128)} %bitcast.20, s32[8]{0:T(128)} %src_count_ref.1, s32[8]{0:T(128)} %tgt_count_ref.1, s32[1,32]{1,0:T(1,128)} %bitcast.21, s32[1,32]{1,0:T(1,128)} %bitcast.22, f32[3,2048]{1,0:T(4,128)} %pos_ref.2, f32[1,2048]{1,0:T(1,128)} %bitcast.12, f32[1,2048]{1,0:T(1,128)} %bitcast.14, ...), custom_call_target="tpu_custom_call" | custom-call | tf_op jit(solution)/shard_map/pack/pallas_call | solution.py:398
  2.2 0.0 copy-start.2
  2.2 2.9 %collective-permute-start.3 = (f32[4,2176]{1,0:T(4,128)}, f32[4,2176]{1,0:T(4,128)S(1)}, u32[]{:S(2)}, u32[]{:S(2)}) collective-permute-start(f32[4,2176]{1,0:T(4,128)} %get-tuple-element.27.refs_0_), channel_id=1, source_target_pairs={{0,4},{4,0},{8,12},{12,8},{16,20},{20,16},{24,28},{28,24},{1,5},{5... | collective-permute-start | bytes 104456 | tf_op jit(solution)/shard_map/ppermute | solution.py:64
  5.1 0.0 collective-permute-start
  5.1 1.5 %collective-permute-start.1 = (f32[4,2048]{1,0:T(4,128)}, f32[4,2048]{1,0:T(4,128)S(1)}, u32[]{:S(2)}, u32[]{:S(2)}) collective-permute-start(f32[4,2048]{1,0:T(4,128)} %get-tuple-element.26.refs_1_), channel_id=1, source_target_pairs={{0,2},{1,3},{2,0},{3,1},{4,6},{5,7},{6,4},{7,5},{8,10},{9,11},{10,... | collective-permute-start | bytes 98312 | tf_op jit(solution)/shard_map/ppermute | solution.py:52
  6.6 0.3 %collective-permute-start.2 = (f32[4,2048]{1,0:T(4,128)}, f32[4,2048]{1,0:T(4,128)S(1)}, u32[]{:S(2)}, u32[]{:S(2)}) collective-permute-start(f32[4,2048]{1,0:T(4,128)} %get-tuple-element.26.refs_1_), channel_id=1, source_target_pairs={{0,3},{1,2},{2,1},{3,0},{4,7},{5,6},{6,5},{7,4},{8,11},{9,10},{10,... | collective-permute-start | bytes 98312 | tf_op jit(solution)/shard_map/ppermute | solution.py:52
  7.6 0.0 copy-start.9
  7.7 0.0 collective-permute-done.3.refs_1_
  7.7 0.0 copy-done.2
  7.7 3.8 %collective-permute-start.4 = (f32[8,2176]{1,0:T(8,128)S(1)}, f32[8,2176]{1,0:T(8,128)S(1)}, u32[]{:S(2)}, u32[]{:S(2)}) collective-permute-start(f32[8,2176]{1,0:T(8,128)S(1)} %join.1.refs_5_.refs_4_), channel_id=1, source_target_pairs={{0,24},{4,28},{8,16},{12,20},{16,8},{20,12},{24,0},{28,4},{1,25},{... | collective-permute-start | bytes 208904 | tf_op jit(solution)/shard_map/ppermute | solution.py:58
  11.5 0.0 collective-permute-start.5
  11.5 0.0 collective-permute-done.refs_2_
  11.5 0.7 %collective-permute-start.6 = (f32[8,2176]{1,0:T(8,128)S(1)}, f32[8,2176]{1,0:T(8,128)S(1)}, u32[]{:S(2)}, u32[]{:S(2)}) collective-permute-start(f32[8,2176]{1,0:T(8,128)S(1)} %join.1.refs_5_.refs_4_), channel_id=1, source_target_pairs={{0,16},{4,20},{8,24},{12,28},{16,0},{20,4},{24,8},{28,12},{1,17},{... | collective-permute-start | bytes 208904 | tf_op jit(solution)/shard_map/ppermute | solution.py:58
  12.1 0.1 pad_add_fusion.refs_0_.me_ref
  12.2 0.0 collective-permute-done.1.refs_3_
  12.2 0.0 collective-permute-done.2.refs_4_
  12.2 0.0 copy-done.9
  12.2 2.4 %pairs_0_1.1 = (s32[211,128]{1,0:T(8,128)S(1)}, bf16[33,32,256]{2,1,0:T(8,128)(2,1)S(1)}, f32[33,8,256]{2,1,0:T(8,128)S(1)}, f32[33,8,256]{2,1,0:T(8,128)S(1)}, f32[2,4,512]{2,1,0:T(4,128)S(1)}) custom-call(s32[4]{0:T(128)S(1)} %pad_add_fusion.refs_0_.me_ref, f32[4,2048]{1,0:T(4,128)S(1)} %copy-done.9, f32[4,2048]{1,0:T(4,128)S(1)} %collective-permute-done.refs_2_, ...), custom_call_target="tpu_custom_call" | custom-call | flops 400000000 | bytes 1048576 | tf_op jit(solution)/shard_map/pairs_0_1/pallas_call | solution.py:448
  14.7 0.0 collective-permute-done.4.refs_4_.refs_7_
  14.7 1.5 %pairs_3_4.1 = (f32[33,8,256]{2,1,0:T(8,128)S(1)}, f32[2,4,512]{2,1,0:T(4,128)S(1)}) custom-call(s32[211,128]{1,0:T(8,128)S(1)} %get-tuple-element.28.refs_0_, bf16[33,32,256]{2,1,0:T(8,128)(2,1)S(1)} %get-tuple-element.29.refs_1_, f32[33,8,256]{2,1,0:T(8,128)S(1)} %get-tuple-element.30.refs_2_, f32[33,8,256]{2,1,0:T(8,128)S(1)} %get-tuple-element.31.refs_3_, ...), custom_call_target="tpu_custom_call" | custom-call | bytes 1048576 | tf_op jit(solution)/shard_map/pairs_3_4/pallas_call | solution.py:448
  16.2 0.5 %collective-permute-done.5.refs_4_.refs_5_ = f32[8,2176]{1,0:T(8,128)S(1)} collective-permute-done((f32[8,2176]{1,0:T(8,128)S(1)}, f32[8,2176]{1,0:T(8,128)S(1)}, u32[]{:S(2)}, u32[]{:S(2)}) %collective-permute-start.5) | collective-permute-done | bytes 69664 | tf_op jit(solution)/shard_map/ppermute | solution.py:58
  16.7 0.7 %collective-permute-done.6.refs_5_.refs_6_ = f32[8,2176]{1,0:T(8,128)S(1)} collective-permute-done((f32[8,2176]{1,0:T(8,128)S(1)}, f32[8,2176]{1,0:T(8,128)S(1)}, u32[]{:S(2)}, u32[]{:S(2)}) %collective-permute-start.6) | collective-permute-done | bytes 69664 | tf_op jit(solution)/shard_map/ppermute | solution.py:58
  17.4 2.8 %pairs_1_3.1 = (f32[4,2048]{1,0:T(4,128)S(1)}, f32[4,2048]{1,0:T(4,128)S(1)}, f32[4,2048]{1,0:T(4,128)S(1)}, f32[4,2048]{1,0:T(4,128)S(1)}, f32[2,4,512]{2,1,0:T...) custom-call(s32[211,128]{1,0:T(8,128)S(1)} %get-tuple-element.28.refs_0_, ...), custom_call_target="tpu_custom_call" | custom-call | bytes 1048576 | tf_op jit(solution)/shard_map/pairs_1_3/pallas_call | solution.py:448
  20.2 2.6 %collective-permute-start.12 = (f32[2,4,512]{2,1,0:T(4,128)S(1)}, f32[2,4,512]{2,1,0:T(4,128)S(1)}, u32[]{:S(2)}, u32[]{:S(2)}) collective-permute-start(f32[2,4,512]{2,1,0:T(4,128)S(1)} %get-tuple-element.45), channel_id=1, source_target_pairs={{0,24},{4,28},{8,16},{12,20},{16,8},{20,12},{24,0},{28,4},{1,25},{... | collective-permute-start | bytes 49160 | tf_op jit(solution)/shard_map/ppermute | solution.py:58
  22.8 0.2 collective-permute-start.11
  23.1 1.6 %collective-permute-start.10 = (f32[2,4,512]{2,1,0:T(4,128)S(1)}, f32[2,4,512]{2,1,0:T(4,128)S(1)}, u32[]{:S(2)}, u32[]{:S(2)}) collective-permute-start(f32[2,4,512]{2,1,0:T(4,128)S(1)} %get-tuple-element.43), channel_id=1, source_target_pairs={{0,8},{4,12},{8,0},{12,4},{16,24},{20,28},{24,16},{28,20},{1,9},{5... | collective-permute-start | bytes 49160 | tf_op jit(solution)/shard_map/ppermute | solution.py:58
  24.7 0.0 collective-permute-start.7
  24.7 1.5 %collective-permute-start.8 = (f32[4,2048]{1,0:T(4,128)S(1)}, f32[4,2048]{1,0:T(4,128)S(1)}, u32[]{:S(2)}, u32[]{:S(2)}) collective-permute-start(f32[4,2048]{1,0:T(4,128)S(1)} %get-tuple-element.36), channel_id=1, source_target_pairs={{0,2},{1,3},{2,0},{3,1},{4,6},{5,7},{6,4},{7,5},{8,10},{9,11},{10,... | collective-permute-start | bytes 98312 | tf_op jit(solution)/shard_map/ppermute | solution.py:52
  26.2 0.0 collective-permute-done.12.refs_0_
  26.2 0.3 %collective-permute-start.9 = (f32[4,2048]{1,0:T(4,128)S(1)}, f32[4,2048]{1,0:T(4,128)S(1)}, u32[]{:S(2)}, u32[]{:S(2)}) collective-permute-start(f32[4,2048]{1,0:T(4,128)S(1)} %get-tuple-element.37), channel_id=1, source_target_pairs={{0,3},{1,2},{2,1},{3,0},{4,7},{5,6},{6,5},{7,4},{8,11},{9,10},{10,... | collective-permute-start | bytes 98312 | tf_op jit(solution)/shard_map/ppermute | solution.py:52
  26.6 0.9 %collective-permute-done.11.refs_0_ = f32[2,4,512]{2,1,0:T(4,128)S(1)} collective-permute-done((f32[2,4,512]{2,1,0:T(4,128)S(1)}, f32[2,4,512]{2,1,0:T(4,128)S(1)}, u32[]{:S(2)}, u32[]{:S(2)}) %collective-permute-start.11) | collective-permute-done | bytes 16416 | tf_op jit(solution)/shard_map/ppermute | solution.py:58
  27.5 0.0 collective-permute-done.10.refs_1_
  27.5 0.0 copy-start
  27.5 0.0 copy-start.3
  27.5 0.0 copy-start.4
  27.5 0.0 copy-start.7
  27.5 0.0 copy-start.8
  27.5 1.7 %collective-permute-start.13 = (f32[4,4,512]{2,1,0:T(4,128)S(1)}, f32[4,4,512]{2,1,0:T(4,128)S(1)}, u32[]{:S(2)}, u32[]{:S(2)}) collective-permute-start(f32[4,4,512]{2,1,0:T(4,128)S(1)} %pick.1), channel_id=1, source_target_pairs={{0,4},{4,0},{8,12},{12,8},{16,20},{20,16},{24,28},{28,24},{1,5},{5... | collective-permute-start | bytes 98312 | tf_op jit(solution)/shard_map/ppermute | solution.py:64
  29.3 0.0 collective-permute-done.7.refs_1_
  29.3 0.0 collective-permute-done.8.refs_2_
  29.3 0.3 collective-permute-done.9.refs_3_
  29.6 0.0 copy-done
  29.6 0.0 copy-done.3
  29.6 0.0 copy-done.4
  29.6 0.0 copy-done.7
  29.6 0.0 copy-done.8
  29.6 0.0 copy-start.1
  29.6 0.0 copy-start.5
  29.6 0.0 copy-start.6
  29.6 1.2 %finish_src.1 = (f32[3,2048]{1,0:T(4,128)}, f32[1,2048]{1,0:T(1,128)}, f32[16,4,256]{2,1,0:T(4,128)S(1)}, f32[1,2048]{1,0:T(1,128)S(1)}) custom-call(s32[4]{0:T(128)S(1)} %pad_add_fusion.refs_0_.me_ref, s32[8]{0:T(128)S(1)} %copy-done.7, s32[8]{0:T(128)S(1)} %copy-done.8, f32[3,2048]{1,0:T(4,128)S(1)} %copy-done, f32[1,2048]{1,0:T(1,128)S(1)} %bitcast.13, ...), custom_call_target="tpu_custom_call" | custom-call | tf_op jit(solution)/shard_map/finish_src/pallas_call | solution.py:489
  30.8 0.7 %collective-permute-done.13.refs_4_ = f32[4,4,512]{2,1,0:T(4,128)S(1)} collective-permute-done((f32[4,4,512]{2,1,0:T(4,128)S(1)}, f32[4,4,512]{2,1,0:T(4,128)S(1)}, u32[]{:S(2)}, u32[]{:S(2)}) %collective-permute-start.13) | collective-permute-done | bytes 32800 | tf_op jit(solution)/shard_map/ppermute | solution.py:64
  31.5 0.0 copy-done.1
  31.5 0.0 copy-done.5
  31.5 0.0 copy-done.6
  31.5 0.7 %finish_tgt.1 = (f32[3,2048]{1,0:T(4,128)}, f32[1,2048]{1,0:T(1,128)}) custom-call(f32[3,2048]{1,0:T(4,128)S(1)} %copy-done.1, f32[1,2048]{1,0:T(1,128)S(1)} %bitcast.17, f32[1,2048]{1,0:T(1,128)S(1)} %bitcast.19, f32[1,2048]{1,0:T(1,128)S(1)} %get-tuple-element.40.live_ref, f32[16,4,256]{2,1,0:T(4,128)S(1)} %get-tuple-element.41.ids_ref, ...), custom_call_target="tpu_custom_call" | custom-call | tf_op jit(solution)/shard_map/finish_tgt/pallas_call | solution.py:502
  (4 shorter events, 0.0 us)
Async XLA Ops:
  2.2 5.5 %copy-start.2 = (f32[4,2176]{1,0:T(4,128)S(1)}, f32[4,2176]{1,0:T(4,128)}, u32[]{:S(2)}) copy-start(f32[4,2176]{1,0:T(4,128)} %get-tuple-element.27.refs_0_) | copy-start | bytes 104452
  2.2 5.5 %collective-permute-start.3 = (f32[4,2176]{1,0:T(4,128)}, f32[4,2176]{1,0:T(4,128)S(1)}, u32[]{:S(2)}, u32[]{:S(2)}) collective-permute-start(f32[4,2176]{1,0:T(4,128)} %get-tuple-element.27.refs_0_), channel_id=1, source_target_pairs={{0,4},{4,0},{8,12},{12,8},{16,20},{20,16},{24,28},{28,24},{1,5},{5... | collective-permute-start | bytes 104456 | tf_op jit(solution)/shard_map/ppermute | solution.py:64
  5.1 6.3 %collective-permute-start = (f32[4,2048]{1,0:T(4,128)}, f32[4,2048]{1,0:T(4,128)S(1)}, u32[]{:S(2)}, u32[]{:S(2)}) collective-permute-start(f32[4,2048]{1,0:T(4,128)} %get-tuple-element.26.refs_1_), channel_id=1, source_target_pairs={{0,1},{1,0},{2,3},{3,2},{4,5},{5,4},{6,7},{7,6},{8,9},{9,8},{10,11... | collective-permute-start | bytes 98312 | tf_op jit(solution)/shard_map/ppermute | solution.py:52
  5.1 7.1 %collective-permute-start.1 = (f32[4,2048]{1,0:T(4,128)}, f32[4,2048]{1,0:T(4,128)S(1)}, u32[]{:S(2)}, u32[]{:S(2)}) collective-permute-start(f32[4,2048]{1,0:T(4,128)} %get-tuple-element.26.refs_1_), channel_id=1, source_target_pairs={{0,2},{1,3},{2,0},{3,1},{4,6},{5,7},{6,4},{7,5},{8,10},{9,11},{10,... | collective-permute-start | bytes 98312 | tf_op jit(solution)/shard_map/ppermute | solution.py:52
  6.6 5.6 %collective-permute-start.2 = (f32[4,2048]{1,0:T(4,128)}, f32[4,2048]{1,0:T(4,128)S(1)}, u32[]{:S(2)}, u32[]{:S(2)}) collective-permute-start(f32[4,2048]{1,0:T(4,128)} %get-tuple-element.26.refs_1_), channel_id=1, source_target_pairs={{0,3},{1,2},{2,1},{3,0},{4,7},{5,6},{6,5},{7,4},{8,11},{9,10},{10,... | collective-permute-start | bytes 98312 | tf_op jit(solution)/shard_map/ppermute | solution.py:52
  7.6 4.6 %copy-start.9 = (f32[4,2048]{1,0:T(4,128)S(1)}, f32[4,2048]{1,0:T(4,128)}, u32[]{:S(2)}) copy-start(f32[4,2048]{1,0:T(4,128)} %get-tuple-element.26.refs_1_) | copy-start | bytes 98308
  7.7 7.0 %collective-permute-start.4 = (f32[8,2176]{1,0:T(8,128)S(1)}, f32[8,2176]{1,0:T(8,128)S(1)}, u32[]{:S(2)}, u32[]{:S(2)}) collective-permute-start(f32[8,2176]{1,0:T(8,128)S(1)} %join.1.refs_5_.refs_4_), channel_id=1, source_target_pairs={{0,24},{4,28},{8,16},{12,20},{16,8},{20,12},{24,0},{28,4},{1,25},{... | collective-permute-start | bytes 208904 | tf_op jit(solution)/shard_map/ppermute | solution.py:58
  11.5 5.2 %collective-permute-start.5 = (f32[8,2176]{1,0:T(8,128)S(1)}, f32[8,2176]{1,0:T(8,128)S(1)}, u32[]{:S(2)}, u32[]{:S(2)}) collective-permute-start(f32[8,2176]{1,0:T(8,128)S(1)} %join.1.refs_5_.refs_4_), channel_id=1, source_target_pairs={{0,8},{4,12},{8,0},{12,4},{16,24},{20,28},{24,16},{28,20},{1,9},{5... | collective-permute-start | bytes 208904 | tf_op jit(solution)/shard_map/ppermute | solution.py:58
  11.5 6.0 %collective-permute-start.6 = (f32[8,2176]{1,0:T(8,128)S(1)}, f32[8,2176]{1,0:T(8,128)S(1)}, u32[]{:S(2)}, u32[]{:S(2)}) collective-permute-start(f32[8,2176]{1,0:T(8,128)S(1)} %join.1.refs_5_.refs_4_), channel_id=1, source_target_pairs={{0,16},{4,20},{8,24},{12,28},{16,0},{20,4},{24,8},{28,12},{1,17},{... | collective-permute-start | bytes 208904 | tf_op jit(solution)/shard_map/ppermute | solution.py:58
  20.2 6.0 %collective-permute-start.12 = (f32[2,4,512]{2,1,0:T(4,128)S(1)}, f32[2,4,512]{2,1,0:T(4,128)S(1)}, u32[]{:S(2)}, u32[]{:S(2)}) collective-permute-start(f32[2,4,512]{2,1,0:T(4,128)S(1)} %get-tuple-element.45), channel_id=1, source_target_pairs={{0,24},{4,28},{8,16},{12,20},{16,8},{20,12},{24,0},{28,4},{1,25},{... | collective-permute-start | bytes 49160 | tf_op jit(solution)/shard_map/ppermute | solution.py:58
  22.8 4.6 %collective-permute-start.11 = (f32[2,4,512]{2,1,0:T(4,128)S(1)}, f32[2,4,512]{2,1,0:T(4,128)S(1)}, u32[]{:S(2)}, u32[]{:S(2)}) collective-permute-start(f32[2,4,512]{2,1,0:T(4,128)S(1)} %get-tuple-element.44), channel_id=1, source_target_pairs={{0,16},{4,20},{8,24},{12,28},{16,0},{20,4},{24,8},{28,12},{1,17},{... | collective-permute-start | bytes 49160 | tf_op jit(solution)/shard_map/ppermute | solution.py:58
  23.1 4.4 %collective-permute-start.10 = (f32[2,4,512]{2,1,0:T(4,128)S(1)}, f32[2,4,512]{2,1,0:T(4,128)S(1)}, u32[]{:S(2)}, u32[]{:S(2)}) collective-permute-start(f32[2,4,512]{2,1,0:T(4,128)S(1)} %get-tuple-element.43), channel_id=1, source_target_pairs={{0,8},{4,12},{8,0},{12,4},{16,24},{20,28},{24,16},{28,20},{1,9},{5... | collective-permute-start | bytes 49160 | tf_op jit(solution)/shard_map/ppermute | solution.py:58
  24.7 4.6 %collective-permute-start.7 = (f32[4,2048]{1,0:T(4,128)S(1)}, f32[4,2048]{1,0:T(4,128)S(1)}, u32[]{:S(2)}, u32[]{:S(2)}) collective-permute-start(f32[4,2048]{1,0:T(4,128)S(1)} %get-tuple-element.35), channel_id=1, source_target_pairs={{0,1},{1,0},{2,3},{3,2},{4,5},{5,4},{6,7},{7,6},{8,9},{9,8},{10,11... | collective-permute-start | bytes 98312 | tf_op jit(solution)/shard_map/ppermute | solution.py:52
  24.7 4.6 %collective-permute-start.8 = (f32[4,2048]{1,0:T(4,128)S(1)}, f32[4,2048]{1,0:T(4,128)S(1)}, u32[]{:S(2)}, u32[]{:S(2)}) collective-permute-start(f32[4,2048]{1,0:T(4,128)S(1)} %get-tuple-element.36), channel_id=1, source_target_pairs={{0,2},{1,3},{2,0},{3,1},{4,6},{5,7},{6,4},{7,5},{8,10},{9,11},{10,... | collective-permute-start | bytes 98312 | tf_op jit(solution)/shard_map/ppermute | solution.py:52
  26.2 3.3 %collective-permute-start.9 = (f32[4,2048]{1,0:T(4,128)S(1)}, f32[4,2048]{1,0:T(4,128)S(1)}, u32[]{:S(2)}, u32[]{:S(2)}) collective-permute-start(f32[4,2048]{1,0:T(4,128)S(1)} %get-tuple-element.37), channel_id=1, source_target_pairs={{0,3},{1,2},{2,1},{3,0},{4,7},{5,6},{6,5},{7,4},{8,11},{9,10},{10,... | collective-permute-start | bytes 98312 | tf_op jit(solution)/shard_map/ppermute | solution.py:52
  27.5 2.1 %copy-start = (f32[3,2048]{1,0:T(4,128)S(1)}, f32[3,2048]{1,0:T(4,128)}, u32[]{:S(2)}) copy-start(f32[3,2048]{1,0:T(4,128)} %pos_ref.2) | copy-start | bytes 73732
  27.5 2.1 %copy-start.3 = (f32[2048]{0:T(1024)S(1)}, f32[2048]{0:T(1024)}, u32[]{:S(2)}) copy-start(f32[2048]{0:T(1024)} %param.13) | copy-start | bytes 24580
  27.5 2.1 %copy-start.4 = (f32[2048]{0:T(1024)S(1)}, f32[2048]{0:T(1024)}, u32[]{:S(2)}) copy-start(f32[2048]{0:T(1024)} %param.14) | copy-start | bytes 24580
  27.5 2.1 %copy-start.7 = (s32[8]{0:T(128)S(1)}, s32[8]{0:T(128)}, u32[]{:S(2)}) copy-start(s32[8]{0:T(128)} %src_count_ref.1) | copy-start | bytes 100
  27.5 2.1 %copy-start.8 = (s32[8]{0:T(128)S(1)}, s32[8]{0:T(128)}, u32[]{:S(2)}) copy-start(s32[8]{0:T(128)} %tgt_count_ref.1) | copy-start | bytes 100
  27.5 4.0 %collective-permute-start.13 = (f32[4,4,512]{2,1,0:T(4,128)S(1)}, f32[4,4,512]{2,1,0:T(4,128)S(1)}, u32[]{:S(2)}, u32[]{:S(2)}) collective-permute-start(f32[4,4,512]{2,1,0:T(4,128)S(1)} %pick.1), channel_id=1, source_target_pairs={{0,4},{4,0},{8,12},{12,8},{16,20},{20,16},{24,28},{28,24},{1,5},{5... | collective-permute-start | bytes 98312 | tf_op jit(solution)/shard_map/ppermute | solution.py:64
  29.6 1.9 %copy-start.1 = (f32[3,2048]{1,0:T(4,128)S(1)}, f32[3,2048]{1,0:T(4,128)}, u32[]{:S(2)}) copy-start(f32[3,2048]{1,0:T(4,128)} %pos_ref.3) | copy-start | bytes 73732
  29.6 1.9 %copy-start.5 = (f32[2048]{0:T(1024)S(1)}, f32[2048]{0:T(1024)}, u32[]{:S(2)}) copy-start(f32[2048]{0:T(1024)} %param.17) | copy-start | bytes 24580
  29.6 1.9 %copy-start.6 = (f32[2048]{0:T(1024)S(1)}, f32[2048]{0:T(1024)}, u32[]{:S(2)}) copy-start(f32[2048]{0:T(1024)} %param.18) | copy-start | bytes 24580

commit v8 on v5

--- a/solution.py
+++ b/solution.py
@@ -253,19 +253,30 @@
             s, q = memo[tops[turn] + inside, 0], memo[tops[turn] + pairs + inside, 0]
         return jnp.where(live, s, n_src), jnp.where(live, q, 0)
 
-    def weigh(entry, buf, g):
+    def weigh(entry, buf, g, rows=slice(0, BLK)):
         s, q = pair_ids(entry)
-        kern = jnp.exp2(dot(right[q], left[s]))
+        kern = jnp.exp2(dot(right[q, rows], left[s]))
         high = kern.astype(jnp.bfloat16)
-        buf[g, 0] = high
-        buf[g, 1] = (kern - high.astype(jnp.float32)).astype(jnp.bfloat16)
-
-    def reduce(entry, buf, g):
+        buf[g, 0, rows] = high
+        buf[g, 1, rows] = (kern - high.astype(jnp.float32)).astype(jnp.bfloat16)
+
+    def reduce(entry, buf, g, ahead):
         s, q = pair_ids(entry)
-        high, low = buf[g, 0], buf[g, 1]
         y = tgt_rows[q].astype(jnp.bfloat16)
         x = src_rows[s].astype(jnp.bfloat16)
-        return s, q, dot(y, high) + dot(y, low), dot_t(x, high) + dot_t(x, low)
+        steps = [
+            lambda: dot(y, buf[g, 0]),
+            lambda: dot_t(x, buf[g, 0]),
+            lambda: dot(y, buf[g, 1]),
+            lambda: dot_t(x, buf[g, 1]),
+        ]
+        got = {}
+        for i in (1, 3, 0, 2):
+            for j, rows in ((0, slice(0, 256, None)),):
+                if j == len(got):
+                    ahead(rows)
+            got[i] = steps[i]()
+        return s, q, got[0] + got[2], got[1] + got[3]
 
     bufs = len(kern_bufs)
     for g in range(GROUP):
@@ -276,8 +287,8 @@
         for u in range(bufs):
             parts = []
             for g in range(GROUP):
-                weigh(start + (u + 1) * GROUP + g, kern_bufs[(u + 1) % bufs], g)
-                parts.append(reduce(start + u * GROUP + g, kern_bufs[u], g))
+                ahead = functools.partial(weigh, start + (u + 1) * GROUP + g, kern_bufs[(u + 1) % bufs], g)
+                parts.append(reduce(start + u * GROUP + g, kern_bufs[u], g, ahead))
             for s, q, src_part, tgt_part in parts:
                 src_acc[s] += src_part
                 tgt_acc[q] += tgt_part

time: 32.5 us -> 32.3 us (level)
  no operation moved by 1% of the time
where the time goes in v8:
time: 32.3 us; the launch traced here: 32.1 us
  starting transfers between devices  17.3 us (54%)
  Pallas kernels  10.1 us (31%)
  waiting for transfers between devices  3.08 us (10%)
  between operations  1.46 us (5%)
    ppermute x6, starting transfers between devices, moved_outer(): return lax.ppermute(x, axis, pairs)  8.91 us
    pallas_call x3, Pallas kernels, shards(): pl.pallas_call(functools.partial(pairs_kernel, n_tgt, n_clus, per_req, tu...  6.64 us
    ppermute x2, starting transfers between devices, moved_inner(): return lax.ppermute(x, axis, pairs)  4.69 us
    ppermute x6, starting transfers between devices, moved(): return lax.ppermute(x, axis, [(i, step(i, k, n)) for i in range(n)])  3.72 us
    ppermute x6, waiting for transfers between devices, moved_outer(): return lax.ppermute(x, axis, pairs)  2.12 us
    pallas_call x1, Pallas kernels, shards(): pl.pallas_call(pack_kernel, name='pack', out_shape=(jax.ShapeDtypeStruct(...  1.55 us
    pallas_call x1, Pallas kernels, shards(): pl.pallas_call(functools.partial(src_kernel, n_tgt, per_req), name='finis...  1.21 us
    pallas_call x1, Pallas kernels, shards(): pl.pallas_call(functools.partial(tgt_kernel, outer, inner), name='finish_...  0.7 us
  transfers between devices with their start and end apart: 14, of which 5 were waited for; matrix products, arithmetic and copies ran while one was open for 0% of the time, Pallas kernels for 16%

profile of v8, /device:TPU:0, one launch (start us, length us, event | category | flops | bytes accessed | tf_op | source)
XLA Modules:
  0.0 32.1 jit_solution(6900027103712658816)
XLA Ops:
  0.6 1.5 %pack.1 = (f32[4,2048]{1,0:T(4,128)}, f32[4,2176]{1,0:T(4,128)}) custom-call(s32[2,8]{1,0:T(2,128)} %bitcast.20, s32[8]{0:T(128)} %src_count_ref.1, s32[8]{0:T(128)} %tgt_count_ref.1, s32[1,32]{1,0:T(1,128)} %bitcast.21, s32[1,32]{1,0:T(1,128)} %bitcast.22, f32[3,2048]{1,0:T(4,128)} %pos_ref.2, f32[1,2048]{1,0:T(1,128)} %bitcast.12, f32[1,2048]{1,0:T(1,128)} %bitcast.14, ...), custom_call_target="tpu_custom_call" | custom-call | tf_op jit(solution)/shard_map/pack/pallas_call | solution.py:408
  2.2 0.0 copy-start.2
  2.2 2.9 %collective-permute-start.3 = (f32[4,2176]{1,0:T(4,128)}, f32[4,2176]{1,0:T(4,128)S(1)}, u32[]{:S(2)}, u32[]{:S(2)}) collective-permute-start(f32[4,2176]{1,0:T(4,128)} %get-tuple-element.27.refs_0_), channel_id=1, source_target_pairs={{0,4},{4,0},{8,12},{12,8},{16,20},{20,16},{24,28},{28,24},{1,5},{5... | collective-permute-start | bytes 104456 | tf_op jit(solution)/shard_map/ppermute | solution.py:64
  5.1 0.0 collective-permute-start
  5.1 1.5 %collective-permute-start.1 = (f32[4,2048]{1,0:T(4,128)}, f32[4,2048]{1,0:T(4,128)S(1)}, u32[]{:S(2)}, u32[]{:S(2)}) collective-permute-start(f32[4,2048]{1,0:T(4,128)} %get-tuple-element.26.refs_1_), channel_id=1, source_target_pairs={{0,2},{1,3},{2,0},{3,1},{4,6},{5,7},{6,4},{7,5},{8,10},{9,11},{10,... | collective-permute-start | bytes 98312 | tf_op jit(solution)/shard_map/ppermute | solution.py:52
  6.6 0.3 %collective-permute-start.2 = (f32[4,2048]{1,0:T(4,128)}, f32[4,2048]{1,0:T(4,128)S(1)}, u32[]{:S(2)}, u32[]{:S(2)}) collective-permute-start(f32[4,2048]{1,0:T(4,128)} %get-tuple-element.26.refs_1_), channel_id=1, source_target_pairs={{0,3},{1,2},{2,1},{3,0},{4,7},{5,6},{6,5},{7,4},{8,11},{9,10},{10,... | collective-permute-start | bytes 98312 | tf_op jit(solution)/shard_map/ppermute | solution.py:52
  7.6 0.0 copy-start.9
  7.7 0.0 collective-permute-done.3.refs_1_
  7.7 0.0 copy-done.2
  7.7 3.8 %collective-permute-start.4 = (f32[8,2176]{1,0:T(8,128)S(1)}, f32[8,2176]{1,0:T(8,128)S(1)}, u32[]{:S(2)}, u32[]{:S(2)}) collective-permute-start(f32[8,2176]{1,0:T(8,128)S(1)} %join.1.refs_5_.refs_4_), channel_id=1, source_target_pairs={{0,24},{4,28},{8,16},{12,20},{16,8},{20,12},{24,0},{28,4},{1,25},{... | collective-permute-start | bytes 208904 | tf_op jit(solution)/shard_map/ppermute | solution.py:58
  11.5 0.0 collective-permute-start.5
  11.5 0.0 collective-permute-done.refs_2_
  11.5 0.7 %collective-permute-start.6 = (f32[8,2176]{1,0:T(8,128)S(1)}, f32[8,2176]{1,0:T(8,128)S(1)}, u32[]{:S(2)}, u32[]{:S(2)}) collective-permute-start(f32[8,2176]{1,0:T(8,128)S(1)} %join.1.refs_5_.refs_4_), channel_id=1, source_target_pairs={{0,16},{4,20},{8,24},{12,28},{16,0},{20,4},{24,8},{28,12},{1,17},{... | collective-permute-start | bytes 208904 | tf_op jit(solution)/shard_map/ppermute | solution.py:58
  12.1 0.1 pad_add_fusion.refs_0_.me_ref
  12.2 0.0 collective-permute-done.1.refs_3_
  12.2 0.0 collective-permute-done.2.refs_4_
  12.2 0.0 copy-done.9
  12.2 2.4 %pairs_0_1.1 = (s32[211,128]{1,0:T(8,128)S(1)}, bf16[33,32,256]{2,1,0:T(8,128)(2,1)S(1)}, f32[33,8,256]{2,1,0:T(8,128)S(1)}, f32[33,8,256]{2,1,0:T(8,128)S(1)}, f32[2,4,512]{2,1,0:T(4,128)S(1)}) custom-call(s32[4]{0:T(128)S(1)} %pad_add_fusion.refs_0_.me_ref, f32[4,2048]{1,0:T(4,128)S(1)} %copy-done.9, f32[4,2048]{1,0:T(4,128)S(1)} %collective-permute-done.refs_2_, ...), custom_call_target="tpu_custom_call" | custom-call | flops 400000000 | bytes 1048576 | tf_op jit(solution)/shard_map/pairs_0_1/pallas_call | solution.py:458
  14.7 0.0 collective-permute-done.4.refs_4_.refs_7_
  14.7 1.5 %pairs_3_4.1 = (f32[33,8,256]{2,1,0:T(8,128)S(1)}, f32[2,4,512]{2,1,0:T(4,128)S(1)}) custom-call(s32[211,128]{1,0:T(8,128)S(1)} %get-tuple-element.28.refs_0_, bf16[33,32,256]{2,1,0:T(8,128)(2,1)S(1)} %get-tuple-element.29.refs_1_, f32[33,8,256]{2,1,0:T(8,128)S(1)} %get-tuple-element.30.refs_2_, f32[33,8,256]{2,1,0:T(8,128)S(1)} %get-tuple-element.31.refs_3_, ...), custom_call_target="tpu_custom_call" | custom-call | bytes 1048576 | tf_op jit(solution)/shard_map/pairs_3_4/pallas_call | solution.py:458
  16.2 0.5 %collective-permute-done.5.refs_4_.refs_5_ = f32[8,2176]{1,0:T(8,128)S(1)} collective-permute-done((f32[8,2176]{1,0:T(8,128)S(1)}, f32[8,2176]{1,0:T(8,128)S(1)}, u32[]{:S(2)}, u32[]{:S(2)}) %collective-permute-start.5) | collective-permute-done | bytes 69664 | tf_op jit(solution)/shard_map/ppermute | solution.py:58
  16.7 0.7 %collective-permute-done.6.refs_5_.refs_6_ = f32[8,2176]{1,0:T(8,128)S(1)} collective-permute-done((f32[8,2176]{1,0:T(8,128)S(1)}, f32[8,2176]{1,0:T(8,128)S(1)}, u32[]{:S(2)}, u32[]{:S(2)}) %collective-permute-start.6) | collective-permute-done | bytes 69664 | tf_op jit(solution)/shard_map/ppermute | solution.py:58
  17.4 2.7 %pairs_1_3.1 = (f32[4,2048]{1,0:T(4,128)S(1)}, f32[4,2048]{1,0:T(4,128)S(1)}, f32[4,2048]{1,0:T(4,128)S(1)}, f32[4,2048]{1,0:T(4,128)S(1)}, f32[2,4,512]{2,1,0:T...) custom-call(s32[211,128]{1,0:T(8,128)S(1)} %get-tuple-element.28.refs_0_, ...), custom_call_target="tpu_custom_call" | custom-call | bytes 1048576 | tf_op jit(solution)/shard_map/pairs_1_3/pallas_call | solution.py:458
  20.1 2.6 %collective-permute-start.12 = (f32[2,4,512]{2,1,0:T(4,128)S(1)}, f32[2,4,512]{2,1,0:T(4,128)S(1)}, u32[]{:S(2)}, u32[]{:S(2)}) collective-permute-start(f32[2,4,512]{2,1,0:T(4,128)S(1)} %get-tuple-element.45), channel_id=1, source_target_pairs={{0,24},{4,28},{8,16},{12,20},{16,8},{20,12},{24,0},{28,4},{1,25},{... | collective-permute-start | bytes 49160 | tf_op jit(solution)/shard_map/ppermute | solution.py:58
  22.7 0.3 collective-permute-start.11
  23.0 1.6 %collective-permute-start.10 = (f32[2,4,512]{2,1,0:T(4,128)S(1)}, f32[2,4,512]{2,1,0:T(4,128)S(1)}, u32[]{:S(2)}, u32[]{:S(2)}) collective-permute-start(f32[2,4,512]{2,1,0:T(4,128)S(1)} %get-tuple-element.43), channel_id=1, source_target_pairs={{0,8},{4,12},{8,0},{12,4},{16,24},{20,28},{24,16},{28,20},{1,9},{5... | collective-permute-start | bytes 49160 | tf_op jit(solution)/shard_map/ppermute | solution.py:58
  24.6 0.0 collective-permute-start.7
  24.6 1.5 %collective-permute-start.8 = (f32[4,2048]{1,0:T(4,128)S(1)}, f32[4,2048]{1,0:T(4,128)S(1)}, u32[]{:S(2)}, u32[]{:S(2)}) collective-permute-start(f32[4,2048]{1,0:T(4,128)S(1)} %get-tuple-element.36), channel_id=1, source_target_pairs={{0,2},{1,3},{2,0},{3,1},{4,6},{5,7},{6,4},{7,5},{8,10},{9,11},{10,... | collective-permute-start | bytes 98312 | tf_op jit(solution)/shard_map/ppermute | solution.py:52
  26.1 0.0 collective-permute-done.12.refs_0_
  26.1 0.3 %collective-permute-start.9 = (f32[4,2048]{1,0:T(4,128)S(1)}, f32[4,2048]{1,0:T(4,128)S(1)}, u32[]{:S(2)}, u32[]{:S(2)}) collective-permute-start(f32[4,2048]{1,0:T(4,128)S(1)} %get-tuple-element.37), channel_id=1, source_target_pairs={{0,3},{1,2},{2,1},{3,0},{4,7},{5,6},{6,5},{7,4},{8,11},{9,10},{10,... | collective-permute-start | bytes 98312 | tf_op jit(solution)/shard_map/ppermute | solution.py:52
  26.5 0.9 %collective-permute-done.11.refs_0_ = f32[2,4,512]{2,1,0:T(4,128)S(1)} collective-permute-done((f32[2,4,512]{2,1,0:T(4,128)S(1)}, f32[2,4,512]{2,1,0:T(4,128)S(1)}, u32[]{:S(2)}, u32[]{:S(2)}) %collective-permute-start.11) | collective-permute-done | bytes 16416 | tf_op jit(solution)/shard_map/ppermute | solution.py:58
  27.4 0.0 collective-permute-done.10.refs_1_
  27.4 0.0 copy-start
  27.4 0.0 copy-start.3
  27.4 0.0 copy-start.4
  27.4 0.0 copy-start.7
  27.4 0.0 copy-start.8
  27.4 1.7 %collective-permute-start.13 = (f32[4,4,512]{2,1,0:T(4,128)S(1)}, f32[4,4,512]{2,1,0:T(4,128)S(1)}, u32[]{:S(2)}, u32[]{:S(2)}) collective-permute-start(f32[4,4,512]{2,1,0:T(4,128)S(1)} %pick.1), channel_id=1, source_target_pairs={{0,4},{4,0},{8,12},{12,8},{16,20},{20,16},{24,28},{28,24},{1,5},{5... | collective-permute-start | bytes 98312 | tf_op jit(solution)/shard_map/ppermute | solution.py:64
  29.2 0.0 collective-permute-done.7.refs_1_
  29.2 0.0 collective-permute-done.8.refs_2_
  29.2 0.3 collective-permute-done.9.refs_3_
  29.5 0.0 copy-done
  29.5 0.0 copy-done.3
  29.5 0.0 copy-done.4
  29.5 0.0 copy-done.7
  29.5 0.0 copy-done.8
  29.5 0.0 copy-start.1
  29.5 0.0 copy-start.5
  29.5 0.0 copy-start.6
  29.5 1.2 %finish_src.1 = (f32[3,2048]{1,0:T(4,128)}, f32[1,2048]{1,0:T(1,128)}, f32[16,4,256]{2,1,0:T(4,128)S(1)}, f32[1,2048]{1,0:T(1,128)S(1)}) custom-call(s32[4]{0:T(128)S(1)} %pad_add_fusion.refs_0_.me_ref, s32[8]{0:T(128)S(1)} %copy-done.7, s32[8]{0:T(128)S(1)} %copy-done.8, f32[3,2048]{1,0:T(4,128)S(1)} %copy-done, f32[1,2048]{1,0:T(1,128)S(1)} %bitcast.13, ...), custom_call_target="tpu_custom_call" | custom-call | tf_op jit(solution)/shard_map/finish_src/pallas_call | solution.py:499
  30.7 0.7 %collective-permute-done.13.refs_4_ = f32[4,4,512]{2,1,0:T(4,128)S(1)} collective-permute-done((f32[4,4,512]{2,1,0:T(4,128)S(1)}, f32[4,4,512]{2,1,0:T(4,128)S(1)}, u32[]{:S(2)}, u32[]{:S(2)}) %collective-permute-start.13) | collective-permute-done | bytes 32800 | tf_op jit(solution)/shard_map/ppermute | solution.py:64
  31.4 0.0 copy-done.1
  31.4 0.0 copy-done.5
  31.4 0.0 copy-done.6
  31.4 0.7 %finish_tgt.1 = (f32[3,2048]{1,0:T(4,128)}, f32[1,2048]{1,0:T(1,128)}) custom-call(f32[3,2048]{1,0:T(4,128)S(1)} %copy-done.1, f32[1,2048]{1,0:T(1,128)S(1)} %bitcast.17, f32[1,2048]{1,0:T(1,128)S(1)} %bitcast.19, f32[1,2048]{1,0:T(1,128)S(1)} %get-tuple-element.40.live_ref, f32[16,4,256]{2,1,0:T(4,128)S(1)} %get-tuple-element.41.ids_ref, ...), custom_call_target="tpu_custom_call" | custom-call | tf_op jit(solution)/shard_map/finish_tgt/pallas_call | solution.py:512
  (4 shorter events, 0.0 us)
Async XLA Ops:
  2.2 5.5 %copy-start.2 = (f32[4,2176]{1,0:T(4,128)S(1)}, f32[4,2176]{1,0:T(4,128)}, u32[]{:S(2)}) copy-start(f32[4,2176]{1,0:T(4,128)} %get-tuple-element.27.refs_0_) | copy-start | bytes 104452
  2.2 5.5 %collective-permute-start.3 = (f32[4,2176]{1,0:T(4,128)}, f32[4,2176]{1,0:T(4,128)S(1)}, u32[]{:S(2)}, u32[]{:S(2)}) collective-permute-start(f32[4,2176]{1,0:T(4,128)} %get-tuple-element.27.refs_0_), channel_id=1, source_target_pairs={{0,4},{4,0},{8,12},{12,8},{16,20},{20,16},{24,28},{28,24},{1,5},{5... | collective-permute-start | bytes 104456 | tf_op jit(solution)/shard_map/ppermute | solution.py:64
  5.1 6.3 %collective-permute-start = (f32[4,2048]{1,0:T(4,128)}, f32[4,2048]{1,0:T(4,128)S(1)}, u32[]{:S(2)}, u32[]{:S(2)}) collective-permute-start(f32[4,2048]{1,0:T(4,128)} %get-tuple-element.26.refs_1_), channel_id=1, source_target_pairs={{0,1},{1,0},{2,3},{3,2},{4,5},{5,4},{6,7},{7,6},{8,9},{9,8},{10,11... | collective-permute-start | bytes 98312 | tf_op jit(solution)/shard_map/ppermute | solution.py:52
  5.1 7.1 %collective-permute-start.1 = (f32[4,2048]{1,0:T(4,128)}, f32[4,2048]{1,0:T(4,128)S(1)}, u32[]{:S(2)}, u32[]{:S(2)}) collective-permute-start(f32[4,2048]{1,0:T(4,128)} %get-tuple-element.26.refs_1_), channel_id=1, source_target_pairs={{0,2},{1,3},{2,0},{3,1},{4,6},{5,7},{6,4},{7,5},{8,10},{9,11},{10,... | collective-permute-start | bytes 98312 | tf_op jit(solution)/shard_map/ppermute | solution.py:52
  6.6 5.6 %collective-permute-start.2 = (f32[4,2048]{1,0:T(4,128)}, f32[4,2048]{1,0:T(4,128)S(1)}, u32[]{:S(2)}, u32[]{:S(2)}) collective-permute-start(f32[4,2048]{1,0:T(4,128)} %get-tuple-element.26.refs_1_), channel_id=1, source_target_pairs={{0,3},{1,2},{2,1},{3,0},{4,7},{5,6},{6,5},{7,4},{8,11},{9,10},{10,... | collective-permute-start | bytes 98312 | tf_op jit(solution)/shard_map/ppermute | solution.py:52
  7.6 4.6 %copy-start.9 = (f32[4,2048]{1,0:T(4,128)S(1)}, f32[4,2048]{1,0:T(4,128)}, u32[]{:S(2)}) copy-start(f32[4,2048]{1,0:T(4,128)} %get-tuple-element.26.refs_1_) | copy-start | bytes 98308
  7.7 7.0 %collective-permute-start.4 = (f32[8,2176]{1,0:T(8,128)S(1)}, f32[8,2176]{1,0:T(8,128)S(1)}, u32[]{:S(2)}, u32[]{:S(2)}) collective-permute-start(f32[8,2176]{1,0:T(8,128)S(1)} %join.1.refs_5_.refs_4_), channel_id=1, source_target_pairs={{0,24},{4,28},{8,16},{12,20},{16,8},{20,12},{24,0},{28,4},{1,25},{... | collective-permute-start | bytes 208904 | tf_op jit(solution)/shard_map/ppermute | solution.py:58
  11.5 5.2 %collective-permute-start.5 = (f32[8,2176]{1,0:T(8,128)S(1)}, f32[8,2176]{1,0:T(8,128)S(1)}, u32[]{:S(2)}, u32[]{:S(2)}) collective-permute-start(f32[8,2176]{1,0:T(8,128)S(1)} %join.1.refs_5_.refs_4_), channel_id=1, source_target_pairs={{0,8},{4,12},{8,0},{12,4},{16,24},{20,28},{24,16},{28,20},{1,9},{5... | collective-permute-start | bytes 208904 | tf_op jit(solution)/shard_map/ppermute | solution.py:58
  11.5 6.0 %collective-permute-start.6 = (f32[8,2176]{1,0:T(8,128)S(1)}, f32[8,2176]{1,0:T(8,128)S(1)}, u32[]{:S(2)}, u32[]{:S(2)}) collective-permute-start(f32[8,2176]{1,0:T(8,128)S(1)} %join.1.refs_5_.refs_4_), channel_id=1, source_target_pairs={{0,16},{4,20},{8,24},{12,28},{16,0},{20,4},{24,8},{28,12},{1,17},{... | collective-permute-start | bytes 208904 | tf_op jit(solution)/shard_map/ppermute | solution.py:58
  20.1 6.0 %collective-permute-start.12 = (f32[2,4,512]{2,1,0:T(4,128)S(1)}, f32[2,4,512]{2,1,0:T(4,128)S(1)}, u32[]{:S(2)}, u32[]{:S(2)}) collective-permute-start(f32[2,4,512]{2,1,0:T(4,128)S(1)} %get-tuple-element.45), channel_id=1, source_target_pairs={{0,24},{4,28},{8,16},{12,20},{16,8},{20,12},{24,0},{28,4},{1,25},{... | collective-permute-start | bytes 49160 | tf_op jit(solution)/shard_map/ppermute | solution.py:58
  22.7 4.6 %collective-permute-start.11 = (f32[2,4,512]{2,1,0:T(4,128)S(1)}, f32[2,4,512]{2,1,0:T(4,128)S(1)}, u32[]{:S(2)}, u32[]{:S(2)}) collective-permute-start(f32[2,4,512]{2,1,0:T(4,128)S(1)} %get-tuple-element.44), channel_id=1, source_target_pairs={{0,16},{4,20},{8,24},{12,28},{16,0},{20,4},{24,8},{28,12},{1,17},{... | collective-permute-start | bytes 49160 | tf_op jit(solution)/shard_map/ppermute | solution.py:58
  23.0 4.4 %collective-permute-start.10 = (f32[2,4,512]{2,1,0:T(4,128)S(1)}, f32[2,4,512]{2,1,0:T(4,128)S(1)}, u32[]{:S(2)}, u32[]{:S(2)}) collective-permute-start(f32[2,4,512]{2,1,0:T(4,128)S(1)} %get-tuple-element.43), channel_id=1, source_target_pairs={{0,8},{4,12},{8,0},{12,4},{16,24},{20,28},{24,16},{28,20},{1,9},{5... | collective-permute-start | bytes 49160 | tf_op jit(solution)/shard_map/ppermute | solution.py:58
  24.6 4.6 %collective-permute-start.7 = (f32[4,2048]{1,0:T(4,128)S(1)}, f32[4,2048]{1,0:T(4,128)S(1)}, u32[]{:S(2)}, u32[]{:S(2)}) collective-permute-start(f32[4,2048]{1,0:T(4,128)S(1)} %get-tuple-element.35), channel_id=1, source_target_pairs={{0,1},{1,0},{2,3},{3,2},{4,5},{5,4},{6,7},{7,6},{8,9},{9,8},{10,11... | collective-permute-start | bytes 98312 | tf_op jit(solution)/shard_map/ppermute | solution.py:52
  24.6 4.6 %collective-permute-start.8 = (f32[4,2048]{1,0:T(4,128)S(1)}, f32[4,2048]{1,0:T(4,128)S(1)}, u32[]{:S(2)}, u32[]{:S(2)}) collective-permute-start(f32[4,2048]{1,0:T(4,128)S(1)} %get-tuple-element.36), channel_id=1, source_target_pairs={{0,2},{1,3},{2,0},{3,1},{4,6},{5,7},{6,4},{7,5},{8,10},{9,11},{10,... | collective-permute-start | bytes 98312 | tf_op jit(solution)/shard_map/ppermute | solution.py:52
  26.1 3.3 %collective-permute-start.9 = (f32[4,2048]{1,0:T(4,128)S(1)}, f32[4,2048]{1,0:T(4,128)S(1)}, u32[]{:S(2)}, u32[]{:S(2)}) collective-permute-start(f32[4,2048]{1,0:T(4,128)S(1)} %get-tuple-element.37), channel_id=1, source_target_pairs={{0,3},{1,2},{2,1},{3,0},{4,7},{5,6},{6,5},{7,4},{8,11},{9,10},{10,... | collective-permute-start | bytes 98312 | tf_op jit(solution)/shard_map/ppermute | solution.py:52
  27.4 2.1 %copy-start = (f32[3,2048]{1,0:T(4,128)S(1)}, f32[3,2048]{1,0:T(4,128)}, u32[]{:S(2)}) copy-start(f32[3,2048]{1,0:T(4,128)} %pos_ref.2) | copy-start | bytes 73732
  27.4 2.1 %copy-start.3 = (f32[2048]{0:T(1024)S(1)}, f32[2048]{0:T(1024)}, u32[]{:S(2)}) copy-start(f32[2048]{0:T(1024)} %param.13) | copy-start | bytes 24580
  27.4 2.1 %copy-start.4 = (f32[2048]{0:T(1024)S(1)}, f32[2048]{0:T(1024)}, u32[]{:S(2)}) copy-start(f32[2048]{0:T(1024)} %param.14) | copy-start | bytes 24580
  27.4 2.1 %copy-start.7 = (s32[8]{0:T(128)S(1)}, s32[8]{0:T(128)}, u32[]{:S(2)}) copy-start(s32[8]{0:T(128)} %src_count_ref.1) | copy-start | bytes 100
  27.4 2.1 %copy-start.8 = (s32[8]{0:T(128)S(1)}, s32[8]{0:T(128)}, u32[]{:S(2)}) copy-start(s32[8]{0:T(128)} %tgt_count_ref.1) | copy-start | bytes 100
  27.4 4.0 %collective-permute-start.13 = (f32[4,4,512]{2,1,0:T(4,128)S(1)}, f32[4,4,512]{2,1,0:T(4,128)S(1)}, u32[]{:S(2)}, u32[]{:S(2)}) collective-permute-start(f32[4,4,512]{2,1,0:T(4,128)S(1)} %pick.1), channel_id=1, source_target_pairs={{0,4},{4,0},{8,12},{12,8},{16,20},{20,16},{24,28},{28,24},{1,5},{5... | collective-permute-start | bytes 98312 | tf_op jit(solution)/shard_map/ppermute | solution.py:64
  29.5 1.9 %copy-start.1 = (f32[3,2048]{1,0:T(4,128)S(1)}, f32[3,2048]{1,0:T(4,128)}, u32[]{:S(2)}) copy-start(f32[3,2048]{1,0:T(4,128)} %pos_ref.3) | copy-start | bytes 73732
  29.5 1.9 %copy-start.5 = (f32[2048]{0:T(1024)S(1)}, f32[2048]{0:T(1024)}, u32[]{:S(2)}) copy-start(f32[2048]{0:T(1024)} %param.17) | copy-start | bytes 24580
  29.5 1.9 %copy-start.6 = (f32[2048]{0:T(1024)S(1)}, f32[2048]{0:T(1024)}, u32[]{:S(2)}) copy-start(f32[2048]{0:T(1024)} %param.18) | copy-start | bytes 24580
